TPU v7x, 32 devices: a whole 2x2x4 slice. The times are simulated.
32 devices in a mesh: sec: 8 (over z, x), op: 4 (over y, core).
Axes of the slice: x: 2, y: 2, z: 4, core: 2. Of those that a mesh axis runs over, the one named last changes fastest.
Arguments:
- state_start: bfloat16 [16, 256, 256], P('sec'), may hold values from -60 to 60
- left_ops: bfloat16 [32, 16, 256, 256], P('op', 'sec'), may hold values from -0.375 to 0.375
- right_ops: bfloat16 [32, 16, 256, 256], P('op', 'sec'), may hold values from -0.0625 to 0.0625
- shift: float32 [16], P('sec'), may hold values from 0.2 to 2.2
- partner: int32 [32, 16], P('op', 'sec'), may hold values from 0 to 5
- kept: int32 [16], P('sec'), may hold values from 128 to 256
Outputs:
- state_final: bfloat16 [16, 256, 256], P('sec')
- new_ops: bfloat16 [32, 16, 256, 256], P('op', 'sec')
Inputs may be any that keep to these rules, and one draw needn't show every extreme that they name: `partner`: position in the window of 6 sector blocks.
All inputs are finite; a program needn't handle non-finite values.
Results may differ from a plain program's by a relative error of at most 0.015.
Values may be sent and summed in bfloat16 or wider, within the bound.
No kernel may reach another device: no remote copies, remote signals or barrier semaphores. Data moves between devices by JAX's collectives and lax.ppermute only.
A program may use at most 64 MiB of HBM per device.

v0:
```python
import jax
import jax.numpy as jnp
from jax import lax
from jax.sharding import PartitionSpec as P

ITERS = 4


step_size = 0.5


def padded(cells, sides, width):
    for axis, dim in sides:
        count = lax.axis_size(axis)
        head = lax.slice_in_dim(cells, 0, width, axis=dim)
        tail = lax.slice_in_dim(cells, cells.shape[dim] - width, cells.shape[dim], axis=dim)
        cells = jnp.concatenate(
            [
                lax.ppermute(tail, axis, [(i, (i + 1) % count) for i in range(count)]),
                cells,
                lax.ppermute(head, axis, [((i + 1) % count, i) for i in range(count)]),
            ],
            axis=dim,
        )
    return cells


def shifted(block, axis, distance):
    devices = range(lax.axis_size(axis))
    route = [((i - distance) % len(devices), i) for i in devices]
    return lax.ppermute(block, axis, route)


def per_device(state_start, left_ops, right_ops, shift, partner, kept):
    sector_local = state_start.shape[0]
    width = state_start.shape[1]
    share_rows = width // lax.axis_size("op")
    share_start = lax.axis_index("op") * share_rows
    count = float(sector_local * lax.axis_size("sec") * width * width)
    shift_col = shift[:, None, None]
    state = state_start
    for iteration in range(ITERS):
        window = padded(state, (("sec", 0),), sector_local)
        sources = window[partner]
        halfway = jnp.einsum(
            "tbij,tbjk->tbik", left_ops, sources, preferred_element_type=jnp.float32
        ).astype(jnp.bfloat16)
        partial_sigma = jnp.einsum(
            "tbij,tbjk->bik", halfway, right_ops, preferred_element_type=jnp.float32
        )
        state_wide = state.astype(jnp.float32)
        state_part = lax.dynamic_slice_in_dim(state_wide, share_start, share_rows, 1)
        sigma = lax.psum(partial_sigma, "op") + shift_col * state_wide
        sigma_part = lax.dynamic_slice_in_dim(sigma, share_start, share_rows, 1)
        energy_sum, norm_sum, square_sum = lax.psum(
            (
                jnp.sum(state_part * sigma_part),
                jnp.sum(state_part * state_part),
                jnp.sum(sigma_part * sigma_part),
            ),
            ("sec", "op"),
        )
        ratio = energy_sum / norm_sum
        updated_part = state_part - step_size * (sigma_part - ratio * state_part)
        new_norm = lax.psum(jnp.sum(updated_part * updated_part), ("sec", "op"))
        factor = jnp.sqrt(count / new_norm)
        updated = state_wide - step_size * (sigma - ratio * state_wide)
        state = (updated * factor).astype(jnp.bfloat16)
    columns = jnp.arange(width, dtype=jnp.int32)
    keep_mask = (columns[None, :] < kept[:, None]).astype(jnp.bfloat16)
    kept_block = state * keep_mask[:, None, :]
    out_scale = 1.0 / float(width) ** 0.5
    projected = jnp.einsum(
        "tbij,bjk->tbik", left_ops, kept_block, preferred_element_type=jnp.float32
    ).astype(jnp.bfloat16)
    renormed = (
        jnp.einsum("bji,tbjk->tbik", kept_block, projected, preferred_element_type=jnp.float32)
        * out_scale
    ).astype(jnp.bfloat16)
    new_ops = shifted(renormed, "sec", 1)
    return (state, new_ops)


def solution(mesh):
    in_specs = (
        P("sec", None, None),
        P("op", "sec", None, None),
        P("op", "sec", None, None),
        P("sec"),
        P("op", "sec"),
        P("sec"),
    )
    out_specs = (P("sec", None, None), P("op", "sec", None, None))
    return jax.shard_map(
        per_device, mesh=mesh, in_specs=in_specs, out_specs=out_specs, check_vma=False
    )
```

profile of v0, /device:TPU:0, one launch (start us, length us, event | category | flops | bytes accessed | tf_op | source)
XLA Modules:
  0.0 638.1 jit_solution(8869017974368356733)
XLA Ops:
  7.2 3.0 collective-permute-start
  10.2 3.1 collective-permute-start.1
  14.2 7.5 %collective-permute-done = bf16[2,256,256]{2,1,0:T(8,128)(2,1)S(1)} collective-permute-done((bf16[2,256,256]{2,1,0:T(8,128)(2,1)}, bf16[2,256,256]{2,1,0:T(8,128)(2,1)S(1)}, u32[]{:S(2)}, u32[]{:S(2)}) %collective-permute-start) | collective-permute-done | bytes 262176 | tf_op jit(solution)/shard_map/ppermute | solution.py:19
  21.7 2.1 collective-permute-done.1
  23.8 1.0 pad_maximum_fusion
  24.9 2.0 gather_fusion
  26.9 4.3 fusion.47
  32.1 32.5 %all-reduce.9.cloned.1.call-done = f32[2,256,256]{2,1,0:T(8,128)} async-done(((f32[2,256,256]{2,1,0:T(8,128)}), f32[2,256,256]{2,1,0:T(8,128)}) %all-reduce.9.cloned.1.call-update) | async-done | bytes 524304 | tf_op jit(solution)/shard_map/psum | solution.py:53
  64.6 1.2 multiply_add_fusion.3
  65.8 1.6 multiply_reduce_fusion.10
  67.4 39.6 %all-reduce.3 = (f32[]{:T(128)}, f32[]{:T(128)}) all-reduce(f32[]{:T(128)} %get-tuple-element.13, f32[]{:T(128)} %get-tuple-element.12), channel_id=1, replica_groups=mesh['sec'=8,'op'=4] {'sec','op'}, use_global_device_ids=true, to_apply=%region_2.0 | all-reduce | flops 2 | bytes 16 | tf_op jit(solution)/shard_map/psum | solution.py:55
  108.3 1.6 multiply_reduce_fusion.9
  109.8 41.4 %psum.115 = f32[]{:T(128)} all-reduce(f32[]{:T(128)} %multiply_reduce_fusion.9), channel_id=1, replica_groups=mesh['sec'=8,'op'=4] {'sec','op'}, use_global_device_ids=true, to_apply=%region_6.0 | all-reduce | flops 1 | bytes 8 | tf_op jit(solution)/shard_map/psum | solution.py:65
  152.8 4.0 collective-permute-start.3
  156.9 4.0 collective-permute-done.3
  160.9 5.1 collective-permute-done.2
  166.0 2.0 gather_fusion.1
  168.0 4.3 fusion.54
  172.4 33.3 %all-reduce.11.cloned.1.call-done = f32[2,256,256]{2,1,0:T(8,128)} async-done(((f32[2,256,256]{2,1,0:T(8,128)}), f32[2,256,256]{2,1,0:T(8,128)}) %all-reduce.11.cloned.1.call-update) | async-done | bytes 524304 | tf_op jit(solution)/shard_map/psum | solution.py:53
  205.7 1.2 multiply_add_fusion.2
  206.9 1.6 multiply_reduce_fusion.7
  208.4 39.6 %all-reduce.2 = (f32[]{:T(128)}, f32[]{:T(128)}) all-reduce(f32[]{:T(128)} %get-tuple-element.11, f32[]{:T(128)} %get-tuple-element.10), channel_id=1, replica_groups=mesh['sec'=8,'op'=4] {'sec','op'}, use_global_device_ids=true, to_apply=%region_9.0 | all-reduce | flops 2 | bytes 16 | tf_op jit(solution)/shard_map/psum | solution.py:55
  249.3 1.6 multiply_reduce_fusion.6
  250.9 41.4 %psum.119 = f32[]{:T(128)} all-reduce(f32[]{:T(128)} %multiply_reduce_fusion.6), channel_id=1, replica_groups=mesh['sec'=8,'op'=4] {'sec','op'}, use_global_device_ids=true, to_apply=%region_13.0 | all-reduce | flops 1 | bytes 8 | tf_op jit(solution)/shard_map/psum | solution.py:65
  293.9 4.0 collective-permute-start.5
  297.9 4.0 collective-permute-done.5
  301.9 5.1 collective-permute-done.4
  307.1 2.0 gather_fusion.2
  309.1 4.3 fusion.61
  313.4 33.3 %all-reduce.13.cloned.1.call-done = f32[2,256,256]{2,1,0:T(8,128)} async-done(((f32[2,256,256]{2,1,0:T(8,128)}), f32[2,256,256]{2,1,0:T(8,128)}) %all-reduce.13.cloned.1.call-update) | async-done | bytes 524304 | tf_op jit(solution)/shard_map/psum | solution.py:53
  346.7 1.2 multiply_add_fusion.1
  347.9 1.6 multiply_reduce_fusion.4
  349.5 39.6 %all-reduce.1 = (f32[]{:T(128)}, f32[]{:T(128)}) all-reduce(f32[]{:T(128)} %get-tuple-element.9, f32[]{:T(128)} %get-tuple-element.8), channel_id=1, replica_groups=mesh['sec'=8,'op'=4] {'sec','op'}, use_global_device_ids=true, to_apply=%region_16.0 | all-reduce | flops 2 | bytes 16 | tf_op jit(solution)/shard_map/psum | solution.py:55
  390.4 1.6 multiply_reduce_fusion.3
  391.9 41.4 %psum.123 = f32[]{:T(128)} all-reduce(f32[]{:T(128)} %multiply_reduce_fusion.3), channel_id=1, replica_groups=mesh['sec'=8,'op'=4] {'sec','op'}, use_global_device_ids=true, to_apply=%region_20.0 | all-reduce | flops 1 | bytes 8 | tf_op jit(solution)/shard_map/psum | solution.py:65
  434.9 4.0 collective-permute-start.7
  439.0 4.0 collective-permute-done.7
  443.0 5.1 collective-permute-done.6
  448.1 2.0 gather_fusion.3
  450.1 4.4 fusion.68
  454.5 33.4 %all-reduce.15.cloned.1.call-done = f32[2,256,256]{2,1,0:T(8,128)} async-done(((f32[2,256,256]{2,1,0:T(8,128)}), f32[2,256,256]{2,1,0:T(8,128)}) %all-reduce.15.cloned.1.call-update) | async-done | bytes 524304 | tf_op jit(solution)/shard_map/psum | solution.py:53
  487.9 1.2 multiply_add_fusion
  489.7 39.6 %all-reduce = (f32[]{:T(128)}, f32[]{:T(128)}) all-reduce(f32[]{:T(128)} %get-tuple-element.7, f32[]{:T(128)} %get-tuple-element.6), channel_id=1, replica_groups=mesh['sec'=8,'op'=4] {'sec','op'}, use_global_device_ids=true, to_apply=%region_23.0 | all-reduce | flops 2 | bytes 16 | tf_op jit(solution)/shard_map/psum | solution.py:55
  531.3 41.4 %psum.127 = f32[]{:T(128)} all-reduce(f32[]{:T(128)} %multiply_reduce_fusion), channel_id=1, replica_groups=mesh['sec'=8,'op'=4] {'sec','op'}, use_global_device_ids=true, to_apply=%region_27.0 | all-reduce | flops 1 | bytes 8 | tf_op jit(solution)/shard_map/psum | solution.py:65
  573.5 4.3 fusion.40
  577.9 2.3 collective-permute-start.8
  580.1 47.5 %collective-permute-done.8 = bf16[8,2,256,256]{2,3,0,1:T(8,128)(2,1)} collective-permute-done((bf16[8,2,256,256]{2,3,0,1:T(8,128)(2,1)}, bf16[8,2,256,256]{2,3,0,1:T(8,128)(2,1)}, u32[]{:S(2)}, u32[]{:S(2)}) %collective-permute-start.8) | collective-permute-done | bytes 2097184 | tf_op jit(solution)/shard_map/ppermute | solution.py:31
  627.6 3.9 copy.19
  (38 shorter events, 6.4 us)
Async XLA Ops:
  7.2 19.7 %copy-start = (bf16[8,2,256,256]{3,2,1,0:T(8,128)(2,1)S(1)}, bf16[8,2,256,256]{3,2,1,0:T(8,128)(2,1)}, u32[]{:S(2)}) copy-start(bf16[8,2,256,256]{3,2,1,0:T(8,128)(2,1)} %param.8) | copy-start | bytes 6291460
  7.2 57.4 %all-reduce.9.cloned.1.call-start = ((), (), s32[]{:S(2)}) async-start(), calls=%async_computation | async-start | bytes 1048576 | tf_op jit(solution)/shard_map/psum | solution.py:53
  7.2 14.5 %collective-permute-start = (bf16[2,256,256]{2,1,0:T(8,128)(2,1)}, bf16[2,256,256]{2,1,0:T(8,128)(2,1)S(1)}, u32[]{:S(2)}, u32[]{:S(2)}) collective-permute-start(bf16[2,256,256]{2,1,0:T(8,128)(2,1)} %param.6), channel_id=1, source_target_pairs={{0,4},{4,8},{8,12},{12,16},{16,20},{20,24},{24,28},{28,0},{1,5},{5... | collective-permute-start | bytes 786440 | tf_op jit(solution)/shard_map/ppermute | solution.py:19
  10.2 13.6 %collective-permute-start.1 = (bf16[2,256,256]{2,1,0:T(8,128)(2,1)}, bf16[2,256,256]{2,1,0:T(8,128)(2,1)S(1)}, u32[]{:S(2)}, u32[]{:S(2)}) collective-permute-start(bf16[2,256,256]{2,1,0:T(8,128)(2,1)} %param.6), channel_id=1, source_target_pairs={{4,0},{8,4},{12,8},{16,12},{20,16},{24,20},{28,24},{0,28},{5,1},{9... | collective-permute-start | bytes 786440 | tf_op jit(solution)/shard_map/ppermute | solution.py:21
  26.9 4.4 copy-start.1
  26.9 37.8 %copy-start.4 = (f32[2]{0:T(128)S(1)}, f32[2]{0:T(128)}, u32[]{:S(2)}) copy-start(f32[2]{0:T(128)} %param.9) | copy-start | bytes 28
  31.2 174.5 %all-reduce.11.cloned.1.call-start = ((), (), s32[]{:S(2)}) async-start(), calls=%async_computation.1 | async-start | bytes 1048576 | tf_op jit(solution)/shard_map/psum | solution.py:53
  152.8 8.0 %collective-permute-start.3 = (bf16[2,256,256]{2,1,0:T(8,128)(2,1)S(1)}, bf16[2,256,256]{2,1,0:T(8,128)(2,1)S(1)}, u32[]{:S(2)}, u32[]{:S(2)}) collective-permute-start(bf16[2,256,256]{2,1,0:T(8,128)(2,1)S(1)} %get-tuple-element.27), channel_id=1, source_target_pairs={{4,0},{8,4},{12,8},{16,12},{20,16},{24,20},{28,24},{0,28},{5,1},{9... | collective-permute-start | bytes 786440 | tf_op jit(solution)/shard_map/ppermute | solution.py:21
  156.8 9.1 %collective-permute-start.2 = (bf16[2,256,256]{2,1,0:T(8,128)(2,1)S(1)}, bf16[2,256,256]{2,1,0:T(8,128)(2,1)S(1)}, u32[]{:S(2)}, u32[]{:S(2)}) collective-permute-start(bf16[2,256,256]{2,1,0:T(8,128)(2,1)S(1)} %get-tuple-element.27), channel_id=1, source_target_pairs={{0,4},{4,8},{8,12},{12,16},{16,20},{20,24},{24,28},{28,0},{1,5},{5... | collective-permute-start | bytes 786440 | tf_op jit(solution)/shard_map/ppermute | solution.py:19
  172.3 174.4 %all-reduce.13.cloned.1.call-start = ((), (), s32[]{:S(2)}) async-start(), calls=%async_computation.2 | async-start | bytes 1048576 | tf_op jit(solution)/shard_map/psum | solution.py:53
  293.9 8.0 %collective-permute-start.5 = (bf16[2,256,256]{2,1,0:T(8,128)(2,1)S(1)}, bf16[2,256,256]{2,1,0:T(8,128)(2,1)S(1)}, u32[]{:S(2)}, u32[]{:S(2)}) collective-permute-start(bf16[2,256,256]{2,1,0:T(8,128)(2,1)S(1)} %get-tuple-element.25), channel_id=1, source_target_pairs={{4,0},{8,4},{12,8},{16,12},{20,16},{24,20},{28,24},{0,28},{5,1},{9... | collective-permute-start | bytes 786440 | tf_op jit(solution)/shard_map/ppermute | solution.py:21
  297.9 9.1 %collective-permute-start.4 = (bf16[2,256,256]{2,1,0:T(8,128)(2,1)S(1)}, bf16[2,256,256]{2,1,0:T(8,128)(2,1)S(1)}, u32[]{:S(2)}, u32[]{:S(2)}) collective-permute-start(bf16[2,256,256]{2,1,0:T(8,128)(2,1)S(1)} %get-tuple-element.25), channel_id=1, source_target_pairs={{0,4},{4,8},{8,12},{12,16},{16,20},{20,24},{24,28},{28,0},{1,5},{5... | collective-permute-start | bytes 786440 | tf_op jit(solution)/shard_map/ppermute | solution.py:19
  313.4 174.5 %all-reduce.15.cloned.1.call-start = ((), (), s32[]{:S(2)}) async-start(), calls=%async_computation.3 | async-start | bytes 1048576 | tf_op jit(solution)/shard_map/psum | solution.py:53
  434.9 8.0 %collective-permute-start.7 = (bf16[2,256,256]{2,1,0:T(8,128)(2,1)S(1)}, bf16[2,256,256]{2,1,0:T(8,128)(2,1)S(1)}, u32[]{:S(2)}, u32[]{:S(2)}) collective-permute-start(bf16[2,256,256]{2,1,0:T(8,128)(2,1)S(1)} %get-tuple-element.23), channel_id=1, source_target_pairs={{4,0},{8,4},{12,8},{16,12},{20,16},{24,20},{28,24},{0,28},{5,1},{9... | collective-permute-start | bytes 786440 | tf_op jit(solution)/shard_map/ppermute | solution.py:21
  439.0 9.1 %collective-permute-start.6 = (bf16[2,256,256]{2,1,0:T(8,128)(2,1)S(1)}, bf16[2,256,256]{2,1,0:T(8,128)(2,1)S(1)}, u32[]{:S(2)}, u32[]{:S(2)}) collective-permute-start(bf16[2,256,256]{2,1,0:T(8,128)(2,1)S(1)} %get-tuple-element.23), channel_id=1, source_target_pairs={{0,4},{4,8},{8,12},{12,16},{16,20},{20,24},{24,28},{28,0},{1,5},{5... | collective-permute-start | bytes 786440 | tf_op jit(solution)/shard_map/ppermute | solution.py:19
  450.1 38.9 %copy-start.2 = (f32[2,256,256]{2,1,0:T(8,128)S(1)}, f32[2,256,256]{2,1,0:T(8,128)}, u32[]{:S(2)}) copy-start(f32[2,256,256]{2,1,0:T(8,128)} %get-tuple-element.22) | copy-start | bytes 1572868
  454.5 76.8 %copy-start.5 = (s32[2]{0:T(128)S(1)}, s32[2]{0:T(128)}, u32[]{:S(2)}) copy-start(s32[2]{0:T(128)} %param.11) | copy-start | bytes 28
  573.5 4.3 copy-start.3
  577.9 49.8 %collective-permute-start.8 = (bf16[8,2,256,256]{2,3,0,1:T(8,128)(2,1)}, bf16[8,2,256,256]{2,3,0,1:T(8,128)(2,1)}, u32[]{:S(2)}, u32[]{:S(2)}) collective-permute-start(bf16[8,2,256,256]{2,3,0,1:T(8,128)(2,1)} %fusion.40), channel_id=1, source_target_pairs={{28,0},{0,4},{4,8},{8,12},{12,16},{16,20},{20,24},{24,28},{29,1},{... | collective-permute-start | bytes 6291464 | tf_op jit(solution)/shard_map/ppermute | solution.py:31
Sparse Core Ops, SparseCore 0:
  31.3 33.2 all-reduce.8
  172.5 33.1 all-reduce.10
  313.5 33.1 all-reduce.12
  454.6 33.1 all-reduce.14
where the time goes:
time: 640 us; the launch traced here: 638 us
  blocking collectives  324 us (51%)
  waiting for transfers between devices  217 us (34%)
  between operations  22.1 us (3%)
  matrix products  21.6 us (3%)
  other arithmetic  21.1 us (3%)
  starting transfers between devices  20.6 us (3%)
  local copies, waits for them, and re-layouts  12.1 us (2%)
    psum x4, blocking collectives, per_device(): new_norm = lax.psum(jnp.sum(updated_part * updated_part), ('sec', 'op'))  165 us
    psum x4, blocking collectives, per_device(): lax.psum((jnp.sum(state_part * sigma_part), jnp.sum(state_part * state_pa...  158 us
    psum x4, waiting for transfers between devices, per_device(): sigma = lax.psum(partial_sigma, 'op') + shift_col * state_wide  132 us
    ppermute x1, waiting for transfers between devices, shifted(): return lax.ppermute(block, axis, route)  47.5 us
    ppermute x4, waiting for transfers between devices, padded(): lax.ppermute(tail, axis, [(i, (i + 1) % count) for i in range(count)])  22.7 us
    dot_general x4, matrix products, per_device(): jnp.einsum('tbij,tbjk->bik', halfway, right_ops, preferred_element_type=j...  17.3 us
    ppermute x4, starting transfers between devices, padded(): lax.ppermute(head, axis, [((i + 1) % count, i) for i in range(count)])  15.2 us
    ppermute x4, waiting for transfers between devices, padded(): lax.ppermute(head, axis, [((i + 1) % count, i) for i in range(count)])  14.1 us
  transfers between devices with their start and end apart: 13, of which 13 were waited for; matrix products, arithmetic and copies ran while one was open for 0% of the time, Pallas kernels for 0%

commit v1 on v0

v1 whole, which is shorter than its diff:
```python
import functools

import jax
import jax.numpy as jnp
from jax import lax
from jax.experimental import pallas as pl
from jax.experimental.pallas import tpu as pltpu
from jax.sharding import PartitionSpec as P

ITERS = 4
step_size = 0.5
F32 = jnp.float32
BF16 = jnp.bfloat16
SMEM = pl.BlockSpec(memory_space=pltpu.SMEM)
VMEM = pl.BlockSpec(memory_space=pltpu.VMEM)


def sec_move(x, distance):
    count = lax.axis_size("sec")
    return lax.ppermute(x, "sec", [(i, (i + distance) % count) for i in range(count)])


def core_swap(x):
    return lax.ppermute(x, "op", [(i, i ^ 1) for i in range(lax.axis_size("op"))])


def chip_sum(x):
    count = lax.axis_size("op")
    chips = count // 2
    parts = [x]
    for distance in range(1, chips):
        route = [(i, (i + 2 * distance) % count) for i in range(count)]
        parts.append(lax.ppermute(x, "op", route))
    if chips == 2:
        return parts[0].astype(F32) + parts[1].astype(F32)
    me = lax.axis_index("op") // 2
    stacked = jnp.stack(parts)[(me - jnp.arange(chips)) % chips]
    total = stacked[0].astype(F32)
    for chip in range(1, chips):
        total = total + stacked[chip].astype(F32)
    return total


def apply_kernel(core, partner, *refs):
    mine, other = refs[0:3], refs[3:6]
    left, right, kept_part, sent_part, window, halfway, total = refs[6:]
    terms, sectors, width, _ = left.shape
    half = width // 2
    here = pl.ds(pl.multiple_of(core[0] * half, half), half)
    there = pl.ds(pl.multiple_of((1 - core[0]) * half, half), half)
    for group in range(3):
        for b in range(sectors):
            window[group * sectors + b, here, :] = mine[group][b]
            window[group * sectors + b, there, :] = other[group][b]
    for b in range(sectors):
        for t in range(terms):
            product = jnp.dot(left[t, b], window[partner[t, b]], preferred_element_type=F32)
            halfway[b, :, t * width : (t + 1) * width] = product.astype(BF16)
        total[b] = jnp.dot(
            halfway[b], right[:, b].reshape(terms * width, width), preferred_element_type=F32
        )
        kept_part[b] = total[b, here, :]
        sent_part[b] = total[b, there, :].astype(BF16)


def apply_terms(core, partner, mine, other, left_ops, right_ops):
    terms, sectors, width, _ = left_ops.shape
    half = (sectors, width // 2, width)
    flops = 4 * terms * sectors * width**3
    return pl.pallas_call(
        apply_kernel,
        out_shape=(
            jax.ShapeDtypeStruct(half, F32),
            jax.ShapeDtypeStruct(half, BF16),
            jax.ShapeDtypeStruct((3 * sectors, width, width), BF16),
        ),
        in_specs=[SMEM, SMEM] + [VMEM] * 8,
        out_specs=(VMEM, VMEM, VMEM),
        scratch_shapes=[
            pltpu.VMEM((sectors, width, terms * width), BF16),
            pltpu.VMEM((sectors, width, width), F32),
        ],
        compiler_params=pltpu.CompilerParams(vmem_limit_bytes=24 * 2**20),
        cost_estimate=pl.CostEstimate(flops=flops, bytes_accessed=2**22, transcendentals=0),
    )(core, partner, *mine, *other, left_ops, right_ops)


def dots_kernel(sectors, state, sigma, out):
    groups = state.shape[0] // sectors
    rows = []
    for group in range(groups):
        block = slice(group * sectors, (group + 1) * sectors)
        s = state[block].astype(F32).reshape(-1, 8, state.shape[-1])
        v = sigma[block].astype(F32).reshape(-1, 8, state.shape[-1])
        for product in (s * v, s * s, v * v):
            lanes = jnp.sum(jnp.sum(product, axis=0), axis=0, keepdims=True)
            rows.append(lanes[:, :128] + lanes[:, 128:])
    rows.append(jnp.zeros((out.shape[0] - len(rows), 128), F32))
    out[...] = jnp.concatenate(rows, axis=0)


def window_dots(state, sigma, sectors):
    return pl.pallas_call(
        functools.partial(dots_kernel, sectors),
        out_shape=jax.ShapeDtypeStruct((16, 128), F32),
        in_specs=[VMEM, VMEM],
        out_specs=VMEM,
        compiler_params=pltpu.CompilerParams(vmem_limit_bytes=16 * 2**20),
        cost_estimate=pl.CostEstimate(flops=2**22, bytes_accessed=2**21, transcendentals=0),
    )(state, sigma)


def scalars(dots, groups, first, count):
    devices = lax.axis_size("sec")
    me = lax.axis_index("sec")
    table = jnp.zeros((devices, 3, 128), F32)
    for step in range(-(-devices // groups)):
        got = dots if step == 0 else sec_move(dots, -groups * step)
        got = got[: 3 * groups].reshape(groups, 3, 128)
        for group in range(groups):
            owner = (me + step * groups + first + group) % devices
            table = lax.dynamic_update_index_in_dim(table, got[group], owner, 0)
    sums = jnp.sum(table, axis=(0, 2))
    energy_sum, norm_sum, square_sum = sums[0], sums[1], sums[2]
    a = 1.0 + step_size * (energy_sum / norm_sum)
    new_norm = a * a * norm_sum - 2.0 * step_size * a * energy_sum + step_size**2 * square_sum
    return a, jnp.sqrt(count / new_norm)


def renorm_kernel(kept_block, left, out):
    terms, sectors, width, _ = left.shape
    for b in range(sectors):
        block = kept_block[b]
        flipped = block.T
        for t in range(terms):
            projected = jnp.dot(left[t, b], block, preferred_element_type=F32).astype(BF16)
            result = jnp.dot(flipped, projected, preferred_element_type=F32)
            out[t, b] = (result * (1.0 / float(width) ** 0.5)).astype(BF16)


def renormalise(kept_block, left_ops):
    terms, sectors, width, _ = left_ops.shape
    step = 2
    blocks = pl.BlockSpec((step, sectors, width, width), lambda i: (i, 0, 0, 0))
    return pl.pallas_call(
        renorm_kernel,
        grid=(terms // step,),
        out_shape=jax.ShapeDtypeStruct(left_ops.shape, BF16),
        in_specs=[pl.BlockSpec(kept_block.shape, lambda i: (0, 0, 0)), blocks],
        out_specs=blocks,
        compiler_params=pltpu.CompilerParams(vmem_limit_bytes=24 * 2**20),
        cost_estimate=pl.CostEstimate(
            flops=4 * terms * sectors * width**3, bytes_accessed=2**22, transcendentals=0
        ),
    )(kept_block, left_ops)


def per_device(state_start, left_ops, right_ops, shift, partner, kept):
    sectors, width, _ = state_start.shape
    half = width // 2
    count = float(sectors * lax.axis_size("sec") * width * width)
    core_index = lax.axis_index("op") % 2
    core = core_index.reshape(1).astype(jnp.int32)
    shift_col = shift[:, None, None]
    moved_left = sec_move(left_ops, 1)
    moved_kept = sec_move(kept, 1)

    def halves(x):
        return (
            lax.dynamic_slice_in_dim(x, core_index * half, half, 1),
            lax.dynamic_slice_in_dim(x, (1 - core_index) * half, half, 1),
        )

    def exchange(own_half, own_other):
        before, after = sec_move(own_half, 1), sec_move(own_half, -1)
        if own_other is None:
            own_other = core_swap(own_half)
        return (before, own_half, after), (core_swap(before), own_other, core_swap(after))

    own, other = halves(state_start)
    mine, others = exchange(own, other)
    state = sigma = sigma_window = None
    for iteration in range(ITERS):
        kept_part, sent_part, window = apply_terms(core, partner, mine, others, left_ops, right_ops)
        if iteration == 0:
            state = window
        else:
            a, factor = scalars(window_dots(state, window, sectors), 3, -1, count)
            sigma_window = window
        chip_part = (kept_part + core_swap(sent_part).astype(F32)).astype(BF16)
        applied = chip_sum(chip_part) + shift_col * mine[1].astype(F32)
        if iteration == 0:
            sigma = applied
        else:
            sigma = factor * (a * sigma - step_size * applied)
            state = factor * (a * state.astype(F32) - step_size * sigma_window.astype(F32))
        rounded = sigma.astype(BF16)
        if iteration < ITERS - 1:
            mine, others = exchange(rounded, None)
    before = sec_move(rounded, 1)
    pairs = jnp.stack([before, rounded]).reshape(2 * sectors, half, width)
    swapped = core_swap(pairs)
    low = jnp.where(core_index == 0, pairs, swapped)
    high = jnp.where(core_index == 0, swapped, pairs)
    sigma_pair = jnp.concatenate([low, high], axis=1)
    state_pair = state[: 2 * sectors]
    a, factor = scalars(window_dots(state_pair, sigma_pair, sectors), 2, -1, count)
    final = (factor * (a * state_pair - step_size * sigma_pair.astype(F32))).astype(BF16)
    columns = jnp.arange(width, dtype=jnp.int32)
    keep_mask = columns[None, :] < moved_kept[:, None]
    kept_block = jnp.where(keep_mask[:, None, :], final[:sectors], jnp.zeros((), BF16))
    return final[sectors:], renormalise(kept_block, moved_left)


def solution(mesh):
    in_specs = (
        P("sec", None, None),
        P("op", "sec", None, None),
        P("op", "sec", None, None),
        P("sec"),
        P("op", "sec"),
        P("sec"),
    )
    out_specs = (P("sec", None, None), P("op", "sec", None, None))
    return jax.shard_map(
        per_device, mesh=mesh, in_specs=in_specs, out_specs=out_specs, check_vma=False
    )
```

time: 640 us -> 183 us (0.29)
  blocking collectives: 324 us -> 0 us
  waiting for transfers between devices: 217 us -> 56 us
  starting transfers between devices: 20.6 us -> 71.9 us
  matrix products: 21.6 us -> 0 us
  Pallas kernels: 0 us -> 14.4 us
  other arithmetic: 21.1 us -> 7.33 us
  between operations: 22.1 us -> 14.1 us
  local copies, waits for them, and re-layouts: 12.1 us -> 18.7 us
    psum x8 -> x0, blocking collectives: 324 us -> none  [the longest x4 165 us: per_device(): new_norm = lax.psum(jnp.sum(updated_part * updated_part), ('sec', 'op'))]
    psum x4 -> x0, waiting for transfers between devices: 132 us -> none  [per_device(): sigma = lax.psum(partial_sigma, 'op') + shift_col * state_wide]
    ppermute x9 -> x40, starting transfers between devices: 20.5 us -> 71.9 us  [the longest x20 67.1 us: sec_move(): lax.ppermute(x, 'sec', [(i, (i + distance) % count) for i in range(count)])]
    ppermute x9 -> x40, waiting for transfers between devices: 84.3 us -> 56 us  [the longest x20 46.3 us: sec_move(): lax.ppermute(x, 'sec', [(i, (i + distance) % count) for i in range(count)])]
    dot_general x5 -> x0, matrix products: 21.6 us -> none  [the longest x4 17.3 us: per_device(): jnp.einsum('tbij,tbjk->bik', halfway, right_ops, preferred_element_type=j...]
    pallas_call x0 -> x9, Pallas kernels: none -> 14.4 us  [the longest x4 8.49 us: apply_terms(): pl.pallas_call(apply_kernel, out_shape=(jax.ShapeDtypeStruct(half, F32),...]
    reduce_sum x8 -> x4, other arithmetic: 10.7 us -> 1.22 us  [scalars(): sums = jnp.sum(table, axis=(0, 2))]
    gather x4 -> x0, local copies, waits for them, and re-layouts: 8 us -> none  [per_device(): sources = window[partner]]
  transfers between devices with their start and end apart: 13 -> 40, of which waited for: 13 -> 22; matrix products, arithmetic and copies ran while one was open for 0% -> 8% of each run, Pallas kernels for 0% -> 1%
where the time goes in v1:
time: 183 us; the launch traced here: 182 us
  starting transfers between devices  71.9 us (39%)
  waiting for transfers between devices  56 us (31%)
  local copies, waits for them, and re-layouts  18.7 us (10%)
  Pallas kernels  14.4 us (8%)
  between operations  14.1 us (8%)
  other arithmetic  7.33 us (4%)
    ppermute x20, starting transfers between devices, sec_move(): lax.ppermute(x, 'sec', [(i, (i + distance) % count) for i in range(count)])  67.1 us
    ppermute x20, waiting for transfers between devices, sec_move(): lax.ppermute(x, 'sec', [(i, (i + distance) % count) for i in range(count)])  46.3 us
    unnamed x51, local copies, waits for them, and re-layouts  9.09 us
    pallas_call x4, Pallas kernels, apply_terms(): pl.pallas_call(apply_kernel, out_shape=(jax.ShapeDtypeStruct(half, F32),...  8.49 us
    dynamic_update_slice x35, local copies, waits for them, and re-layouts, scalars(): table = lax.dynamic_update_index_in_dim(table, got[group], owner, 0)  5.45 us
    ppermute x4, waiting for transfers between devices, chip_sum(): parts.append(lax.ppermute(x, 'op', route))  5.11 us
    pallas_call x1, Pallas kernels, renormalise(): pl.pallas_call(renorm_kernel, grid=(terms // step,), out_shape=jax.ShapeD...  4.95 us
    ppermute x16, waiting for transfers between devices, core_swap(): lax.ppermute(x, 'op', [(i, i ^ 1) for i in range(lax.axis_size('op'))])  4.57 us
  transfers between devices with their start and end apart: 40, of which 22 were waited for; matrix products, arithmetic and copies ran while one was open for 8% of the time, Pallas kernels for 1%

profile of v1, /device:TPU:0, one launch (start us, length us, event | category | flops | bytes accessed | tf_op | source)
XLA Modules:
  0.0 182.4 jit_solution(16081755319553647202)
XLA Ops:
  0.7 1.0 constant_dynamic-slice_fusion
  1.7 6.0 %collective-permute-start.1 = (bf16[2,128,256]{2,1,0:T(8,128)(2,1)S(1)}, bf16[2,128,256]{2,1,0:T(8,128)(2,1)S(1)}, u32[]{:S(2)}, u32[]{:S(2)}) collective-permute-start(bf16[2,128,256]{2,1,0:T(8,128)(2,1)S(1)} %get-tuple-element.33.refs_1_), channel_id=1, source_target_pairs={{0,28},{4,0},{8,4},{12,8},{16,12},{20,16},{24,20},{28,24},{1,29},{... | collective-permute-start | bytes 393224 | tf_op jit(solution)/shard_map/ppermute | solution.py:20
  7.7 2.8 %collective-permute-done.1.refs_2_ = bf16[2,128,256]{2,1,0:T(8,128)(2,1)S(1)} collective-permute-done((bf16[2,128,256]{2,1,0:T(8,128)(2,1)S(1)}, bf16[2,128,256]{2,1,0:T(8,128)(2,1)S(1)}, u32[]{:S(2)}, u32[]{:S(2)}) %collective-permute-start.1) | collective-permute-done | bytes 131104 | tf_op jit(solution)/shard_map/ppermute | solution.py:20
  10.4 4.9 %collective-permute-done.refs_0_ = bf16[2,128,256]{2,1,0:T(8,128)(2,1)S(1)} collective-permute-done((bf16[2,128,256]{2,1,0:T(8,128)(2,1)S(1)}, bf16[2,128,256]{2,1,0:T(8,128)(2,1)S(1)}, u32[]{:S(2)}, u32[]{:S(2)}) %collective-permute-start) | collective-permute-done | bytes 131104 | tf_op jit(solution)/shard_map/ppermute | solution.py:20
  15.3 0.8 copy.8.partner
  17.4 1.6 copy-done
  18.9 1.6 copy-done.2
  20.5 0.9 copy-done.13
  21.4 2.0 %shard_map.77 = (f32[2,128,256]{2,1,0:T(8,128)S(1)}, bf16[2,128,256]{2,1,0:T(8,128)(2,1)S(1)}, bf16[6,256,256]{2,1,0:T(8,128)(2,1)S(1)}) custom-call(s32[1]{0:T(128)} %bitcast.core, s32[8,2]{1,0:T(8,128)S(1)} %copy.8.partner, bf16[2,128,256]{2,1,0:T(8,128)(2,1)S(1)} %collective-permute-done.refs_0_, bf16[2,128,256]{2,1,0:T(8,128)(2,1)S(1)} %get-tuple-element.33.refs_1_, ...), custom_call_target="tpu_custom_call" | custom-call | flops 1073741824 | bytes 4194304 | tf_op jit(solution)/shard_map/pallas_call | solution.py:70
  23.7 1.2 collective-permute-done.4
  24.9 1.6 collective-permute-start.5
  26.5 4.0 %collective-permute-done.5 = bf16[2,128,256]{2,1,0:T(8,128)(2,1)S(1)} collective-permute-done((bf16[2,128,256]{2,1,0:T(8,128)(2,1)S(1)}, bf16[2,128,256]{2,1,0:T(8,128)(2,1)S(1)}, u32[]{:S(2)}, u32[]{:S(2)}) %collective-permute-start.5) | collective-permute-done | bytes 131104 | tf_op jit(solution)/shard_map/ppermute | solution.py:33
  30.7 0.8 collective-permute-start.7
  31.5 1.3 collective-permute-start.6
  32.7 2.9 %collective-permute-done.7.refs_2_ = bf16[2,128,256]{2,1,0:T(8,128)(2,1)S(1)} collective-permute-done((bf16[2,128,256]{2,1,0:T(8,128)(2,1)S(1)}, bf16[2,128,256]{2,1,0:T(8,128)(2,1)S(1)}, u32[]{:S(2)}, u32[]{:S(2)}) %collective-permute-start.7) | collective-permute-done | bytes 131104 | tf_op jit(solution)/shard_map/ppermute | solution.py:20
  35.7 3.4 %collective-permute-done.6.refs_0_ = bf16[2,128,256]{2,1,0:T(8,128)(2,1)S(1)} collective-permute-done((bf16[2,128,256]{2,1,0:T(8,128)(2,1)S(1)}, bf16[2,128,256]{2,1,0:T(8,128)(2,1)S(1)}, u32[]{:S(2)}, u32[]{:S(2)}) %collective-permute-start.6) | collective-permute-done | bytes 131104 | tf_op jit(solution)/shard_map/ppermute | solution.py:20
  39.2 1.5 collective-permute-done.8.refs_3_
  40.6 1.6 copy-done.3
  42.2 2.4 %shard_map.78 = (f32[2,128,256]{2,1,0:T(8,128)S(1)}, bf16[2,128,256]{2,1,0:T(8,128)(2,1)S(1)}, bf16[6,256,256]{2,1,0:T(8,128)(2,1)S(1)}) custom-call(s32[1]{0:T(128)} %bitcast.core, s32[8,2]{1,0:T(8,128)S(1)} %copy.8.partner, bf16[2,128,256]{2,1,0:T(8,128)(2,1)S(1)} %collective-permute-done.6.refs_0_, bf16[2,128,256]{2,1,0:T(8,128)(2,1)S(1)} %fusion.2.refs_1_, ...), custom_call_target="tpu_custom_call" | custom-call | flops 1073741824 | bytes 4194304 | tf_op jit(solution)/shard_map/pallas_call | solution.py:70
  44.8 0.9 copy-done.9
  45.7 1.2 collective-permute-start.11
  49.2 1.0 collective-permute-done.11
  53.2 1.6 collective-permute-start.14
  55.3 0.8 reduce_sum.36
  60.1 1.2 fusion.4
  61.3 2.8 %collective-permute-start.16 = (bf16[2,128,256]{2,1,0:T(8,128)(2,1)S(1)}, bf16[2,128,256]{2,1,0:T(8,128)(2,1)S(1)}, u32[]{:S(2)}, u32[]{:S(2)}) collective-permute-start(bf16[2,128,256]{2,1,0:T(8,128)(2,1)S(1)} %get-tuple-element.26.refs_1_), channel_id=1, source_target_pairs={{0,28},{4,0},{8,4},{12,8},{16,12},{20,16},{24,20},{28,24},{1,29},{... | collective-permute-start | bytes 393224 | tf_op jit(solution)/shard_map/ppermute | solution.py:20
  64.5 5.2 %collective-permute-done.16.refs_2_ = bf16[2,128,256]{2,1,0:T(8,128)(2,1)S(1)} collective-permute-done((bf16[2,128,256]{2,1,0:T(8,128)(2,1)S(1)}, bf16[2,128,256]{2,1,0:T(8,128)(2,1)S(1)}, u32[]{:S(2)}, u32[]{:S(2)}) %collective-permute-start.16) | collective-permute-done | bytes 131104 | tf_op jit(solution)/shard_map/ppermute | solution.py:20
  69.7 2.0 %collective-permute-done.15.refs_0_ = bf16[2,128,256]{2,1,0:T(8,128)(2,1)S(1)} collective-permute-done((bf16[2,128,256]{2,1,0:T(8,128)(2,1)S(1)}, bf16[2,128,256]{2,1,0:T(8,128)(2,1)S(1)}, u32[]{:S(2)}, u32[]{:S(2)}) %collective-permute-start.15) | collective-permute-done | bytes 131104 | tf_op jit(solution)/shard_map/ppermute | solution.py:20
  72.1 1.0 collective-permute-done.17.refs_3_
  73.1 2.0 %shard_map.80 = (f32[2,128,256]{2,1,0:T(8,128)S(1)}, bf16[2,128,256]{2,1,0:T(8,128)(2,1)S(1)}, bf16[6,256,256]{2,1,0:T(8,128)(2,1)S(1)}) custom-call(s32[1]{0:T(128)} %bitcast.core, s32[8,2]{1,0:T(8,128)S(1)} %copy.8.partner, bf16[2,128,256]{2,1,0:T(8,128)(2,1)S(1)} %collective-permute-done.15.refs_0_, bf16[2,128,256]{2,1,0:T(8,128)(2,1)S(1)} %get-tuple-element.26.refs_1_, ...), custom_call_target="tpu_custom_call" | custom-call | flops 1073741824 | bytes 4194304 | tf_op jit(solution)/shard_map/pallas_call | solution.py:70
  75.9 1.9 %collective-permute-start.20 = (f32[16,128]{1,0:T(8,128)S(1)}, f32[16,128]{1,0:T(8,128)S(1)}, u32[]{:S(2)}, u32[]{:S(2)}) collective-permute-start(f32[16,128]{1,0:T(8,128)S(1)} %shard_map.81), channel_id=1, source_target_pairs={{0,20},{4,24},{8,28},{12,0},{16,4},{20,8},{24,12},{28,16},{1,21},{... | collective-permute-start | bytes 24584 | tf_op jit(solution)/shard_map/ppermute | solution.py:20
  77.9 2.6 %collective-permute-done.20 = f32[16,128]{1,0:T(8,128)S(1)} collective-permute-done((f32[16,128]{1,0:T(8,128)S(1)}, f32[16,128]{1,0:T(8,128)S(1)}, u32[]{:S(2)}, u32[]{:S(2)}) %collective-permute-start.20) | collective-permute-done | bytes 8224 | tf_op jit(solution)/shard_map/ppermute | solution.py:20
  86.8 4.5 %collective-permute-start.25 = (bf16[2,128,256]{2,1,0:T(8,128)(2,1)S(1)}, bf16[2,128,256]{2,1,0:T(8,128)(2,1)S(1)}, u32[]{:S(2)}, u32[]{:S(2)}) collective-permute-start(bf16[2,128,256]{2,1,0:T(8,128)(2,1)S(1)} %fusion.3.refs_1_), channel_id=1, source_target_pairs={{0,28},{4,0},{8,4},{12,8},{16,12},{20,16},{24,20},{28,24},{1,29},{... | collective-permute-start | bytes 393224 | tf_op jit(solution)/shard_map/ppermute | solution.py:20
  91.8 2.0 %collective-permute-done.25.refs_2_ = bf16[2,128,256]{2,1,0:T(8,128)(2,1)S(1)} collective-permute-done((bf16[2,128,256]{2,1,0:T(8,128)(2,1)S(1)}, bf16[2,128,256]{2,1,0:T(8,128)(2,1)S(1)}, u32[]{:S(2)}, u32[]{:S(2)}) %collective-permute-start.25) | collective-permute-done | bytes 131104 | tf_op jit(solution)/shard_map/ppermute | solution.py:20
  93.8 6.6 %collective-permute-done.24.refs_0_ = bf16[2,128,256]{2,1,0:T(8,128)(2,1)S(1)} collective-permute-done((bf16[2,128,256]{2,1,0:T(8,128)(2,1)S(1)}, bf16[2,128,256]{2,1,0:T(8,128)(2,1)S(1)}, u32[]{:S(2)}, u32[]{:S(2)}) %collective-permute-start.24) | collective-permute-done | bytes 131104 | tf_op jit(solution)/shard_map/ppermute | solution.py:20
  100.4 1.7 subtract_multiply_fusion.state
  102.1 2.0 %shard_map.82 = (f32[2,128,256]{2,1,0:T(8,128)S(1)}, bf16[2,128,256]{2,1,0:T(8,128)(2,1)S(1)}, bf16[6,256,256]{2,1,0:T(8,128)(2,1)S(1)}) custom-call(s32[1]{0:T(128)} %bitcast.core, s32[8,2]{1,0:T(8,128)S(1)} %copy.8.partner, bf16[2,128,256]{2,1,0:T(8,128)(2,1)S(1)} %collective-permute-done.24.refs_0_, bf16[2,128,256]{2,1,0:T(8,128)(2,1)S(1)} %fusion.3.refs_1_, ...), custom_call_target="tpu_custom_call" | custom-call | flops 1073741824 | bytes 4194304 | tf_op jit(solution)/shard_map/pallas_call | solution.py:70
  105.0 41.2 %collective-permute-start.30 = (f32[16,128]{1,0:T(8,128)S(1)}, f32[16,128]{1,0:T(8,128)S(1)}, u32[]{:S(2)}, u32[]{:S(2)}) collective-permute-start(f32[16,128]{1,0:T(8,128)S(1)} %shard_map.83), channel_id=1, source_target_pairs={{0,8},{4,12},{8,16},{12,20},{16,24},{20,28},{24,0},{28,4},{1,9},{5... | collective-permute-start | bytes 24584 | tf_op jit(solution)/shard_map/ppermute | solution.py:20
  146.2 1.0 collective-permute-start.29
  147.3 3.5 %collective-permute-done.29 = f32[16,128]{1,0:T(8,128)S(1)} collective-permute-done((f32[16,128]{1,0:T(8,128)S(1)}, f32[16,128]{1,0:T(8,128)S(1)}, u32[]{:S(2)}, u32[]{:S(2)}) %collective-permute-start.29) | collective-permute-done | bytes 8224 | tf_op jit(solution)/shard_map/ppermute | solution.py:20
  156.1 1.2 collective-permute-start.33
  157.4 6.4 %collective-permute-done.33 = bf16[2,128,256]{2,1,0:T(8,128)(2,1)S(1)} collective-permute-done((bf16[2,128,256]{2,1,0:T(8,128)(2,1)S(1)}, bf16[2,128,256]{2,1,0:T(8,128)(2,1)S(1)}, u32[]{:S(2)}, u32[]{:S(2)}) %collective-permute-start.33) | collective-permute-done | bytes 131104 | tf_op jit(solution)/shard_map/ppermute | solution.py:20
  164.0 1.2 fusion.1.state
  165.9 2.6 %collective-permute-start.36 = (f32[16,128]{1,0:T(8,128)S(1)}, f32[16,128]{1,0:T(8,128)S(1)}, u32[]{:S(2)}, u32[]{:S(2)}) collective-permute-start(f32[16,128]{1,0:T(8,128)S(1)} %shard_map.84), channel_id=1, source_target_pairs={{0,16},{4,20},{8,24},{12,28},{16,0},{20,4},{24,8},{28,12},{1,17},{... | collective-permute-start | bytes 24584 | tf_op jit(solution)/shard_map/ppermute | solution.py:20
  168.5 1.2 collective-permute-start.35
  169.7 2.4 %collective-permute-done.35 = f32[16,128]{1,0:T(8,128)S(1)} collective-permute-done((f32[16,128]{1,0:T(8,128)S(1)}, f32[16,128]{1,0:T(8,128)S(1)}, u32[]{:S(2)}, u32[]{:S(2)}) %collective-permute-start.35) | collective-permute-done | bytes 8224 | tf_op jit(solution)/shard_map/ppermute | solution.py:20
  176.7 0.7 slice_select_fusion
  177.4 5.0 %shard_map.85 = bf16[8,2,256,256]{3,2,1,0:T(8,128)(2,1)} custom-call(bf16[2,256,256]{2,1,0:T(8,128)(2,1)S(1)} %get-tuple-element.28.kept_block, bf16[8,2,256,256]{3,2,1,0:T(8,128)(2,1)} %collective-permute-done.39.left), custom_call_target="tpu_custom_call" | custom-call | flops 1073741824 | bytes 4194304 | tf_op jit(solution)/shard_map/pallas_call | solution.py:145
  (157 shorter events, 18.6 us)
Async XLA Ops:
  1.7 8.8 %collective-permute-start.1 = (bf16[2,128,256]{2,1,0:T(8,128)(2,1)S(1)}, bf16[2,128,256]{2,1,0:T(8,128)(2,1)S(1)}, u32[]{:S(2)}, u32[]{:S(2)}) collective-permute-start(bf16[2,128,256]{2,1,0:T(8,128)(2,1)S(1)} %get-tuple-element.33.refs_1_), channel_id=1, source_target_pairs={{0,28},{4,0},{8,4},{12,8},{16,12},{20,16},{24,20},{28,24},{1,29},{... | collective-permute-start | bytes 393224 | tf_op jit(solution)/shard_map/ppermute | solution.py:20
  7.7 7.7 %collective-permute-start = (bf16[2,128,256]{2,1,0:T(8,128)(2,1)S(1)}, bf16[2,128,256]{2,1,0:T(8,128)(2,1)S(1)}, u32[]{:S(2)}, u32[]{:S(2)}) collective-permute-start(bf16[2,128,256]{2,1,0:T(8,128)(2,1)S(1)} %get-tuple-element.33.refs_1_), channel_id=1, source_target_pairs={{0,4},{4,8},{8,12},{12,16},{16,20},{20,24},{24,28},{28,0},{1,5},{5... | collective-permute-start | bytes 393224 | tf_op jit(solution)/shard_map/ppermute | solution.py:20
  10.4 5.7 %collective-permute-start.3 = (bf16[2,128,256]{2,1,0:T(8,128)(2,1)S(1)}, bf16[2,128,256]{2,1,0:T(8,128)(2,1)S(1)}, u32[]{:S(2)}, u32[]{:S(2)}) collective-permute-start(bf16[2,128,256]{2,1,0:T(8,128)(2,1)S(1)} %collective-permute-done.1.refs_2_), channel_id=1, source_target_pairs={{0,1},{1,0},{2,3},{3,2},{4,5},{5,4},{6,7},{7,6},{8,9},{9,8},{10,11... | collective-permute-start | bytes 393224 | tf_op jit(solution)/shard_map/ppermute | solution.py:24
  15.3 1.3 collective-permute-start.2
  21.4 19.2 %copy-start.1 = (bf16[8,2,256,256]{3,2,1,0:T(8,128)(2,1)S(1)}, bf16[8,2,256,256]{3,2,1,0:T(8,128)(2,1)}, u32[]{:S(2)}) copy-start(bf16[8,2,256,256]{3,2,1,0:T(8,128)(2,1)} %refs_7_.7) | copy-start | bytes 6291460
  23.5 1.4 collective-permute-start.4
  24.9 5.6 %collective-permute-start.5 = (bf16[2,128,256]{2,1,0:T(8,128)(2,1)S(1)}, bf16[2,128,256]{2,1,0:T(8,128)(2,1)S(1)}, u32[]{:S(2)}, u32[]{:S(2)}) collective-permute-start(bf16[2,128,256]{2,1,0:T(8,128)(2,1)S(1)} %add_convert_fusion.3), channel_id=1, source_target_pairs={{0,2},{1,3},{2,0},{3,1},{4,6},{5,7},{6,4},{7,5},{8,10},{9,11},{10,... | collective-permute-start | bytes 393224 | tf_op jit(solution)/shard_map/ppermute | solution.py:33
  30.7 5.0 %collective-permute-start.7 = (bf16[2,128,256]{2,1,0:T(8,128)(2,1)S(1)}, bf16[2,128,256]{2,1,0:T(8,128)(2,1)S(1)}, u32[]{:S(2)}, u32[]{:S(2)}) collective-permute-start(bf16[2,128,256]{2,1,0:T(8,128)(2,1)S(1)} %fusion.2.refs_1_), channel_id=1, source_target_pairs={{0,28},{4,0},{8,4},{12,8},{16,12},{20,16},{24,20},{28,24},{1,29},{... | collective-permute-start | bytes 393224 | tf_op jit(solution)/shard_map/ppermute | solution.py:20
  31.5 7.7 %collective-permute-start.6 = (bf16[2,128,256]{2,1,0:T(8,128)(2,1)S(1)}, bf16[2,128,256]{2,1,0:T(8,128)(2,1)S(1)}, u32[]{:S(2)}, u32[]{:S(2)}) collective-permute-start(bf16[2,128,256]{2,1,0:T(8,128)(2,1)S(1)} %fusion.2.refs_1_), channel_id=1, source_target_pairs={{0,4},{4,8},{8,12},{12,16},{16,20},{20,24},{24,28},{28,0},{1,5},{5... | collective-permute-start | bytes 393224 | tf_op jit(solution)/shard_map/ppermute | solution.py:20
  32.7 6.4 %collective-permute-start.9 = (bf16[2,128,256]{2,1,0:T(8,128)(2,1)S(1)}, bf16[2,128,256]{2,1,0:T(8,128)(2,1)S(1)}, u32[]{:S(2)}, u32[]{:S(2)}) collective-permute-start(bf16[2,128,256]{2,1,0:T(8,128)(2,1)S(1)} %fusion.2.refs_1_), channel_id=1, source_target_pairs={{0,1},{1,0},{2,3},{3,2},{4,5},{5,4},{6,7},{7,6},{8,9},{9,8},{10,11... | collective-permute-start | bytes 393224 | tf_op jit(solution)/shard_map/ppermute | solution.py:24
  35.7 3.5 %collective-permute-start.10 = (bf16[2,128,256]{2,1,0:T(8,128)(2,1)S(1)}, bf16[2,128,256]{2,1,0:T(8,128)(2,1)}, u32[]{:S(2)}, u32[]{:S(2)}) collective-permute-start(bf16[2,128,256]{2,1,0:T(8,128)(2,1)S(1)} %collective-permute-done.7.refs_2_), channel_id=1, source_target_pairs={{0,1},{1,0},{2,3},{3,2},{4,5},{5,4},{6,7},{7,6},{8,9},{9,8},{10,11... | collective-permute-start | bytes 393224 | tf_op jit(solution)/shard_map/ppermute | solution.py:24
  39.1 1.5 collective-permute-start.8
  44.6 15.4 %copy-start.15 = (bf16[2,128,256]{2,1,0:T(8,128)(2,1)S(1)}, bf16[2,128,256]{2,1,0:T(8,128)(2,1)}, u32[]{:S(2)}) copy-start(bf16[2,128,256]{2,1,0:T(8,128)(2,1)} %copy-done.14) | copy-start | bytes 393220
  44.6 15.4 %copy-start.19 = (bf16[2,128,256]{2,1,0:T(8,128)(2,1)S(1)}, bf16[2,128,256]{2,1,0:T(8,128)(2,1)}, u32[]{:S(2)}) copy-start(bf16[2,128,256]{2,1,0:T(8,128)(2,1)} %copy-done.18) | copy-start | bytes 393220
  45.7 6.3 %collective-permute-start.12 = (f32[16,128]{1,0:T(8,128)S(1)}, f32[16,128]{1,0:T(8,128)S(1)}, u32[]{:S(2)}, u32[]{:S(2)}) collective-permute-start(f32[16,128]{1,0:T(8,128)S(1)} %shard_map.79), channel_id=1, source_target_pairs={{0,8},{4,12},{8,16},{12,20},{16,24},{20,28},{24,0},{28,4},{1,9},{5... | collective-permute-start | bytes 24584 | tf_op jit(solution)/shard_map/ppermute | solution.py:20
  45.7 4.5 %collective-permute-start.11 = (f32[16,128]{1,0:T(8,128)S(1)}, f32[16,128]{1,0:T(8,128)S(1)}, u32[]{:S(2)}, u32[]{:S(2)}) collective-permute-start(f32[16,128]{1,0:T(8,128)S(1)} %shard_map.79), channel_id=1, source_target_pairs={{0,20},{4,24},{8,28},{12,0},{16,4},{20,8},{24,12},{28,16},{1,21},{... | collective-permute-start | bytes 24584 | tf_op jit(solution)/shard_map/ppermute | solution.py:20
  46.9 6.2 %collective-permute-start.13 = (bf16[2,128,256]{2,1,0:T(8,128)(2,1)S(1)}, bf16[2,128,256]{2,1,0:T(8,128)(2,1)S(1)}, u32[]{:S(2)}, u32[]{:S(2)}) collective-permute-start(bf16[2,128,256]{2,1,0:T(8,128)(2,1)S(1)} %get-tuple-element.19), channel_id=1, source_target_pairs={{0,1},{1,0},{2,3},{3,2},{4,5},{5,4},{6,7},{7,6},{8,9},{9,8},{10,11... | collective-permute-start | bytes 393224 | tf_op jit(solution)/shard_map/ppermute | solution.py:24
  53.2 6.9 %collective-permute-start.14 = (bf16[2,128,256]{2,1,0:T(8,128)(2,1)S(1)}, bf16[2,128,256]{2,1,0:T(8,128)(2,1)}, u32[]{:S(2)}, u32[]{:S(2)}) collective-permute-start(bf16[2,128,256]{2,1,0:T(8,128)(2,1)S(1)} %add_convert_fusion.2), channel_id=1, source_target_pairs={{0,2},{1,3},{2,0},{3,1},{4,6},{5,7},{6,4},{7,5},{8,10},{9,11},{10,... | collective-permute-start | bytes 393224 | tf_op jit(solution)/shard_map/ppermute | solution.py:33
  61.3 11.9 %copy-start.4 = (bf16[8,2,256,256]{3,2,1,0:T(8,128)(2,1)S(1)}, bf16[8,2,256,256]{3,2,1,0:T(8,128)(2,1)}, u32[]{:S(2)}) copy-start(bf16[8,2,256,256]{3,2,1,0:T(8,128)(2,1)} %refs_6_.7) | copy-start | bytes 6291460
  61.3 8.4 %collective-permute-start.16 = (bf16[2,128,256]{2,1,0:T(8,128)(2,1)S(1)}, bf16[2,128,256]{2,1,0:T(8,128)(2,1)S(1)}, u32[]{:S(2)}, u32[]{:S(2)}) collective-permute-start(bf16[2,128,256]{2,1,0:T(8,128)(2,1)S(1)} %get-tuple-element.26.refs_1_), channel_id=1, source_target_pairs={{0,28},{4,0},{8,4},{12,8},{16,12},{20,16},{24,20},{28,24},{1,29},{... | collective-permute-start | bytes 393224 | tf_op jit(solution)/shard_map/ppermute | solution.py:20
  64.1 7.7 %collective-permute-start.15 = (bf16[2,128,256]{2,1,0:T(8,128)(2,1)S(1)}, bf16[2,128,256]{2,1,0:T(8,128)(2,1)S(1)}, u32[]{:S(2)}, u32[]{:S(2)}) collective-permute-start(bf16[2,128,256]{2,1,0:T(8,128)(2,1)S(1)} %get-tuple-element.26.refs_1_), channel_id=1, source_target_pairs={{0,4},{4,8},{8,12},{12,16},{16,20},{20,24},{24,28},{28,0},{1,5},{5... | collective-permute-start | bytes 393224 | tf_op jit(solution)/shard_map/ppermute | solution.py:20
  64.5 7.6 %collective-permute-start.18 = (bf16[2,128,256]{2,1,0:T(8,128)(2,1)S(1)}, bf16[2,128,256]{2,1,0:T(8,128)(2,1)S(1)}, u32[]{:S(2)}, u32[]{:S(2)}) collective-permute-start(bf16[2,128,256]{2,1,0:T(8,128)(2,1)S(1)} %get-tuple-element.26.refs_1_), channel_id=1, source_target_pairs={{0,1},{1,0},{2,3},{3,2},{4,5},{5,4},{6,7},{7,6},{8,9},{9,8},{10,11... | collective-permute-start | bytes 393224 | tf_op jit(solution)/shard_map/ppermute | solution.py:24
  69.7 2.4 %collective-permute-start.19 = (bf16[2,128,256]{2,1,0:T(8,128)(2,1)S(1)}, bf16[2,128,256]{2,1,0:T(8,128)(2,1)S(1)}, u32[]{:S(2)}, u32[]{:S(2)}) collective-permute-start(bf16[2,128,256]{2,1,0:T(8,128)(2,1)S(1)} %collective-permute-done.16.refs_2_), channel_id=1, source_target_pairs={{0,1},{1,0},{2,3},{3,2},{4,5},{5,4},{6,7},{7,6},{8,9},{9,8},{10,11... | collective-permute-start | bytes 393224 | tf_op jit(solution)/shard_map/ppermute | solution.py:24
  71.8 1.3 collective-permute-start.17
  75.2 16.4 %copy-start.24 = (s32[2]{0:T(128)S(1)}, s32[2]{0:T(128)}, u32[]{:S(2)}) copy-start(s32[2]{0:T(128)} %param.11) | copy-start | bytes 28
  75.5 5.5 %collective-permute-start.21 = (f32[16,128]{1,0:T(8,128)S(1)}, f32[16,128]{1,0:T(8,128)S(1)}, u32[]{:S(2)}, u32[]{:S(2)}) collective-permute-start(f32[16,128]{1,0:T(8,128)S(1)} %shard_map.81), channel_id=1, source_target_pairs={{0,8},{4,12},{8,16},{12,20},{16,24},{20,28},{24,0},{28,4},{1,9},{5... | collective-permute-start | bytes 24584 | tf_op jit(solution)/shard_map/ppermute | solution.py:20
  75.9 4.5 %collective-permute-start.20 = (f32[16,128]{1,0:T(8,128)S(1)}, f32[16,128]{1,0:T(8,128)S(1)}, u32[]{:S(2)}, u32[]{:S(2)}) collective-permute-start(f32[16,128]{1,0:T(8,128)S(1)} %shard_map.81), channel_id=1, source_target_pairs={{0,20},{4,24},{8,28},{12,0},{16,4},{20,8},{24,12},{28,16},{1,21},{... | collective-permute-start | bytes 24584 | tf_op jit(solution)/shard_map/ppermute | solution.py:20
  77.8 3.2 %collective-permute-start.22 = (bf16[2,128,256]{2,1,0:T(8,128)(2,1)S(1)}, bf16[2,128,256]{2,1,0:T(8,128)(2,1)S(1)}, u32[]{:S(2)}, u32[]{:S(2)}) collective-permute-start(bf16[2,128,256]{2,1,0:T(8,128)(2,1)S(1)} %get-tuple-element.22), channel_id=1, source_target_pairs={{0,1},{1,0},{2,3},{3,2},{4,5},{5,4},{6,7},{7,6},{8,9},{9,8},{10,11... | collective-permute-start | bytes 393224 | tf_op jit(solution)/shard_map/ppermute | solution.py:24
  81.1 5.0 %collective-permute-start.23 = (bf16[2,128,256]{2,1,0:T(8,128)(2,1)S(1)}, bf16[2,128,256]{2,1,0:T(8,128)(2,1)S(1)}, u32[]{:S(2)}, u32[]{:S(2)}) collective-permute-start(bf16[2,128,256]{2,1,0:T(8,128)(2,1)S(1)} %add_convert_fusion.1), channel_id=1, source_target_pairs={{0,2},{1,3},{2,0},{3,1},{4,6},{5,7},{6,4},{7,5},{8,10},{9,11},{10,... | collective-permute-start | bytes 393224 | tf_op jit(solution)/shard_map/ppermute | solution.py:33
  86.8 7.0 %collective-permute-start.25 = (bf16[2,128,256]{2,1,0:T(8,128)(2,1)S(1)}, bf16[2,128,256]{2,1,0:T(8,128)(2,1)S(1)}, u32[]{:S(2)}, u32[]{:S(2)}) collective-permute-start(bf16[2,128,256]{2,1,0:T(8,128)(2,1)S(1)} %fusion.3.refs_1_), channel_id=1, source_target_pairs={{0,28},{4,0},{8,4},{12,8},{16,12},{20,16},{24,20},{28,24},{1,29},{... | collective-permute-start | bytes 393224 | tf_op jit(solution)/shard_map/ppermute | solution.py:20
  91.2 9.1 %collective-permute-start.24 = (bf16[2,128,256]{2,1,0:T(8,128)(2,1)S(1)}, bf16[2,128,256]{2,1,0:T(8,128)(2,1)S(1)}, u32[]{:S(2)}, u32[]{:S(2)}) collective-permute-start(bf16[2,128,256]{2,1,0:T(8,128)(2,1)S(1)} %fusion.3.refs_1_), channel_id=1, source_target_pairs={{0,4},{4,8},{8,12},{12,16},{16,20},{20,24},{24,28},{28,0},{1,5},{5... | collective-permute-start | bytes 393224 | tf_op jit(solution)/shard_map/ppermute | solution.py:20
  91.2 86.2 %collective-permute-start.39 = (bf16[8,2,256,256]{3,2,1,0:T(8,128)(2,1)}, bf16[8,2,256,256]{3,2,1,0:T(8,128)(2,1)}, u32[]{:S(2)}, u32[]{:S(2)}) collective-permute-start(bf16[8,2,256,256]{3,2,1,0:T(8,128)(2,1)} %refs_6_.7), channel_id=1, source_target_pairs={{0,4},{4,8},{8,12},{12,16},{16,20},{20,24},{24,28},{28,0},{1,5},{5... | collective-permute-start | bytes 6291464 | tf_op jit(solution)/shard_map/ppermute | solution.py:20
  91.5 65.8 %collective-permute-start.38 = (s32[2]{0:T(128)S(1)}, s32[2]{0:T(128)S(1)}, u32[]{:S(2)}, u32[]{:S(2)}) collective-permute-start(s32[2]{0:T(128)S(1)} %copy-done.24), channel_id=1, source_target_pairs={{0,4},{4,8},{8,12},{12,16},{16,20},{20,24},{24,28},{28,0},{1,5},{5... | collective-permute-start | bytes 32 | tf_op jit(solution)/shard_map/ppermute | solution.py:20
  91.8 10.3 %collective-permute-start.27 = (bf16[2,128,256]{2,1,0:T(8,128)(2,1)S(1)}, bf16[2,128,256]{2,1,0:T(8,128)(2,1)S(1)}, u32[]{:S(2)}, u32[]{:S(2)}) collective-permute-start(bf16[2,128,256]{2,1,0:T(8,128)(2,1)S(1)} %fusion.3.refs_1_), channel_id=1, source_target_pairs={{0,1},{1,0},{2,3},{3,2},{4,5},{5,4},{6,7},{7,6},{8,9},{9,8},{10,11... | collective-permute-start | bytes 393224 | tf_op jit(solution)/shard_map/ppermute | solution.py:24
  93.8 8.3 %collective-permute-start.28 = (bf16[2,128,256]{2,1,0:T(8,128)(2,1)S(1)}, bf16[2,128,256]{2,1,0:T(8,128)(2,1)S(1)}, u32[]{:S(2)}, u32[]{:S(2)}) collective-permute-start(bf16[2,128,256]{2,1,0:T(8,128)(2,1)S(1)} %collective-permute-done.25.refs_2_), channel_id=1, source_target_pairs={{0,1},{1,0},{2,3},{3,2},{4,5},{5,4},{6,7},{7,6},{8,9},{9,8},{10,11... | collective-permute-start | bytes 393224 | tf_op jit(solution)/shard_map/ppermute | solution.py:24
  100.4 1.7 collective-permute-start.26
  104.2 51.7 %copy-start.17 = (bf16[2,128,256]{2,1,0:T(8,128)(2,1)S(1)}, bf16[2,128,256]{2,1,0:T(8,128)(2,1)}, u32[]{:S(2)}) copy-start(bf16[2,128,256]{2,1,0:T(8,128)(2,1)} %copy-done.16) | copy-start | bytes 393220
  104.2 51.7 %copy-start.21 = (bf16[2,128,256]{2,1,0:T(8,128)(2,1)S(1)}, bf16[2,128,256]{2,1,0:T(8,128)(2,1)}, u32[]{:S(2)}) copy-start(bf16[2,128,256]{2,1,0:T(8,128)(2,1)} %copy-done.20) | copy-start | bytes 393220
  105.0 58.9 %copy-start.8 = (f32[6,256,256]{2,1,0:T(8,128)S(1)}, f32[6,256,256]{2,1,0:T(8,128)}, u32[]{:S(2)}) copy-start(f32[6,256,256]{2,1,0:T(8,128)} %copy-done.7) | copy-start | bytes 4718596
  105.0 45.8 %collective-permute-start.30 = (f32[16,128]{1,0:T(8,128)S(1)}, f32[16,128]{1,0:T(8,128)S(1)}, u32[]{:S(2)}, u32[]{:S(2)}) collective-permute-start(f32[16,128]{1,0:T(8,128)S(1)} %shard_map.83), channel_id=1, source_target_pairs={{0,8},{4,12},{8,16},{12,20},{16,24},{20,28},{24,0},{28,4},{1,9},{5... | collective-permute-start | bytes 24584 | tf_op jit(solution)/shard_map/ppermute | solution.py:20
  146.2 4.5 %collective-permute-start.29 = (f32[16,128]{1,0:T(8,128)S(1)}, f32[16,128]{1,0:T(8,128)S(1)}, u32[]{:S(2)}, u32[]{:S(2)}) collective-permute-start(f32[16,128]{1,0:T(8,128)S(1)} %shard_map.83), channel_id=1, source_target_pairs={{0,20},{4,24},{8,28},{12,0},{16,4},{20,8},{24,12},{28,16},{1,21},{... | collective-permute-start | bytes 24584 | tf_op jit(solution)/shard_map/ppermute | solution.py:20
  147.2 3.6 %collective-permute-start.31 = (bf16[2,128,256]{2,1,0:T(8,128)(2,1)S(1)}, bf16[2,128,256]{2,1,0:T(8,128)(2,1)S(1)}, u32[]{:S(2)}, u32[]{:S(2)}) collective-permute-start(bf16[2,128,256]{2,1,0:T(8,128)(2,1)S(1)} %get-tuple-element.25), channel_id=1, source_target_pairs={{0,1},{1,0},{2,3},{3,2},{4,5},{5,4},{6,7},{7,6},{8,9},{9,8},{10,11... | collective-permute-start | bytes 393224 | tf_op jit(solution)/shard_map/ppermute | solution.py:24
  150.9 5.0 %collective-permute-start.32 = (bf16[2,128,256]{2,1,0:T(8,128)(2,1)S(1)}, bf16[2,128,256]{2,1,0:T(8,128)(2,1)S(1)}, u32[]{:S(2)}, u32[]{:S(2)}) collective-permute-start(bf16[2,128,256]{2,1,0:T(8,128)(2,1)S(1)} %add_convert_fusion), channel_id=1, source_target_pairs={{0,2},{1,3},{2,0},{3,1},{4,6},{5,7},{6,4},{7,5},{8,10},{9,11},{10,... | collective-permute-start | bytes 393224 | tf_op jit(solution)/shard_map/ppermute | solution.py:33
  156.1 7.7 %collective-permute-start.33 = (bf16[2,128,256]{2,1,0:T(8,128)(2,1)S(1)}, bf16[2,128,256]{2,1,0:T(8,128)(2,1)S(1)}, u32[]{:S(2)}, u32[]{:S(2)}) collective-permute-start(bf16[2,128,256]{2,1,0:T(8,128)(2,1)S(1)} %multiply_convert_fusion.1), channel_id=1, source_target_pairs={{0,4},{4,8},{8,12},{12,16},{16,20},{20,24},{24,28},{28,0},{1,5},{5... | collective-permute-start | bytes 393224 | tf_op jit(solution)/shard_map/ppermute | solution.py:20
  163.9 1.6 collective-permute-start.34
  165.8 6.4 %collective-permute-start.37 = (f32[16,128]{1,0:T(8,128)S(1)}, f32[16,128]{1,0:T(8,128)S(1)}, u32[]{:S(2)}, u32[]{:S(2)}) collective-permute-start(f32[16,128]{1,0:T(8,128)S(1)} %shard_map.84), channel_id=1, source_target_pairs={{0,8},{4,12},{8,16},{12,20},{16,24},{20,28},{24,0},{28,4},{1,9},{5... | collective-permute-start | bytes 24584 | tf_op jit(solution)/shard_map/ppermute | solution.py:20
  165.9 6.3 %collective-permute-start.36 = (f32[16,128]{1,0:T(8,128)S(1)}, f32[16,128]{1,0:T(8,128)S(1)}, u32[]{:S(2)}, u32[]{:S(2)}) collective-permute-start(f32[16,128]{1,0:T(8,128)S(1)} %shard_map.84), channel_id=1, source_target_pairs={{0,16},{4,20},{8,24},{12,28},{16,0},{20,4},{24,8},{28,12},{1,17},{... | collective-permute-start | bytes 24584 | tf_op jit(solution)/shard_map/ppermute | solution.py:20
  168.5 3.7 %collective-permute-start.35 = (f32[16,128]{1,0:T(8,128)S(1)}, f32[16,128]{1,0:T(8,128)S(1)}, u32[]{:S(2)}, u32[]{:S(2)}) collective-permute-start(f32[16,128]{1,0:T(8,128)S(1)} %shard_map.84), channel_id=1, source_target_pairs={{0,24},{4,28},{8,0},{12,4},{16,8},{20,12},{24,16},{28,20},{1,25},{... | collective-permute-start | bytes 24584 | tf_op jit(solution)/shard_map/ppermute | solution.py:20
  (17 other events, 71.3 us)

commit v2 on v0

v2 whole, which is shorter than its diff:
```python
import functools

import jax
import jax.numpy as jnp
from jax import lax
from jax.experimental import pallas as pl
from jax.experimental.pallas import tpu as pltpu
from jax.sharding import PartitionSpec as P

ITERS = 4
step_size = 0.5
PLAN = (4, 4, 4, 4)
STAGE_LIMIT = 52
PACK_FLOPS = 0
GATE = False
APPLY_LIMIT = 8
F32 = jnp.float32
BF16 = jnp.bfloat16
SMEM = pl.BlockSpec(memory_space=pltpu.SMEM)
VMEM = pl.BlockSpec(memory_space=pltpu.VMEM)
ANY = pl.BlockSpec(memory_space=pl.ANY)
HBM = pl.BlockSpec(memory_space=pltpu.HBM)
MIB = 2**20


def sec_move(x, distance):
    count = lax.axis_size("sec")
    return lax.ppermute(x, "sec", [(i, (i + distance) % count) for i in range(count)])


def core_swap(x):
    return lax.ppermute(x, "op", [(i, i ^ 1) for i in range(lax.axis_size("op"))])


def chip_parts(x):
    count = lax.axis_size("op")
    chips = count // 2
    parts = [x]
    for distance in range(1, chips):
        route = [(i, (i + 2 * distance) % count) for i in range(count)]
        parts.append(lax.ppermute(x, "op", route))
    if chips <= 2:
        return parts
    me = lax.axis_index("op") // 2
    stacked = jnp.stack(parts)[(me - jnp.arange(chips)) % chips]
    return [stacked[chip] for chip in range(chips)]


def struct(shape, dtype=F32):
    return jax.ShapeDtypeStruct(shape, dtype)


def call(kernel, outs, ins, specs, limit=4, scratch=(), alias=None, flops=0):
    return pl.pallas_call(
        kernel,
        out_shape=tuple(outs),
        in_specs=specs,
        out_specs=tuple(VMEM for _ in outs),
        scratch_shapes=list(scratch),
        input_output_aliases=alias or {},
        compiler_params=pltpu.CompilerParams(vmem_limit_bytes=limit * MIB),
        cost_estimate=pl.CostEstimate(flops=flops, bytes_accessed=0, transcendentals=0),
    )(*ins)


def row_halves(core, width):
    half = width // 2
    here = pl.ds(pl.multiple_of(core[0] * half, half), half)
    there = pl.ds(pl.multiple_of((1 - core[0]) * half, half), half)
    return here, there


def first_blocks_kernel(left, out, sem):
    copy = pltpu.make_async_copy(left.at[pl.ds(0, out.shape[0])], out, sem)
    copy.start()
    copy.wait()


def first_blocks(left_ops, size):
    _, sectors, width, _ = left_ops.shape
    (terms,) = call(
        first_blocks_kernel,
        [struct((size // sectors,) + left_ops.shape[1:], BF16)],
        (left_ops,),
        [HBM],
        STAGE_LIMIT,
        [pltpu.SemaphoreType.DMA],
    )
    return terms.reshape(size, width, width)


def fill_window(rows, parts, window):
    sectors = window.shape[0] // len(parts[0])
    for side in range(2):
        for group, (ref, place) in enumerate(parts[side]):
            for b in range(sectors):
                yield group * sectors + b, rows[side], ref[place + b]


def products(partner, left, right, window, kept_part, sent_part, halfway, total, rows):
    terms, sectors, width, _ = left.shape
    for b in range(sectors):
        for t in range(terms):
            product = jnp.dot(left[t, b], window[partner[t, b]], preferred_element_type=F32)
            halfway[b, :, t * width : (t + 1) * width] = product.astype(BF16)
        total[b] = jnp.dot(
            halfway[b], right[:, b].reshape(terms * width, width), preferred_element_type=F32
        )
        kept_part[b] = total[b, rows[0], :]
        sent_part[b] = total[b, rows[1], :].astype(BF16)


def emit_blocks(left, first, outs):
    sectors = left.shape[1]
    for out in outs:
        for i in range(out.shape[0]):
            out[i] = left[(first + i) // sectors, (first + i) % sectors]
        first += out.shape[0]


def window_pieces(sectors, own, own_other, pair, pair_other):
    mine = [(pair, 0), (own, 0), (pair, sectors)]
    other = [(pair_other, 0), (own_other, 0), (pair_other, sectors)]
    return mine, other


def first_apply_kernel(emit, core, partner, left, right, *refs):
    pieces, (kept_part, sent_part, window, *blocks, halfway, total) = refs[:4], refs[4:]
    rows = row_halves(core, left.shape[-1])
    for place, row, value in fill_window(rows, window_pieces(left.shape[1], *pieces), window):
        window[place, row, :] = value
    emit_blocks(left, emit, blocks)
    products(partner, left, right, window, kept_part, sent_part, halfway, total, rows)


def step_factors(count, sums):
    sums = jnp.sum(sums, axis=1, keepdims=True)
    energy_sum, norm_sum, square_sum = sums[0:1], sums[1:2], sums[2:3]
    a = 1.0 + step_size * (energy_sum / norm_sum)
    new_norm = a * a * norm_sum - 2.0 * step_size * a * energy_sum + step_size**2 * square_sum
    factor = jnp.sqrt(count / new_norm)
    return factor * a, -step_size * factor


def apply_kernel(emit, count, core, partner, left, right, *refs):
    pieces, refs = refs[:4], refs[4:]
    sums, state, kept_part, sent_part, window, *blocks, halfway, total = refs
    rows = row_halves(core, left.shape[-1])
    alpha, beta = step_factors(count, sums[...])
    for place, row, value in fill_window(rows, window_pieces(left.shape[1], *pieces), window):
        new = alpha * state[place, row, :].astype(F32) + beta * value.astype(F32)
        window[place, row, :] = new.astype(BF16)
    emit_blocks(left, emit, blocks)
    products(partner, left, right, window, kept_part, sent_part, halfway, total, rows)


def apply_terms(core, partner, pieces, left, right, count, sums, state, emit, sizes):
    terms, sectors, width, _ = left.shape
    half = (sectors, width // 2, width)
    outs = [struct(half), struct(half, BF16), struct((3 * sectors, width, width), BF16)]
    outs += [struct((size, width, width), BF16) for size in sizes]
    scratch = [
        pltpu.VMEM((sectors, width, terms * width), BF16),
        pltpu.VMEM((sectors, width, width), F32),
    ]
    ins = (core, partner, left, right, *pieces)
    specs = [SMEM, SMEM] + [VMEM] * 6
    if sums is None:
        kernel = functools.partial(first_apply_kernel, emit)
        return call(kernel, outs, ins, specs, APPLY_LIMIT, scratch)
    kernel = functools.partial(apply_kernel, emit, count)
    specs += [VMEM, VMEM]
    return call(kernel, outs, ins + (sums, state), specs, APPLY_LIMIT, scratch, {9: 2})


def combine_kernel(count, core, shift, state, *refs):
    parts, (rounded, sums) = refs[:count], refs[-2:]
    sectors, half, width = rounded.shape
    here, _ = row_halves(core, width)
    totals = [jnp.zeros((8, width), F32) for _ in range(3)]
    for b in range(sectors):
        total = parts[0][b].astype(F32)
        for part in parts[1:]:
            total = total + part[b].astype(F32)
        s = state[sectors + b, here, :].astype(F32)
        total = total + shift[b] * s
        rounded[b] = total.astype(BF16)
        for i, product in enumerate((s * total, s * s, total * total)):
            totals[i] = totals[i] + jnp.sum(product.reshape(-1, 8, width), axis=0)
    lines = []
    for total in totals:
        lanes = jnp.sum(total, axis=0, keepdims=True)
        lines.append(sum(lanes[:, i : i + 128] for i in range(0, width, 128)))
    lines.append(jnp.zeros((5, 128), F32))
    sums[...] = jnp.concatenate(lines, axis=0)


def pack_kernel(before, after, *refs):
    out = refs[-1]
    sectors = before.shape[0]
    out[:sectors] = before[...]
    out[sectors:] = after[...]


def hold_kernel(*refs):
    pass


def hold(x, *after):
    specs = [VMEM] + [ANY] * len(after)
    return call(hold_kernel, [struct(x.shape, x.dtype)], (x, *after), specs, alias={0: 0})[0]


def finish_kernel(count, sizes, core, kept, sums, state, own, own_other, before, before_other, *refs):
    pieces, refs = refs[: len(sizes)], refs[len(sizes) :]
    final, new_ops, window, results, sems = refs
    sectors, width, _ = final.shape
    alpha, beta = step_factors(count, sums[...])
    rows = row_halves(core, width)
    parts = ([(before, 0), (own, 0)], [(before_other, 0), (own_other, 0)])
    for place, row, value in fill_window(rows, parts, window):
        new = alpha * state[place, row, :].astype(F32) + beta * value.astype(F32)
        window[place, row, :] = new.astype(BF16)
    final[...] = window[sectors:]
    columns = lax.broadcasted_iota(jnp.int32, (width, width), 1)
    blocks = []
    for b in range(sectors):
        block = jnp.where(columns < kept[b], window[b].astype(F32), 0.0).astype(BF16)
        blocks.append((block, block.T))
    copies = []
    unit = 0
    for piece, size in zip(pieces, sizes):
        for i in range(size):
            t, b = unit // sectors, unit % sectors
            block, flipped = blocks[b]
            projected = jnp.dot(piece[i], block, preferred_element_type=F32).astype(BF16)
            result = jnp.dot(flipped, projected, preferred_element_type=F32)
            results[t, b] = (result * (1.0 / float(width) ** 0.5)).astype(BF16)
            if b == sectors - 1:
                copy = pltpu.make_async_copy(results.at[t], new_ops.at[t], sems.at[t])
                copy.start()
                copies.append(copy)
            unit += 1
    for copy in copies:
        copy.wait()


def xor_sum(x, axes, masks):
    size = 1
    for axis in axes:
        size *= lax.axis_size(axis)

    def other(mask):
        return lax.ppermute(x, axes, [(i, i ^ mask) for i in range(size)])

    if len(masks) == 1:
        return x + other(masks[0])
    low, high = masks
    both, one, two = other(low ^ high), other(low), other(high)
    return (x + one) + (two + both)


def far_sums(sums):
    devices = lax.axis_size("sec")
    bits = [1 << i for i in range(1, devices.bit_length() - 1)][::-1]
    while bits:
        sums = xor_sum(sums, ("sec",), bits[:2])
        bits = bits[2:]
    return sums


def near_sums(sums):
    return xor_sum(sums, ("sec", "op"), [1, lax.axis_size("op")])


def per_device(state_start, left_ops, right_ops, shift, partner, kept):
    terms, sectors, width, _ = left_ops.shape
    half = width // 2
    devices = lax.axis_size("sec")
    count = float(sectors * devices * width * width)
    core_index = lax.axis_index("op") % 2
    core = core_index.reshape(1).astype(jnp.int32)
    half_shape = (sectors, half, width)
    units = terms * sectors
    plan = list(PLAN[:-1]) + [units - sum(PLAN[:-1])]

    def pack(before, after):
        (pair,) = call(
            pack_kernel,
            [struct((2 * sectors, half, width), BF16)],
            (before, after),
            [VMEM, VMEM],
            flops=PACK_FLOPS,
        )
        return pair

    own = lax.dynamic_slice_in_dim(state_start, core_index * half, half, 1)
    own_other = lax.dynamic_slice_in_dim(state_start, (1 - core_index) * half, half, 1)
    pair = pack(sec_move(own, 1), sec_move(own, -1))
    pieces = [sec_move(first_blocks(left_ops, plan[0]), 1)]
    moved_kept = sec_move(kept, 1)
    sums = state = None
    for iteration in range(ITERS):
        kept_part, sent_part, state, *blocks = apply_terms(
            core,
            partner,
            (own, own_other, pair, core_swap(pair)),
            left_ops,
            right_ops,
            count,
            sums,
            state,
            sum(plan[: iteration + 1]),
            plan[iteration + 1 : iteration + 2],
        )
        chip_part = (kept_part + core_swap(sent_part).astype(F32)).astype(BF16)
        parts = chip_parts(chip_part)
        gates = [pieces[-1]] + ([moved_kept] if iteration == 0 else [])
        own, sums = call(
            functools.partial(combine_kernel, len(parts)),
            [struct(half_shape, BF16), struct((8, 128))],
            (core, shift, state, *parts, *gates),
            [SMEM, SMEM] + [VMEM] * (1 + len(parts)) + [ANY] * len(gates),
        )
        sums = far_sums(sums)
        own_other = core_swap(own)
        before = sec_move(own, 1)
        if iteration < ITERS - 1:
            pair = pack(before, sec_move(own, -1))
            if GATE:
                pair = hold(pair, sums)
            sums = near_sums(sums)
            pieces.append(sec_move(blocks[0], 1))
    if GATE:
        before = hold(before, sums)
    sums = near_sums(sums)
    final, new_ops = pl.pallas_call(
        functools.partial(finish_kernel, count, tuple(plan)),
        out_shape=(struct(state_start.shape, BF16), struct(left_ops.shape, BF16)),
        in_specs=[SMEM] * 2 + [VMEM] * (6 + len(pieces)),
        out_specs=(VMEM, ANY),
        scratch_shapes=[
            pltpu.VMEM((2 * sectors, width, width), BF16),
            pltpu.VMEM(left_ops.shape, BF16),
            pltpu.SemaphoreType.DMA((terms,)),
        ],
        compiler_params=pltpu.CompilerParams(vmem_limit_bytes=8 * MIB),
        cost_estimate=pl.CostEstimate(
            flops=4 * terms * sectors * width**3, bytes_accessed=4 * MIB, transcendentals=0
        ),
    )(core, moved_kept, sums, state, own, own_other, before, core_swap(before), *pieces)
    return final, new_ops


def solution(mesh):
    in_specs = (
        P("sec", None, None),
        P("op", "sec", None, None),
        P("op", "sec", None, None),
        P("sec"),
        P("op", "sec"),
        P("sec"),
    )
    out_specs = (P("sec", None, None), P("op", "sec", None, None))
    return jax.shard_map(
        per_device, mesh=mesh, in_specs=in_specs, out_specs=out_specs, check_vma=False
    )
```

time: 640 us -> 136 us (0.21)
  blocking collectives: 324 us -> 0 us
  waiting for transfers between devices: 217 us -> 63.1 us
  starting transfers between devices: 20.6 us -> 50.1 us
  matrix products: 21.6 us -> 0 us
  between operations: 22.1 us -> 1.06 us
  other arithmetic: 21.1 us -> 0.18 us
  Pallas kernels: 0 us -> 17.3 us
  local copies, waits for them, and re-layouts: 12.1 us -> 4.39 us
    psum x8 -> x0, blocking collectives: 324 us -> none  [the longest x4 165 us: per_device(): new_norm = lax.psum(jnp.sum(updated_part * updated_part), ('sec', 'op'))]
    psum x4 -> x0, waiting for transfers between devices: 132 us -> none  [per_device(): sigma = lax.psum(partial_sigma, 'op') + shift_col * state_wide]
    ppermute x9 -> x55, starting transfers between devices: 20.5 us -> 50.1 us  [the longest x24 26.1 us: other(): return lax.ppermute(x, axes, [(i, i ^ mask) for i in range(size)])]
    dot_general x5 -> x0, matrix products: 21.6 us -> none  [the longest x4 17.3 us: per_device(): jnp.einsum('tbij,tbjk->bik', halfway, right_ops, preferred_element_type=j...]
    ppermute x9 -> x55, waiting for transfers between devices: 84.3 us -> 63.1 us  [the longest x14 51.1 us: sec_move(): lax.ppermute(x, 'sec', [(i, (i + distance) % count) for i in range(count)])]
    pallas_call x0 -> x14, Pallas kernels: none -> 17.3 us  [the longest x13 13.5 us: call(): pl.pallas_call(kernel, out_shape=tuple(outs), in_specs=specs, out_specs=t...]
    reduce_sum x8 -> x0, other arithmetic: 10.7 us -> none  [the longest x4 5.4 us: per_device(): jnp.sum(state_part * state_part)]
    gather x4 -> x0, local copies, waits for them, and re-layouts: 8 us -> none  [per_device(): sources = window[partner]]
  transfers between devices with their start and end apart: 13 -> 55, of which waited for: 13 -> 24; matrix products, arithmetic and copies ran while one was open for 0% -> 0% of each run, Pallas kernels for 0% -> 8%
where the time goes in v2:
time: 136 us
  waiting for transfers between devices  63.1 us (46%)
  starting transfers between devices  50.1 us (37%)
  Pallas kernels  17.3 us (13%)
  local copies, waits for them, and re-layouts  4.39 us (3%)
    ppermute x14, waiting for transfers between devices, sec_move(): lax.ppermute(x, 'sec', [(i, (i + distance) % count) for i in range(count)])  51.1 us
    ppermute x24, starting transfers between devices, other(): return lax.ppermute(x, axes, [(i, i ^ mask) for i in range(size)])  26.1 us
    ppermute x14, starting transfers between devices, sec_move(): lax.ppermute(x, 'sec', [(i, (i + distance) % count) for i in range(count)])  16.4 us
    pallas_call x13, Pallas kernels, call(): pl.pallas_call(kernel, out_shape=tuple(outs), in_specs=specs, out_specs=t...  13.5 us
    ppermute x13, waiting for transfers between devices, core_swap(): lax.ppermute(x, 'op', [(i, i ^ 1) for i in range(lax.axis_size('op'))])  9.78 us
    ppermute x4, starting transfers between devices, chip_parts(): parts.append(lax.ppermute(x, 'op', route))  6.34 us
    pallas_call x1, Pallas kernels, per_device(): pl.pallas_call(functools.partial(finish_kernel, count, tuple(plan)), out_...  3.79 us
    unnamed x17, local copies, waits for them, and re-layouts  3.26 us
  transfers between devices with their start and end apart: 55, of which 24 were waited for; matrix products, arithmetic and copies ran while one was open for 0% of the time, Pallas kernels for 8%

profile of v2, /device:TPU:0, one launch (start us, length us, event | category | flops | bytes accessed | tf_op | source)
XLA Modules:
  0.0 136.1 jit_solution(10449194712676696020)
XLA Ops:
  0.7 1.1 constant_dynamic-slice_fusion
  1.8 6.0 %collective-permute-start.2 = (bf16[2,128,256]{2,1,0:T(8,128)(2,1)S(1)}, bf16[2,128,256]{2,1,0:T(8,128)(2,1)S(1)}, u32[]{:S(2)}, u32[]{:S(2)}) collective-permute-start(bf16[2,128,256]{2,1,0:T(8,128)(2,1)S(1)} %get-tuple-element.49.refs_0_), channel_id=1, source_target_pairs={{0,28},{4,0},{8,4},{12,8},{16,12},{20,16},{24,20},{28,24},{1,29},{... | collective-permute-start | bytes 393224 | tf_op jit(solution)/shard_map/ppermute | solution.py:28
  8.5 2.1 %collective-permute-done.2.after = bf16[2,128,256]{2,1,0:T(8,128)(2,1)S(1)} collective-permute-done((bf16[2,128,256]{2,1,0:T(8,128)(2,1)S(1)}, bf16[2,128,256]{2,1,0:T(8,128)(2,1)S(1)}, u32[]{:S(2)}, u32[]{:S(2)}) %collective-permute-start.2) | collective-permute-done | bytes 131104 | tf_op jit(solution)/shard_map/ppermute | solution.py:28
  10.6 4.9 %collective-permute-done.1.before = bf16[2,128,256]{2,1,0:T(8,128)(2,1)S(1)} collective-permute-done((bf16[2,128,256]{2,1,0:T(8,128)(2,1)S(1)}, bf16[2,128,256]{2,1,0:T(8,128)(2,1)S(1)}, u32[]{:S(2)}, u32[]{:S(2)}) %collective-permute-start.1) | collective-permute-done | bytes 131104 | tf_op jit(solution)/shard_map/ppermute | solution.py:28
  15.6 1.1 shard_map.79
  17.3 1.6 %copy-done.1 = bf16[8,2,256,256]{3,2,1,0:T(8,128)(2,1)S(1)} copy-done((bf16[8,2,256,256]{3,2,1,0:T(8,128)(2,1)S(1)}, bf16[8,2,256,256]{3,2,1,0:T(8,128)(2,1)}, u32[]{:S(2)}) %copy-start.1) | copy-done | bytes 2097176
  18.9 0.9 copy-done.4
  19.8 2.5 %shard_map.78 = (f32[2,128,256]{2,1,0:T(8,128)S(1)}, bf16[2,128,256]{2,1,0:T(8,128)(2,1)S(1)}, bf16[6,256,256]{2,1,0:T(8,128)(2,1)S(1)}, bf16[4,256,256]{2,1,0:T(8,128)(2,1)S(1)}) custom-call(s32[1]{0:T(128)} %bitcast.core, s32[8,2]{1,0:T(8,128)S(1)} %copy.14.partner, bf16[8,2,256,256]{3,2,1,0:T(8,128)(2,1)S(1)} %copy-done, ...), custom_call_target="tpu_custom_call" | custom-call | tf_op jit(solution)/shard_map/pallas_call | solution.py:54
  22.5 1.2 collective-permute-done.4
  23.7 1.6 %collective-permute-start.5 = (bf16[2,128,256]{2,1,0:T(8,128)(2,1)S(1)}, bf16[2,128,256]{2,1,0:T(8,128)(2,1)S(1)}, u32[]{:S(2)}, u32[]{:S(2)}) collective-permute-start(bf16[2,128,256]{2,1,0:T(8,128)(2,1)S(1)} %add_convert_fusion.3.refs_0_), channel_id=1, source_target_pairs={{0,2},{1,3},{2,0},{3,1},{4,6},{5,7},{6,4},{7,5},{8,10},{9,11},{10,... | collective-permute-start | bytes 393224 | tf_op jit(solution)/shard_map/ppermute | solution.py:41
  25.3 8.5 %collective-permute-done.refs_3_.kept = s32[2]{0:T(128)S(1)} collective-permute-done((s32[2]{0:T(128)S(1)}, s32[2]{0:T(128)S(1)}, u32[]{:S(2)}, u32[]{:S(2)}) %collective-permute-start) | collective-permute-done | bytes 40 | tf_op jit(solution)/shard_map/ppermute | solution.py:28
  34.5 2.0 %collective-permute-start.8 = (bf16[2,128,256]{2,1,0:T(8,128)(2,1)S(1)}, bf16[2,128,256]{2,1,0:T(8,128)(2,1)S(1)}, u32[]{:S(2)}, u32[]{:S(2)}) collective-permute-start(bf16[2,128,256]{2,1,0:T(8,128)(2,1)S(1)} %get-tuple-element.28.refs_0_), channel_id=1, source_target_pairs={{0,4},{4,8},{8,12},{12,16},{16,20},{20,24},{24,28},{28,0},{1,5},{5... | collective-permute-start | bytes 393224 | tf_op jit(solution)/shard_map/ppermute | solution.py:28
  36.6 4.4 %collective-permute-start.11 = (f32[8,128]{1,0:T(8,128)S(1)}, f32[8,128]{1,0:T(8,128)S(1)}, u32[]{:S(2)}, u32[]{:S(2)}) collective-permute-start(f32[8,128]{1,0:T(8,128)S(1)} %get-tuple-element.29), channel_id=1, source_target_pairs={{0,16},{4,20},{8,24},{12,28},{16,0},{20,4},{24,8},{28,12},{1,17},{... | collective-permute-start | bytes 12296 | tf_op jit(solution)/shard_map/ppermute | solution.py:254
  40.9 1.5 %collective-permute-done.8.before = bf16[2,128,256]{2,1,0:T(8,128)(2,1)S(1)} collective-permute-done((bf16[2,128,256]{2,1,0:T(8,128)(2,1)S(1)}, bf16[2,128,256]{2,1,0:T(8,128)(2,1)S(1)}, u32[]{:S(2)}, u32[]{:S(2)}) %collective-permute-start.8) | collective-permute-done | bytes 131104 | tf_op jit(solution)/shard_map/ppermute | solution.py:28
  42.7 2.1 %collective-permute-start.15 = (f32[8,128]{1,0:T(8,128)S(1)}, f32[8,128]{1,0:T(8,128)S(1)}, u32[]{:S(2)}, u32[]{:S(2)}) collective-permute-start(f32[8,128]{1,0:T(8,128)S(1)} %add_add_fusion.7), channel_id=1, source_target_pairs={{0,4},{1,5},{2,6},{3,7},{4,0},{5,1},{6,2},{7,3},{8,12},{9,13},{10,... | collective-permute-start | bytes 12296 | tf_op jit(solution)/shard_map/ppermute | solution.py:254
  44.8 1.4 %collective-permute-start.19 = (bf16[4,256,256]{2,1,0:T(8,128)(2,1)S(1)}, bf16[4,256,256]{2,1,0:T(8,128)(2,1)S(1)}, u32[]{:S(2)}, u32[]{:S(2)}) collective-permute-start(bf16[4,256,256]{2,1,0:T(8,128)(2,1)S(1)} %get-tuple-element.33), channel_id=1, source_target_pairs={{0,4},{4,8},{8,12},{12,16},{16,20},{20,24},{24,28},{28,0},{1,5},{5... | collective-permute-start | bytes 1572872 | tf_op jit(solution)/shard_map/ppermute | solution.py:28
  46.5 1.2 collective-permute-done.7.refs_1_
  47.6 2.4 %shard_map.82 = (f32[2,128,256]{2,1,0:T(8,128)S(1)}, bf16[2,128,256]{2,1,0:T(8,128)(2,1)S(1)}, bf16[6,256,256]{2,1,0:T(8,128)(2,1)S(1)}, bf16[4,256,256]{2,1,0:T(8,128)(2,1)S(1)}) custom-call(s32[1]{0:T(128)} %bitcast.core, s32[8,2]{1,0:T(8,128)S(1)} %copy.14.partner, bf16[8,2,256,256]{3,2,1,0:T(8,128)(2,1)S(1)} %copy-done, ...), custom_call_target="tpu_custom_call", output_to_operand_aliasing={{2}: (9, {})} | custom-call | tf_op jit(solution)/shard_map/pallas_call | solution.py:54
  50.3 1.2 collective-permute-done.17
  51.5 1.6 %collective-permute-start.18 = (bf16[2,128,256]{2,1,0:T(8,128)(2,1)S(1)}, bf16[2,128,256]{2,1,0:T(8,128)(2,1)S(1)}, u32[]{:S(2)}, u32[]{:S(2)}) collective-permute-start(bf16[2,128,256]{2,1,0:T(8,128)(2,1)S(1)} %add_convert_fusion.2.refs_0_), channel_id=1, source_target_pairs={{0,2},{1,3},{2,0},{3,1},{4,6},{5,7},{6,4},{7,5},{8,10},{9,11},{10,... | collective-permute-start | bytes 393224 | tf_op jit(solution)/shard_map/ppermute | solution.py:41
  53.1 8.7 %collective-permute-done.19.refs_2_.refs_1_ = bf16[4,256,256]{2,1,0:T(8,128)(2,1)S(1)} collective-permute-done((bf16[4,256,256]{2,1,0:T(8,128)(2,1)S(1)}, bf16[4,256,256]{2,1,0:T(8,128)(2,1)S(1)}, u32[]{:S(2)}, u32[]{:S(2)}) %collective-permute-start.19) | collective-permute-done | bytes 524320 | tf_op jit(solution)/shard_map/ppermute | solution.py:28
  62.6 2.0 %collective-permute-start.21 = (bf16[2,128,256]{2,1,0:T(8,128)(2,1)S(1)}, bf16[2,128,256]{2,1,0:T(8,128)(2,1)S(1)}, u32[]{:S(2)}, u32[]{:S(2)}) collective-permute-start(bf16[2,128,256]{2,1,0:T(8,128)(2,1)S(1)} %get-tuple-element.34.refs_0_), channel_id=1, source_target_pairs={{0,4},{4,8},{8,12},{12,16},{16,20},{20,24},{24,28},{28,0},{1,5},{5... | collective-permute-start | bytes 393224 | tf_op jit(solution)/shard_map/ppermute | solution.py:28
  64.6 0.8 collective-permute-start.25
  65.4 3.6 %collective-permute-start.24 = (f32[8,128]{1,0:T(8,128)S(1)}, f32[8,128]{1,0:T(8,128)S(1)}, u32[]{:S(2)}, u32[]{:S(2)}) collective-permute-start(f32[8,128]{1,0:T(8,128)S(1)} %get-tuple-element.35), channel_id=1, source_target_pairs={{0,16},{4,20},{8,24},{12,28},{16,0},{20,4},{24,8},{28,12},{1,17},{... | collective-permute-start | bytes 12296 | tf_op jit(solution)/shard_map/ppermute | solution.py:254
  69.0 1.6 %collective-permute-done.21.before = bf16[2,128,256]{2,1,0:T(8,128)(2,1)S(1)} collective-permute-done((bf16[2,128,256]{2,1,0:T(8,128)(2,1)S(1)}, bf16[2,128,256]{2,1,0:T(8,128)(2,1)S(1)}, u32[]{:S(2)}, u32[]{:S(2)}) %collective-permute-start.21) | collective-permute-done | bytes 131104 | tf_op jit(solution)/shard_map/ppermute | solution.py:28
  70.9 2.1 %collective-permute-start.28 = (f32[8,128]{1,0:T(8,128)S(1)}, f32[8,128]{1,0:T(8,128)S(1)}, u32[]{:S(2)}, u32[]{:S(2)}) collective-permute-start(f32[8,128]{1,0:T(8,128)S(1)} %add_add_fusion.5), channel_id=1, source_target_pairs={{0,4},{1,5},{2,6},{3,7},{4,0},{5,1},{6,2},{7,3},{8,12},{9,13},{10,... | collective-permute-start | bytes 12296 | tf_op jit(solution)/shard_map/ppermute | solution.py:254
  73.0 1.3 collective-permute-start.32
  74.6 1.0 collective-permute-done.20.refs_1_
  75.7 2.4 %shard_map.85 = (f32[2,128,256]{2,1,0:T(8,128)S(1)}, bf16[2,128,256]{2,1,0:T(8,128)(2,1)S(1)}, bf16[6,256,256]{2,1,0:T(8,128)(2,1)S(1)}, bf16[4,256,256]{2,1,0:T(8,128)(2,1)S(1)}) custom-call(s32[1]{0:T(128)} %bitcast.core, s32[8,2]{1,0:T(8,128)S(1)} %copy.14.partner, bf16[8,2,256,256]{3,2,1,0:T(8,128)(2,1)S(1)} %copy-done, ...), custom_call_target="tpu_custom_call", output_to_operand_aliasing={{2}: (9, {})} | custom-call | tf_op jit(solution)/shard_map/pallas_call | solution.py:54
  78.3 1.2 collective-permute-done.30
  79.6 1.6 %collective-permute-start.31 = (bf16[2,128,256]{2,1,0:T(8,128)(2,1)S(1)}, bf16[2,128,256]{2,1,0:T(8,128)(2,1)S(1)}, u32[]{:S(2)}, u32[]{:S(2)}) collective-permute-start(bf16[2,128,256]{2,1,0:T(8,128)(2,1)S(1)} %add_convert_fusion.1.refs_0_), channel_id=1, source_target_pairs={{0,2},{1,3},{2,0},{3,1},{4,6},{5,7},{6,4},{7,5},{8,10},{9,11},{10,... | collective-permute-start | bytes 393224 | tf_op jit(solution)/shard_map/ppermute | solution.py:41
  81.1 8.9 %collective-permute-done.32.refs_2_ = bf16[4,256,256]{2,1,0:T(8,128)(2,1)S(1)} collective-permute-done((bf16[4,256,256]{2,1,0:T(8,128)(2,1)S(1)}, bf16[4,256,256]{2,1,0:T(8,128)(2,1)S(1)}, u32[]{:S(2)}, u32[]{:S(2)}) %collective-permute-start.32) | collective-permute-done | bytes 524320 | tf_op jit(solution)/shard_map/ppermute | solution.py:28
  90.7 2.0 %collective-permute-start.34 = (bf16[2,128,256]{2,1,0:T(8,128)(2,1)S(1)}, bf16[2,128,256]{2,1,0:T(8,128)(2,1)S(1)}, u32[]{:S(2)}, u32[]{:S(2)}) collective-permute-start(bf16[2,128,256]{2,1,0:T(8,128)(2,1)S(1)} %get-tuple-element.40.refs_0_), channel_id=1, source_target_pairs={{0,4},{4,8},{8,12},{12,16},{16,20},{20,24},{24,28},{28,0},{1,5},{5... | collective-permute-start | bytes 393224 | tf_op jit(solution)/shard_map/ppermute | solution.py:28
  93.4 3.8 %collective-permute-start.37 = (f32[8,128]{1,0:T(8,128)S(1)}, f32[8,128]{1,0:T(8,128)S(1)}, u32[]{:S(2)}, u32[]{:S(2)}) collective-permute-start(f32[8,128]{1,0:T(8,128)S(1)} %get-tuple-element.41), channel_id=1, source_target_pairs={{0,16},{4,20},{8,24},{12,28},{16,0},{20,4},{24,8},{28,12},{1,17},{... | collective-permute-start | bytes 12296 | tf_op jit(solution)/shard_map/ppermute | solution.py:254
  97.2 1.6 %collective-permute-done.34.before = bf16[2,128,256]{2,1,0:T(8,128)(2,1)S(1)} collective-permute-done((bf16[2,128,256]{2,1,0:T(8,128)(2,1)S(1)}, bf16[2,128,256]{2,1,0:T(8,128)(2,1)S(1)}, u32[]{:S(2)}, u32[]{:S(2)}) %collective-permute-start.34) | collective-permute-done | bytes 131104 | tf_op jit(solution)/shard_map/ppermute | solution.py:28
  99.0 2.1 %collective-permute-start.41 = (f32[8,128]{1,0:T(8,128)S(1)}, f32[8,128]{1,0:T(8,128)S(1)}, u32[]{:S(2)}, u32[]{:S(2)}) collective-permute-start(f32[8,128]{1,0:T(8,128)S(1)} %add_add_fusion.3), channel_id=1, source_target_pairs={{0,4},{1,5},{2,6},{3,7},{4,0},{5,1},{6,2},{7,3},{8,12},{9,13},{10,... | collective-permute-start | bytes 12296 | tf_op jit(solution)/shard_map/ppermute | solution.py:254
  101.2 1.3 collective-permute-start.45
  102.8 1.0 collective-permute-done.33.refs_1_
  103.8 2.4 %shard_map.88 = (f32[2,128,256]{2,1,0:T(8,128)S(1)}, bf16[2,128,256]{2,1,0:T(8,128)(2,1)S(1)}, bf16[6,256,256]{2,1,0:T(8,128)(2,1)S(1)}) custom-call(s32[1]{0:T(128)} %bitcast.core, s32[8,2]{1,0:T(8,128)S(1)} %copy.14.partner, bf16[8,2,256,256]{3,2,1,0:T(8,128)(2,1)S(1)} %copy-done, ...), custom_call_target="tpu_custom_call", output_to_operand_aliasing={{2}: (9, {})} | custom-call | tf_op jit(solution)/shard_map/pallas_call | solution.py:54
  106.5 1.2 collective-permute-done.43
  107.7 1.6 %collective-permute-start.44 = (bf16[2,128,256]{2,1,0:T(8,128)(2,1)S(1)}, bf16[2,128,256]{2,1,0:T(8,128)(2,1)S(1)}, u32[]{:S(2)}, u32[]{:S(2)}) collective-permute-start(bf16[2,128,256]{2,1,0:T(8,128)(2,1)S(1)} %add_convert_fusion.refs_0_), channel_id=1, source_target_pairs={{0,2},{1,3},{2,0},{3,1},{4,6},{5,7},{6,4},{7,5},{8,10},{9,11},{10,... | collective-permute-start | bytes 393224 | tf_op jit(solution)/shard_map/ppermute | solution.py:41
  109.3 8.9 %collective-permute-done.45.refs_2_.refs_3_ = bf16[4,256,256]{2,1,0:T(8,128)(2,1)S(1)} collective-permute-done((bf16[4,256,256]{2,1,0:T(8,128)(2,1)S(1)}, bf16[4,256,256]{2,1,0:T(8,128)(2,1)S(1)}, u32[]{:S(2)}, u32[]{:S(2)}) %collective-permute-start.45) | collective-permute-done | bytes 524320 | tf_op jit(solution)/shard_map/ppermute | solution.py:28
  119.5 3.8 %collective-permute-start.46 = (f32[8,128]{1,0:T(8,128)S(1)}, f32[8,128]{1,0:T(8,128)S(1)}, u32[]{:S(2)}, u32[]{:S(2)}) collective-permute-start(f32[8,128]{1,0:T(8,128)S(1)} %get-tuple-element.46), channel_id=1, source_target_pairs={{0,16},{4,20},{8,24},{12,28},{16,0},{20,4},{24,8},{28,12},{1,17},{... | collective-permute-start | bytes 12296 | tf_op jit(solution)/shard_map/ppermute | solution.py:254
  123.3 1.0 collective-permute-done.48
  125.0 1.8 %collective-permute-start.49 = (f32[8,128]{1,0:T(8,128)S(1)}, f32[8,128]{1,0:T(8,128)S(1)}, u32[]{:S(2)}, u32[]{:S(2)}) collective-permute-start(f32[8,128]{1,0:T(8,128)S(1)} %add_add_fusion.1), channel_id=1, source_target_pairs={{0,1},{1,0},{2,3},{3,2},{4,5},{5,4},{6,7},{7,6},{8,9},{9,8},{10,11... | collective-permute-start | bytes 12296 | tf_op jit(solution)/shard_map/ppermute | solution.py:254
  126.8 4.2 %collective-permute-done.53.before = bf16[2,128,256]{2,1,0:T(8,128)(2,1)S(1)} collective-permute-done((bf16[2,128,256]{2,1,0:T(8,128)(2,1)S(1)}, bf16[2,128,256]{2,1,0:T(8,128)(2,1)S(1)}, u32[]{:S(2)}, u32[]{:S(2)}) %collective-permute-start.53) | collective-permute-done | bytes 131104 | tf_op jit(solution)/shard_map/ppermute | solution.py:28
  131.0 1.3 collective-permute-done.54.before_other
  132.3 3.8 %shard_map.90 = (bf16[2,256,256]{2,1,0:T(8,128)(2,1)}, bf16[8,2,256,256]{3,2,1,0:T(8,128)(2,1)}) custom-call(s32[1]{0:T(128)} %bitcast.core, s32[2]{0:T(128)S(1)} %collective-permute-done.refs_3_.kept, f32[8,128]{1,0:T(8,128)S(1)} %add_add_fusion.sums, bf16[6,256,256]{2,1,0:T(8,128)(2,1)S(1)} %get-tuple-element.42.state, ...), custom_call_target="tpu_custom_call" | custom-call | flops 1073741824 | bytes 4194304 | tf_op jit(solution)/shard_map/pallas_call | solution.py:337
  (106 shorter events, 8.5 us)
Async XLA Ops:
  1.8 8.8 %collective-permute-start.2 = (bf16[2,128,256]{2,1,0:T(8,128)(2,1)S(1)}, bf16[2,128,256]{2,1,0:T(8,128)(2,1)S(1)}, u32[]{:S(2)}, u32[]{:S(2)}) collective-permute-start(bf16[2,128,256]{2,1,0:T(8,128)(2,1)S(1)} %get-tuple-element.49.refs_0_), channel_id=1, source_target_pairs={{0,28},{4,0},{8,4},{12,8},{16,12},{20,16},{24,20},{28,24},{1,29},{... | collective-permute-start | bytes 393224 | tf_op jit(solution)/shard_map/ppermute | solution.py:28
  7.8 7.7 %collective-permute-start.1 = (bf16[2,128,256]{2,1,0:T(8,128)(2,1)S(1)}, bf16[2,128,256]{2,1,0:T(8,128)(2,1)S(1)}, u32[]{:S(2)}, u32[]{:S(2)}) collective-permute-start(bf16[2,128,256]{2,1,0:T(8,128)(2,1)S(1)} %get-tuple-element.49.refs_0_), channel_id=1, source_target_pairs={{0,4},{4,8},{8,12},{12,16},{16,20},{20,24},{24,28},{28,0},{1,5},{5... | collective-permute-start | bytes 393224 | tf_op jit(solution)/shard_map/ppermute | solution.py:28
  15.5 1.7 %collective-permute-start.3 = (bf16[4,128,256]{2,1,0:T(8,128)(2,1)S(1)}, bf16[4,128,256]{2,1,0:T(8,128)(2,1)}, u32[]{:S(2)}, u32[]{:S(2)}) collective-permute-start(bf16[4,128,256]{2,1,0:T(8,128)(2,1)S(1)} %shard_map.77.refs_2_), channel_id=1, source_target_pairs={{0,1},{1,0},{2,3},{3,2},{4,5},{5,4},{6,7},{7,6},{8,9},{9,8},{10,11... | collective-permute-start | bytes 786440 | tf_op jit(solution)/shard_map/ppermute | solution.py:32
  16.7 17.1 %collective-permute-start.6 = (bf16[4,256,256]{2,1,0:T(8,128)(2,1)S(1)}, bf16[4,256,256]{2,1,0:T(8,128)(2,1)S(1)}, u32[]{:S(2)}, u32[]{:S(2)}) collective-permute-start(bf16[4,256,256]{2,1,0:T(8,128)(2,1)S(1)} %bitcast.2), channel_id=1, source_target_pairs={{0,4},{4,8},{8,12},{12,16},{16,20},{20,24},{24,28},{28,0},{1,5},{5... | collective-permute-start | bytes 1572872 | tf_op jit(solution)/shard_map/ppermute | solution.py:28
  22.3 1.4 %collective-permute-start.4 = (bf16[2,128,256]{2,1,0:T(8,128)(2,1)S(1)}, bf16[2,128,256]{2,1,0:T(8,128)(2,1)S(1)}, u32[]{:S(2)}, u32[]{:S(2)}) collective-permute-start(bf16[2,128,256]{2,1,0:T(8,128)(2,1)S(1)} %get-tuple-element.27), channel_id=1, source_target_pairs={{0,1},{1,0},{2,3},{3,2},{4,5},{5,4},{6,7},{7,6},{8,9},{9,8},{10,11... | collective-permute-start | bytes 393224 | tf_op jit(solution)/shard_map/ppermute | solution.py:32
  23.7 10.1 %collective-permute-start.5 = (bf16[2,128,256]{2,1,0:T(8,128)(2,1)S(1)}, bf16[2,128,256]{2,1,0:T(8,128)(2,1)S(1)}, u32[]{:S(2)}, u32[]{:S(2)}) collective-permute-start(bf16[2,128,256]{2,1,0:T(8,128)(2,1)S(1)} %add_convert_fusion.3.refs_0_), channel_id=1, source_target_pairs={{0,2},{1,3},{2,0},{3,1},{4,6},{5,7},{6,4},{7,5},{8,10},{9,11},{10,... | collective-permute-start | bytes 393224 | tf_op jit(solution)/shard_map/ppermute | solution.py:41
  25.3 8.5 %collective-permute-start = (s32[2]{0:T(128)S(1)}, s32[2]{0:T(128)S(1)}, u32[]{:S(2)}, u32[]{:S(2)}) collective-permute-start(s32[2]{0:T(128)S(1)} %copy-done.7), channel_id=1, source_target_pairs={{0,4},{4,8},{8,12},{12,16},{16,20},{20,24},{24,28},{28,0},{1,5},{5... | collective-permute-start | bytes 32 | tf_op jit(solution)/shard_map/ppermute | solution.py:28
  34.5 6.5 %collective-permute-start.9 = (bf16[2,128,256]{2,1,0:T(8,128)(2,1)S(1)}, bf16[2,128,256]{2,1,0:T(8,128)(2,1)S(1)}, u32[]{:S(2)}, u32[]{:S(2)}) collective-permute-start(bf16[2,128,256]{2,1,0:T(8,128)(2,1)S(1)} %get-tuple-element.28.refs_0_), channel_id=1, source_target_pairs={{0,28},{4,0},{8,4},{12,8},{16,12},{20,16},{24,20},{28,24},{1,29},{... | collective-permute-start | bytes 393224 | tf_op jit(solution)/shard_map/ppermute | solution.py:28
  34.5 7.9 %collective-permute-start.8 = (bf16[2,128,256]{2,1,0:T(8,128)(2,1)S(1)}, bf16[2,128,256]{2,1,0:T(8,128)(2,1)S(1)}, u32[]{:S(2)}, u32[]{:S(2)}) collective-permute-start(bf16[2,128,256]{2,1,0:T(8,128)(2,1)S(1)} %get-tuple-element.28.refs_0_), channel_id=1, source_target_pairs={{0,4},{4,8},{8,12},{12,16},{16,20},{20,24},{24,28},{28,0},{1,5},{5... | collective-permute-start | bytes 393224 | tf_op jit(solution)/shard_map/ppermute | solution.py:28
  36.6 6.0 %collective-permute-start.13 = (f32[8,128]{1,0:T(8,128)S(1)}, f32[8,128]{1,0:T(8,128)S(1)}, u32[]{:S(2)}, u32[]{:S(2)}) collective-permute-start(f32[8,128]{1,0:T(8,128)S(1)} %get-tuple-element.29), channel_id=1, source_target_pairs={{0,24},{4,28},{8,16},{12,20},{16,8},{20,12},{24,0},{28,4},{1,25},{... | collective-permute-start | bytes 12296 | tf_op jit(solution)/shard_map/ppermute | solution.py:254
  36.6 6.0 %collective-permute-start.12 = (f32[8,128]{1,0:T(8,128)S(1)}, f32[8,128]{1,0:T(8,128)S(1)}, u32[]{:S(2)}, u32[]{:S(2)}) collective-permute-start(f32[8,128]{1,0:T(8,128)S(1)} %get-tuple-element.29), channel_id=1, source_target_pairs={{0,8},{4,12},{8,0},{12,4},{16,24},{20,28},{24,16},{28,20},{1,9},{5... | collective-permute-start | bytes 12296 | tf_op jit(solution)/shard_map/ppermute | solution.py:254
  36.6 6.0 %collective-permute-start.11 = (f32[8,128]{1,0:T(8,128)S(1)}, f32[8,128]{1,0:T(8,128)S(1)}, u32[]{:S(2)}, u32[]{:S(2)}) collective-permute-start(f32[8,128]{1,0:T(8,128)S(1)} %get-tuple-element.29), channel_id=1, source_target_pairs={{0,16},{4,20},{8,24},{12,28},{16,0},{20,4},{24,8},{28,12},{1,17},{... | collective-permute-start | bytes 12296 | tf_op jit(solution)/shard_map/ppermute | solution.py:254
  42.5 5.1 %collective-permute-start.10 = (bf16[4,128,256]{2,1,0:T(8,128)(2,1)S(1)}, bf16[4,128,256]{2,1,0:T(8,128)(2,1)S(1)}, u32[]{:S(2)}, u32[]{:S(2)}) collective-permute-start(bf16[4,128,256]{2,1,0:T(8,128)(2,1)S(1)} %shard_map.81.refs_2_), channel_id=1, source_target_pairs={{0,1},{1,0},{2,3},{3,2},{4,5},{5,4},{6,7},{7,6},{8,9},{9,8},{10,11... | collective-permute-start | bytes 786440 | tf_op jit(solution)/shard_map/ppermute | solution.py:32
  42.6 3.6 %collective-permute-start.16 = (f32[8,128]{1,0:T(8,128)S(1)}, f32[8,128]{1,0:T(8,128)S(1)}, u32[]{:S(2)}, u32[]{:S(2)}) collective-permute-start(f32[8,128]{1,0:T(8,128)S(1)} %add_add_fusion.7), channel_id=1, source_target_pairs={{0,5},{1,4},{2,7},{3,6},{4,1},{5,0},{6,3},{7,2},{8,13},{9,12},{10,... | collective-permute-start | bytes 12296 | tf_op jit(solution)/shard_map/ppermute | solution.py:254
  42.7 3.8 %collective-permute-start.15 = (f32[8,128]{1,0:T(8,128)S(1)}, f32[8,128]{1,0:T(8,128)S(1)}, u32[]{:S(2)}, u32[]{:S(2)}) collective-permute-start(f32[8,128]{1,0:T(8,128)S(1)} %add_add_fusion.7), channel_id=1, source_target_pairs={{0,4},{1,5},{2,6},{3,7},{4,0},{5,1},{6,2},{7,3},{8,12},{9,13},{10,... | collective-permute-start | bytes 12296 | tf_op jit(solution)/shard_map/ppermute | solution.py:254
  44.8 1.6 %collective-permute-start.14 = (f32[8,128]{1,0:T(8,128)S(1)}, f32[8,128]{1,0:T(8,128)S(1)}, u32[]{:S(2)}, u32[]{:S(2)}) collective-permute-start(f32[8,128]{1,0:T(8,128)S(1)} %add_add_fusion.7), channel_id=1, source_target_pairs={{0,1},{1,0},{2,3},{3,2},{4,5},{5,4},{6,7},{7,6},{8,9},{9,8},{10,11... | collective-permute-start | bytes 12296 | tf_op jit(solution)/shard_map/ppermute | solution.py:254
  44.8 17.0 %collective-permute-start.19 = (bf16[4,256,256]{2,1,0:T(8,128)(2,1)S(1)}, bf16[4,256,256]{2,1,0:T(8,128)(2,1)S(1)}, u32[]{:S(2)}, u32[]{:S(2)}) collective-permute-start(bf16[4,256,256]{2,1,0:T(8,128)(2,1)S(1)} %get-tuple-element.33), channel_id=1, source_target_pairs={{0,4},{4,8},{8,12},{12,16},{16,20},{20,24},{24,28},{28,0},{1,5},{5... | collective-permute-start | bytes 1572872 | tf_op jit(solution)/shard_map/ppermute | solution.py:28
  51.5 10.3 %collective-permute-start.18 = (bf16[2,128,256]{2,1,0:T(8,128)(2,1)S(1)}, bf16[2,128,256]{2,1,0:T(8,128)(2,1)S(1)}, u32[]{:S(2)}, u32[]{:S(2)}) collective-permute-start(bf16[2,128,256]{2,1,0:T(8,128)(2,1)S(1)} %add_convert_fusion.2.refs_0_), channel_id=1, source_target_pairs={{0,2},{1,3},{2,0},{3,1},{4,6},{5,7},{6,4},{7,5},{8,10},{9,11},{10,... | collective-permute-start | bytes 393224 | tf_op jit(solution)/shard_map/ppermute | solution.py:41
  62.5 6.5 %collective-permute-start.22 = (bf16[2,128,256]{2,1,0:T(8,128)(2,1)S(1)}, bf16[2,128,256]{2,1,0:T(8,128)(2,1)S(1)}, u32[]{:S(2)}, u32[]{:S(2)}) collective-permute-start(bf16[2,128,256]{2,1,0:T(8,128)(2,1)S(1)} %get-tuple-element.34.refs_0_), channel_id=1, source_target_pairs={{0,28},{4,0},{8,4},{12,8},{16,12},{20,16},{24,20},{28,24},{1,29},{... | collective-permute-start | bytes 393224 | tf_op jit(solution)/shard_map/ppermute | solution.py:28
  62.6 8.1 %collective-permute-start.21 = (bf16[2,128,256]{2,1,0:T(8,128)(2,1)S(1)}, bf16[2,128,256]{2,1,0:T(8,128)(2,1)S(1)}, u32[]{:S(2)}, u32[]{:S(2)}) collective-permute-start(bf16[2,128,256]{2,1,0:T(8,128)(2,1)S(1)} %get-tuple-element.34.refs_0_), channel_id=1, source_target_pairs={{0,4},{4,8},{8,12},{12,16},{16,20},{20,24},{24,28},{28,0},{1,5},{5... | collective-permute-start | bytes 393224 | tf_op jit(solution)/shard_map/ppermute | solution.py:28
  64.6 6.1 %collective-permute-start.26 = (f32[8,128]{1,0:T(8,128)S(1)}, f32[8,128]{1,0:T(8,128)S(1)}, u32[]{:S(2)}, u32[]{:S(2)}) collective-permute-start(f32[8,128]{1,0:T(8,128)S(1)} %get-tuple-element.35), channel_id=1, source_target_pairs={{0,24},{4,28},{8,16},{12,20},{16,8},{20,12},{24,0},{28,4},{1,25},{... | collective-permute-start | bytes 12296 | tf_op jit(solution)/shard_map/ppermute | solution.py:254
  64.6 6.2 %collective-permute-start.25 = (f32[8,128]{1,0:T(8,128)S(1)}, f32[8,128]{1,0:T(8,128)S(1)}, u32[]{:S(2)}, u32[]{:S(2)}) collective-permute-start(f32[8,128]{1,0:T(8,128)S(1)} %get-tuple-element.35), channel_id=1, source_target_pairs={{0,8},{4,12},{8,0},{12,4},{16,24},{20,28},{24,16},{28,20},{1,9},{5... | collective-permute-start | bytes 12296 | tf_op jit(solution)/shard_map/ppermute | solution.py:254
  65.4 5.4 %collective-permute-start.24 = (f32[8,128]{1,0:T(8,128)S(1)}, f32[8,128]{1,0:T(8,128)S(1)}, u32[]{:S(2)}, u32[]{:S(2)}) collective-permute-start(f32[8,128]{1,0:T(8,128)S(1)} %get-tuple-element.35), channel_id=1, source_target_pairs={{0,16},{4,20},{8,24},{12,28},{16,0},{20,4},{24,8},{28,12},{1,17},{... | collective-permute-start | bytes 12296 | tf_op jit(solution)/shard_map/ppermute | solution.py:254
  70.7 5.0 %collective-permute-start.23 = (bf16[4,128,256]{2,1,0:T(8,128)(2,1)S(1)}, bf16[4,128,256]{2,1,0:T(8,128)(2,1)S(1)}, u32[]{:S(2)}, u32[]{:S(2)}) collective-permute-start(bf16[4,128,256]{2,1,0:T(8,128)(2,1)S(1)} %shard_map.84.refs_2_), channel_id=1, source_target_pairs={{0,1},{1,0},{2,3},{3,2},{4,5},{5,4},{6,7},{7,6},{8,9},{9,8},{10,11... | collective-permute-start | bytes 786440 | tf_op jit(solution)/shard_map/ppermute | solution.py:32
  70.8 3.5 %collective-permute-start.29 = (f32[8,128]{1,0:T(8,128)S(1)}, f32[8,128]{1,0:T(8,128)S(1)}, u32[]{:S(2)}, u32[]{:S(2)}) collective-permute-start(f32[8,128]{1,0:T(8,128)S(1)} %add_add_fusion.5), channel_id=1, source_target_pairs={{0,5},{1,4},{2,7},{3,6},{4,1},{5,0},{6,3},{7,2},{8,13},{9,12},{10,... | collective-permute-start | bytes 12296 | tf_op jit(solution)/shard_map/ppermute | solution.py:254
  70.9 3.8 %collective-permute-start.28 = (f32[8,128]{1,0:T(8,128)S(1)}, f32[8,128]{1,0:T(8,128)S(1)}, u32[]{:S(2)}, u32[]{:S(2)}) collective-permute-start(f32[8,128]{1,0:T(8,128)S(1)} %add_add_fusion.5), channel_id=1, source_target_pairs={{0,4},{1,5},{2,6},{3,7},{4,0},{5,1},{6,2},{7,3},{8,12},{9,13},{10,... | collective-permute-start | bytes 12296 | tf_op jit(solution)/shard_map/ppermute | solution.py:254
  73.0 1.6 %collective-permute-start.27 = (f32[8,128]{1,0:T(8,128)S(1)}, f32[8,128]{1,0:T(8,128)S(1)}, u32[]{:S(2)}, u32[]{:S(2)}) collective-permute-start(f32[8,128]{1,0:T(8,128)S(1)} %add_add_fusion.5), channel_id=1, source_target_pairs={{0,1},{1,0},{2,3},{3,2},{4,5},{5,4},{6,7},{7,6},{8,9},{9,8},{10,11... | collective-permute-start | bytes 12296 | tf_op jit(solution)/shard_map/ppermute | solution.py:254
  73.0 17.0 %collective-permute-start.32 = (bf16[4,256,256]{2,1,0:T(8,128)(2,1)S(1)}, bf16[4,256,256]{2,1,0:T(8,128)(2,1)S(1)}, u32[]{:S(2)}, u32[]{:S(2)}) collective-permute-start(bf16[4,256,256]{2,1,0:T(8,128)(2,1)S(1)} %get-tuple-element.39), channel_id=1, source_target_pairs={{0,4},{4,8},{8,12},{12,16},{16,20},{20,24},{24,28},{28,0},{1,5},{5... | collective-permute-start | bytes 1572872 | tf_op jit(solution)/shard_map/ppermute | solution.py:28
  79.6 10.5 %collective-permute-start.31 = (bf16[2,128,256]{2,1,0:T(8,128)(2,1)S(1)}, bf16[2,128,256]{2,1,0:T(8,128)(2,1)S(1)}, u32[]{:S(2)}, u32[]{:S(2)}) collective-permute-start(bf16[2,128,256]{2,1,0:T(8,128)(2,1)S(1)} %add_convert_fusion.1.refs_0_), channel_id=1, source_target_pairs={{0,2},{1,3},{2,0},{3,1},{4,6},{5,7},{6,4},{7,5},{8,10},{9,11},{10,... | collective-permute-start | bytes 393224 | tf_op jit(solution)/shard_map/ppermute | solution.py:41
  90.7 6.5 %collective-permute-start.35 = (bf16[2,128,256]{2,1,0:T(8,128)(2,1)S(1)}, bf16[2,128,256]{2,1,0:T(8,128)(2,1)S(1)}, u32[]{:S(2)}, u32[]{:S(2)}) collective-permute-start(bf16[2,128,256]{2,1,0:T(8,128)(2,1)S(1)} %get-tuple-element.40.refs_0_), channel_id=1, source_target_pairs={{0,28},{4,0},{8,4},{12,8},{16,12},{20,16},{24,20},{28,24},{1,29},{... | collective-permute-start | bytes 393224 | tf_op jit(solution)/shard_map/ppermute | solution.py:28
  90.7 8.1 %collective-permute-start.34 = (bf16[2,128,256]{2,1,0:T(8,128)(2,1)S(1)}, bf16[2,128,256]{2,1,0:T(8,128)(2,1)S(1)}, u32[]{:S(2)}, u32[]{:S(2)}) collective-permute-start(bf16[2,128,256]{2,1,0:T(8,128)(2,1)S(1)} %get-tuple-element.40.refs_0_), channel_id=1, source_target_pairs={{0,4},{4,8},{8,12},{12,16},{16,20},{20,24},{24,28},{28,0},{1,5},{5... | collective-permute-start | bytes 393224 | tf_op jit(solution)/shard_map/ppermute | solution.py:28
  92.8 6.1 %collective-permute-start.39 = (f32[8,128]{1,0:T(8,128)S(1)}, f32[8,128]{1,0:T(8,128)S(1)}, u32[]{:S(2)}, u32[]{:S(2)}) collective-permute-start(f32[8,128]{1,0:T(8,128)S(1)} %get-tuple-element.41), channel_id=1, source_target_pairs={{0,24},{4,28},{8,16},{12,20},{16,8},{20,12},{24,0},{28,4},{1,25},{... | collective-permute-start | bytes 12296 | tf_op jit(solution)/shard_map/ppermute | solution.py:254
  92.8 6.2 %collective-permute-start.38 = (f32[8,128]{1,0:T(8,128)S(1)}, f32[8,128]{1,0:T(8,128)S(1)}, u32[]{:S(2)}, u32[]{:S(2)}) collective-permute-start(f32[8,128]{1,0:T(8,128)S(1)} %get-tuple-element.41), channel_id=1, source_target_pairs={{0,8},{4,12},{8,0},{12,4},{16,24},{20,28},{24,16},{28,20},{1,9},{5... | collective-permute-start | bytes 12296 | tf_op jit(solution)/shard_map/ppermute | solution.py:254
  93.4 5.5 %collective-permute-start.37 = (f32[8,128]{1,0:T(8,128)S(1)}, f32[8,128]{1,0:T(8,128)S(1)}, u32[]{:S(2)}, u32[]{:S(2)}) collective-permute-start(f32[8,128]{1,0:T(8,128)S(1)} %get-tuple-element.41), channel_id=1, source_target_pairs={{0,16},{4,20},{8,24},{12,28},{16,0},{20,4},{24,8},{28,12},{1,17},{... | collective-permute-start | bytes 12296 | tf_op jit(solution)/shard_map/ppermute | solution.py:254
  98.8 5.0 %collective-permute-start.36 = (bf16[4,128,256]{2,1,0:T(8,128)(2,1)S(1)}, bf16[4,128,256]{2,1,0:T(8,128)(2,1)S(1)}, u32[]{:S(2)}, u32[]{:S(2)}) collective-permute-start(bf16[4,128,256]{2,1,0:T(8,128)(2,1)S(1)} %shard_map.87.refs_2_), channel_id=1, source_target_pairs={{0,1},{1,0},{2,3},{3,2},{4,5},{5,4},{6,7},{7,6},{8,9},{9,8},{10,11... | collective-permute-start | bytes 786440 | tf_op jit(solution)/shard_map/ppermute | solution.py:32
  98.9 3.5 %collective-permute-start.42 = (f32[8,128]{1,0:T(8,128)S(1)}, f32[8,128]{1,0:T(8,128)S(1)}, u32[]{:S(2)}, u32[]{:S(2)}) collective-permute-start(f32[8,128]{1,0:T(8,128)S(1)} %add_add_fusion.3), channel_id=1, source_target_pairs={{0,5},{1,4},{2,7},{3,6},{4,1},{5,0},{6,3},{7,2},{8,13},{9,12},{10,... | collective-permute-start | bytes 12296 | tf_op jit(solution)/shard_map/ppermute | solution.py:254
  99.0 3.8 %collective-permute-start.41 = (f32[8,128]{1,0:T(8,128)S(1)}, f32[8,128]{1,0:T(8,128)S(1)}, u32[]{:S(2)}, u32[]{:S(2)}) collective-permute-start(f32[8,128]{1,0:T(8,128)S(1)} %add_add_fusion.3), channel_id=1, source_target_pairs={{0,4},{1,5},{2,6},{3,7},{4,0},{5,1},{6,2},{7,3},{8,12},{9,13},{10,... | collective-permute-start | bytes 12296 | tf_op jit(solution)/shard_map/ppermute | solution.py:254
  101.2 1.6 %collective-permute-start.40 = (f32[8,128]{1,0:T(8,128)S(1)}, f32[8,128]{1,0:T(8,128)S(1)}, u32[]{:S(2)}, u32[]{:S(2)}) collective-permute-start(f32[8,128]{1,0:T(8,128)S(1)} %add_add_fusion.3), channel_id=1, source_target_pairs={{0,1},{1,0},{2,3},{3,2},{4,5},{5,4},{6,7},{7,6},{8,9},{9,8},{10,11... | collective-permute-start | bytes 12296 | tf_op jit(solution)/shard_map/ppermute | solution.py:254
  101.2 17.0 %collective-permute-start.45 = (bf16[4,256,256]{2,1,0:T(8,128)(2,1)S(1)}, bf16[4,256,256]{2,1,0:T(8,128)(2,1)S(1)}, u32[]{:S(2)}, u32[]{:S(2)}) collective-permute-start(bf16[4,256,256]{2,1,0:T(8,128)(2,1)S(1)} %get-tuple-element.45), channel_id=1, source_target_pairs={{0,4},{4,8},{8,12},{12,16},{16,20},{20,24},{24,28},{28,0},{1,5},{5... | collective-permute-start | bytes 1572872 | tf_op jit(solution)/shard_map/ppermute | solution.py:28
  107.7 10.5 %collective-permute-start.44 = (bf16[2,128,256]{2,1,0:T(8,128)(2,1)S(1)}, bf16[2,128,256]{2,1,0:T(8,128)(2,1)S(1)}, u32[]{:S(2)}, u32[]{:S(2)}) collective-permute-start(bf16[2,128,256]{2,1,0:T(8,128)(2,1)S(1)} %add_convert_fusion.refs_0_), channel_id=1, source_target_pairs={{0,2},{1,3},{2,0},{3,1},{4,6},{5,7},{6,4},{7,5},{8,10},{9,11},{10,... | collective-permute-start | bytes 393224 | tf_op jit(solution)/shard_map/ppermute | solution.py:41
  118.8 5.5 %collective-permute-start.48 = (f32[8,128]{1,0:T(8,128)S(1)}, f32[8,128]{1,0:T(8,128)S(1)}, u32[]{:S(2)}, u32[]{:S(2)}) collective-permute-start(f32[8,128]{1,0:T(8,128)S(1)} %get-tuple-element.46), channel_id=1, source_target_pairs={{0,24},{4,28},{8,16},{12,20},{16,8},{20,12},{24,0},{28,4},{1,25},{... | collective-permute-start | bytes 12296 | tf_op jit(solution)/shard_map/ppermute | solution.py:254
  118.9 5.4 %collective-permute-start.47 = (f32[8,128]{1,0:T(8,128)S(1)}, f32[8,128]{1,0:T(8,128)S(1)}, u32[]{:S(2)}, u32[]{:S(2)}) collective-permute-start(f32[8,128]{1,0:T(8,128)S(1)} %get-tuple-element.46), channel_id=1, source_target_pairs={{0,8},{4,12},{8,0},{12,4},{16,24},{20,28},{24,16},{28,20},{1,9},{5... | collective-permute-start | bytes 12296 | tf_op jit(solution)/shard_map/ppermute | solution.py:254
  119.5 5.3 %collective-permute-start.46 = (f32[8,128]{1,0:T(8,128)S(1)}, f32[8,128]{1,0:T(8,128)S(1)}, u32[]{:S(2)}, u32[]{:S(2)}) collective-permute-start(f32[8,128]{1,0:T(8,128)S(1)} %get-tuple-element.46), channel_id=1, source_target_pairs={{0,16},{4,20},{8,24},{12,28},{16,0},{20,4},{24,8},{28,12},{1,17},{... | collective-permute-start | bytes 12296 | tf_op jit(solution)/shard_map/ppermute | solution.py:254
  123.3 7.7 %collective-permute-start.53 = (bf16[2,128,256]{2,1,0:T(8,128)(2,1)S(1)}, bf16[2,128,256]{2,1,0:T(8,128)(2,1)S(1)}, u32[]{:S(2)}, u32[]{:S(2)}) collective-permute-start(bf16[2,128,256]{2,1,0:T(8,128)(2,1)S(1)} %get-tuple-element.47.own), channel_id=1, source_target_pairs={{0,4},{4,8},{8,12},{12,16},{16,20},{20,24},{24,28},{28,0},{1,5},{5... | collective-permute-start | bytes 393224 | tf_op jit(solution)/shard_map/ppermute | solution.py:28
  124.9 6.1 %collective-permute-start.51 = (f32[8,128]{1,0:T(8,128)S(1)}, f32[8,128]{1,0:T(8,128)S(1)}, u32[]{:S(2)}, u32[]{:S(2)}) collective-permute-start(f32[8,128]{1,0:T(8,128)S(1)} %add_add_fusion.1), channel_id=1, source_target_pairs={{0,5},{1,4},{2,7},{3,6},{4,1},{5,0},{6,3},{7,2},{8,13},{9,12},{10,... | collective-permute-start | bytes 12296 | tf_op jit(solution)/shard_map/ppermute | solution.py:254
  124.9 6.1 %collective-permute-start.50 = (f32[8,128]{1,0:T(8,128)S(1)}, f32[8,128]{1,0:T(8,128)S(1)}, u32[]{:S(2)}, u32[]{:S(2)}) collective-permute-start(f32[8,128]{1,0:T(8,128)S(1)} %add_add_fusion.1), channel_id=1, source_target_pairs={{0,4},{1,5},{2,6},{3,7},{4,0},{5,1},{6,2},{7,3},{8,12},{9,13},{10,... | collective-permute-start | bytes 12296 | tf_op jit(solution)/shard_map/ppermute | solution.py:254
  125.0 6.0 %collective-permute-start.49 = (f32[8,128]{1,0:T(8,128)S(1)}, f32[8,128]{1,0:T(8,128)S(1)}, u32[]{:S(2)}, u32[]{:S(2)}) collective-permute-start(f32[8,128]{1,0:T(8,128)S(1)} %add_add_fusion.1), channel_id=1, source_target_pairs={{0,1},{1,0},{2,3},{3,2},{4,5},{5,4},{6,7},{7,6},{8,9},{9,8},{10,11... | collective-permute-start | bytes 12296 | tf_op jit(solution)/shard_map/ppermute | solution.py:254
  126.8 4.3 %collective-permute-start.52 = (bf16[2,128,256]{2,1,0:T(8,128)(2,1)S(1)}, bf16[2,128,256]{2,1,0:T(8,128)(2,1)S(1)}, u32[]{:S(2)}, u32[]{:S(2)}) collective-permute-start(bf16[2,128,256]{2,1,0:T(8,128)(2,1)S(1)} %get-tuple-element.47.own), channel_id=1, source_target_pairs={{0,1},{1,0},{2,3},{3,2},{4,5},{5,4},{6,7},{7,6},{8,9},{9,8},{10,11... | collective-permute-start | bytes 393224 | tf_op jit(solution)/shard_map/ppermute | solution.py:32
  (15 other events, 90.5 us)

commit v3 on v2

--- a/solution.py
+++ b/solution.py
@@ -9,10 +9,10 @@
 
 ITERS = 4
 step_size = 0.5
-PLAN = (4, 4, 4, 4)
+PLAN = (4, 5, 5, 2)
+THREE = True
+LATE = (1, 2, 3)
 STAGE_LIMIT = 52
-PACK_FLOPS = 0
-GATE = False
 APPLY_LIMIT = 8
 F32 = jnp.float32
 BF16 = jnp.bfloat16
@@ -50,7 +50,7 @@
     return jax.ShapeDtypeStruct(shape, dtype)
 
 
-def call(kernel, outs, ins, specs, limit=4, scratch=(), alias=None, flops=0):
+def call(kernel, outs, ins, specs, limit=4, scratch=(), alias=None):
     return pl.pallas_call(
         kernel,
         out_shape=tuple(outs),
@@ -59,7 +59,7 @@
         scratch_shapes=list(scratch),
         input_output_aliases=alias or {},
         compiler_params=pltpu.CompilerParams(vmem_limit_bytes=limit * MIB),
-        cost_estimate=pl.CostEstimate(flops=flops, bytes_accessed=0, transcendentals=0),
+        cost_estimate=pl.CostEstimate(flops=0, bytes_accessed=0, transcendentals=0),
     )(*ins)
 
 
@@ -70,23 +70,28 @@
     return here, there
 
 
-def first_blocks_kernel(left, out, sem):
-    copy = pltpu.make_async_copy(left.at[pl.ds(0, out.shape[0])], out, sem)
-    copy.start()
-    copy.wait()
+def first_blocks_kernel(left, out, sems):
+    sectors = left.shape[1]
+    copies = [
+        pltpu.make_async_copy(left.at[i // sectors, i % sectors], out.at[i], sems.at[i])
+        for i in range(out.shape[0])
+    ]
+    for copy in copies:
+        copy.start()
+    for copy in copies:
+        copy.wait()
 
 
 def first_blocks(left_ops, size):
-    _, sectors, width, _ = left_ops.shape
-    (terms,) = call(
+    width = left_ops.shape[-1]
+    return call(
         first_blocks_kernel,
-        [struct((size // sectors,) + left_ops.shape[1:], BF16)],
+        [struct((size, width, width), BF16)],
         (left_ops,),
         [HBM],
         STAGE_LIMIT,
-        [pltpu.SemaphoreType.DMA],
-    )
-    return terms.reshape(size, width, width)
+        [pltpu.SemaphoreType.DMA((size,))],
+    )[0]
 
 
 def fill_window(rows, parts, window):
@@ -195,11 +200,11 @@
     sums[...] = jnp.concatenate(lines, axis=0)
 
 
-def pack_kernel(before, after, *refs):
-    out = refs[-1]
-    sectors = before.shape[0]
-    out[:sectors] = before[...]
-    out[sectors:] = after[...]
+def pack_kernel(*refs):
+    *parts, out = refs
+    held = parts[0].shape[0]
+    for i, part in enumerate(parts):
+        out[i * held : (i + 1) * held] = part[...]
 
 
 def hold_kernel(*refs):
@@ -211,13 +216,13 @@
     return call(hold_kernel, [struct(x.shape, x.dtype)], (x, *after), specs, alias={0: 0})[0]
 
 
-def finish_kernel(count, sizes, core, kept, sums, state, own, own_other, before, before_other, *refs):
+def finish_kernel(count, sizes, core, kept, sums, state, pair, pair_other, *refs):
     pieces, refs = refs[: len(sizes)], refs[len(sizes) :]
     final, new_ops, window, results, sems = refs
     sectors, width, _ = final.shape
     alpha, beta = step_factors(count, sums[...])
     rows = row_halves(core, width)
-    parts = ([(before, 0), (own, 0)], [(before_other, 0), (own_other, 0)])
+    parts = [[(ref, 0), (ref, sectors)] for ref in (pair, pair_other)]
     for place, row, value in fill_window(rows, parts, window):
         new = alpha * state[place, row, :].astype(F32) + beta * value.astype(F32)
         window[place, row, :] = new.astype(BF16)
@@ -245,27 +250,29 @@
         copy.wait()
 
 
-def xor_sum(x, axes, masks):
+def xor_sum(x, axes, masks, late=()):
     size = 1
     for axis in axes:
         size *= lax.axis_size(axis)
 
-    def other(mask):
-        return lax.ppermute(x, axes, [(i, i ^ mask) for i in range(size)])
+    def other(mask, sent):
+        return lax.ppermute(sent, axes, [(i, i ^ mask) for i in range(size)])
+
+    last = hold(x, *late) if late else x
 
     if len(masks) == 1:
-        return x + other(masks[0])
+        return x + other(masks[0], last)
     low, high = masks
-    both, one, two = other(low ^ high), other(low), other(high)
+    both, one, two = other(low ^ high, x), other(low, x), other(high, last)
     return (x + one) + (two + both)
 
 
-def far_sums(sums):
+def far_sums(sums, late):
     devices = lax.axis_size("sec")
     bits = [1 << i for i in range(1, devices.bit_length() - 1)][::-1]
     while bits:
-        sums = xor_sum(sums, ("sec",), bits[:2])
-        bits = bits[2:]
+        sums = xor_sum(sums, ("sec",), bits[:2], late)
+        bits, late = bits[2:], ()
     return sums
 
 
@@ -283,21 +290,22 @@
     half_shape = (sectors, half, width)
     units = terms * sectors
     plan = list(PLAN[:-1]) + [units - sum(PLAN[:-1])]
-
-    def pack(before, after):
-        (pair,) = call(
+    plan = [size for size in plan if size]
+
+    def pack(*parts):
+        return call(
             pack_kernel,
             [struct((2 * sectors, half, width), BF16)],
-            (before, after),
-            [VMEM, VMEM],
-            flops=PACK_FLOPS,
-        )
-        return pair
+            parts,
+            [VMEM] * len(parts),
+        )[0]
 
     own = lax.dynamic_slice_in_dim(state_start, core_index * half, half, 1)
     own_other = lax.dynamic_slice_in_dim(state_start, (1 - core_index) * half, half, 1)
-    pair = pack(sec_move(own, 1), sec_move(own, -1))
-    pieces = [sec_move(first_blocks(left_ops, plan[0]), 1)]
+    before, after = sec_move(own, 1), sec_move(own, -1)
+    first = first_blocks(left_ops, plan[0])
+    pair = pack(before, hold(after, first))
+    pieces = [sec_move(first, 1)]
     moved_kept = sec_move(kept, 1)
     sums = state = None
     for iteration in range(ITERS):
@@ -315,29 +323,30 @@
         )
         chip_part = (kept_part + core_swap(sent_part).astype(F32)).astype(BF16)
         parts = chip_parts(chip_part)
-        gates = [pieces[-1]] + ([moved_kept] if iteration == 0 else [])
+        gates = [moved_kept] if iteration == 0 else []
+        late = [pieces[-1]] if len(pieces) > iteration else []
+        if iteration not in LATE:
+            gates, late = gates + late, []
         own, sums = call(
             functools.partial(combine_kernel, len(parts)),
             [struct(half_shape, BF16), struct((8, 128))],
             (core, shift, state, *parts, *gates),
             [SMEM, SMEM] + [VMEM] * (1 + len(parts)) + [ANY] * len(gates),
         )
-        sums = far_sums(sums)
-        own_other = core_swap(own)
-        before = sec_move(own, 1)
+        sums = far_sums(sums, late)
         if iteration < ITERS - 1:
-            pair = pack(before, sec_move(own, -1))
-            if GATE:
-                pair = hold(pair, sums)
-            sums = near_sums(sums)
-            pieces.append(sec_move(blocks[0], 1))
-    if GATE:
-        before = hold(before, sums)
-    sums = near_sums(sums)
+            own_other = core_swap(own)
+            pair = pack(sec_move(own, 1), sec_move(own, -1))
+            if blocks:
+                pieces.append(sec_move(blocks[0], 1))
+        else:
+            pair = pack(sec_move(own, 1), own)
+        sums = near_sums(sums)
+    pair_other = core_swap(pair)
     final, new_ops = pl.pallas_call(
         functools.partial(finish_kernel, count, tuple(plan)),
         out_shape=(struct(state_start.shape, BF16), struct(left_ops.shape, BF16)),
-        in_specs=[SMEM] * 2 + [VMEM] * (6 + len(pieces)),
+        in_specs=[SMEM] * 2 + [VMEM] * (4 + len(pieces)),
         out_specs=(VMEM, ANY),
         scratch_shapes=[
             pltpu.VMEM((2 * sectors, width, width), BF16),
@@ -348,7 +357,7 @@
         cost_estimate=pl.CostEstimate(
             flops=4 * terms * sectors * width**3, bytes_accessed=4 * MIB, transcendentals=0
         ),
-    )(core, moved_kept, sums, state, own, own_other, before, core_swap(before), *pieces)
+    )(core, moved_kept, sums, state, pair, pair_other, *pieces)
     return final, new_ops
 
 

time: 136 us -> 129 us (0.949)
  waiting for transfers between devices: 63.1 us -> 52.5 us
  starting transfers between devices: 50.1 us -> 53.8 us
    ppermute x14, waiting for transfers between devices: 51.1 us -> 28.4 us  [sec_move(): lax.ppermute(x, 'sec', [(i, (i + distance) % count) for i in range(count)])]
    ppermute x4, waiting for transfers between devices: 0.01 us -> 12.3 us  [chip_parts(): parts.append(lax.ppermute(x, 'op', route))]
    ppermute x14, starting transfers between devices: 16.4 us -> 19.4 us  [sec_move(): lax.ppermute(x, 'sec', [(i, (i + distance) % count) for i in range(count)])]
    ppermute x13 -> x12, waiting for transfers between devices: 9.78 us -> 6.89 us  [core_swap(): lax.ppermute(x, 'op', [(i, i ^ 1) for i in range(lax.axis_size('op'))])]
    ppermute x24, waiting for transfers between devices: 2.25 us -> 4.87 us  [other(): return lax.ppermute(sent, axes, [(i, i ^ mask) for i in range(size)])]
    ppermute x13 -> x12, starting transfers between devices: 1.3 us -> 3.17 us  [core_swap(): lax.ppermute(x, 'op', [(i, i ^ 1) for i in range(lax.axis_size('op'))])]
    unnamed x17 -> x20, local copies, waits for them, and re-layouts: 3.26 us -> 2.61 us
    pallas_call x13 -> x18, Pallas kernels: 13.5 us -> 13.6 us  [call(): pl.pallas_call(kernel, out_shape=tuple(outs), in_specs=specs, out_specs=t...]
  transfers between devices with their start and end apart: 55 -> 54, of which waited for: 24 -> 26; matrix products, arithmetic and copies ran while one was open for 0% -> 0% of each run, Pallas kernels for 8% -> 8%
where the time goes in v3:
time: 129 us; the launch traced here: 128 us
  starting transfers between devices  53.8 us (42%)
  waiting for transfers between devices  52.5 us (41%)
  Pallas kernels  17.4 us (13%)
  local copies, waits for them, and re-layouts  3.61 us (3%)
    ppermute x14, waiting for transfers between devices, sec_move(): lax.ppermute(x, 'sec', [(i, (i + distance) % count) for i in range(count)])  28.4 us
    ppermute x24, starting transfers between devices, other(): return lax.ppermute(sent, axes, [(i, i ^ mask) for i in range(size)])  24.9 us
    ppermute x14, starting transfers between devices, sec_move(): lax.ppermute(x, 'sec', [(i, (i + distance) % count) for i in range(count)])  19.4 us
    pallas_call x18, Pallas kernels, call(): pl.pallas_call(kernel, out_shape=tuple(outs), in_specs=specs, out_specs=t...  13.6 us
    ppermute x4, waiting for transfers between devices, chip_parts(): parts.append(lax.ppermute(x, 'op', route))  12.3 us
    ppermute x12, waiting for transfers between devices, core_swap(): lax.ppermute(x, 'op', [(i, i ^ 1) for i in range(lax.axis_size('op'))])  6.89 us
    ppermute x4, starting transfers between devices, chip_parts(): parts.append(lax.ppermute(x, 'op', route))  6.35 us
    ppermute x24, waiting for transfers between devices, other(): return lax.ppermute(sent, axes, [(i, i ^ mask) for i in range(size)])  4.87 us
  transfers between devices with their start and end apart: 54, of which 26 were waited for; matrix products, arithmetic and copies ran while one was open for 0% of the time, Pallas kernels for 8%

profile of v3, /device:TPU:0, one launch (start us, length us, event | category | flops | bytes accessed | tf_op | source)
XLA Modules:
  0.0 128.5 jit_solution(138483717837324735)
XLA Ops:
  0.6 1.0 constant_dynamic-slice_fusion
  1.7 6.0 %collective-permute-start.2 = (bf16[2,128,256]{2,1,0:T(8,128)(2,1)S(1)}, bf16[2,128,256]{2,1,0:T(8,128)(2,1)S(1)}, u32[]{:S(2)}, u32[]{:S(2)}) collective-permute-start(bf16[2,128,256]{2,1,0:T(8,128)(2,1)S(1)} %get-tuple-element.49.refs_0_), channel_id=1, source_target_pairs={{0,28},{4,0},{8,4},{12,8},{16,12},{20,16},{24,20},{28,24},{1,29},{... | collective-permute-start | bytes 393224 | tf_op jit(solution)/shard_map/ppermute | solution.py:28
  7.7 1.1 shard_map.77.refs_1_
  8.9 1.6 %collective-permute-done.2.refs_0_ = bf16[2,128,256]{2,1,0:T(8,128)(2,1)S(1)} collective-permute-done((bf16[2,128,256]{2,1,0:T(8,128)(2,1)S(1)}, bf16[2,128,256]{2,1,0:T(8,128)(2,1)S(1)}, u32[]{:S(2)}, u32[]{:S(2)}) %collective-permute-start.2) | collective-permute-done | bytes 131104 | tf_op jit(solution)/shard_map/ppermute | solution.py:28
  10.5 4.9 %collective-permute-done.1.refs_0_ = bf16[2,128,256]{2,1,0:T(8,128)(2,1)S(1)} collective-permute-done((bf16[2,128,256]{2,1,0:T(8,128)(2,1)S(1)}, bf16[2,128,256]{2,1,0:T(8,128)(2,1)S(1)}, u32[]{:S(2)}, u32[]{:S(2)}) %collective-permute-start.1) | collective-permute-done | bytes 131104 | tf_op jit(solution)/shard_map/ppermute | solution.py:28
  15.6 1.5 %collective-permute-done.3.refs_3_ = bf16[4,128,256]{2,1,0:T(8,128)(2,1)} collective-permute-done((bf16[4,128,256]{2,1,0:T(8,128)(2,1)S(1)}, bf16[4,128,256]{2,1,0:T(8,128)(2,1)}, u32[]{:S(2)}, u32[]{:S(2)}) %collective-permute-start.3) | collective-permute-done | bytes 262176 | tf_op jit(solution)/shard_map/ppermute | solution.py:32
  17.1 1.6 %copy-done.1 = bf16[8,2,256,256]{3,2,1,0:T(8,128)(2,1)S(1)} copy-done((bf16[8,2,256,256]{3,2,1,0:T(8,128)(2,1)S(1)}, bf16[8,2,256,256]{3,2,1,0:T(8,128)(2,1)}, u32[]{:S(2)}) %copy-start.1) | copy-done | bytes 2097176
  19.6 2.5 %shard_map.80 = (f32[2,128,256]{2,1,0:T(8,128)S(1)}, bf16[2,128,256]{2,1,0:T(8,128)(2,1)S(1)}, bf16[6,256,256]{2,1,0:T(8,128)(2,1)S(1)}, bf16[5,256,256]{2,1,0:T(8,128)(2,1)S(1)}) custom-call(s32[1]{0:T(128)} %bitcast.core, s32[8,2]{1,0:T(8,128)S(1)} %copy.18.partner, bf16[8,2,256,256]{3,2,1,0:T(8,128)(2,1)S(1)} %copy-done, ...), custom_call_target="tpu_custom_call" | custom-call | tf_op jit(solution)/shard_map/pallas_call | solution.py:54
  22.3 1.2 collective-permute-done.4
  23.6 1.6 %collective-permute-start.5 = (bf16[2,128,256]{2,1,0:T(8,128)(2,1)S(1)}, bf16[2,128,256]{2,1,0:T(8,128)(2,1)S(1)}, u32[]{:S(2)}, u32[]{:S(2)}) collective-permute-start(bf16[2,128,256]{2,1,0:T(8,128)(2,1)S(1)} %add_convert_fusion.3.refs_0_), channel_id=1, source_target_pairs={{0,2},{1,3},{2,0},{3,1},{4,6},{5,7},{6,4},{7,5},{8,10},{9,11},{10,... | collective-permute-start | bytes 393224 | tf_op jit(solution)/shard_map/ppermute | solution.py:41
  25.2 7.4 %collective-permute-done.refs_2_.kept = s32[2]{0:T(128)S(1)} collective-permute-done((s32[2]{0:T(128)S(1)}, s32[2]{0:T(128)S(1)}, u32[]{:S(2)}, u32[]{:S(2)}) %collective-permute-start) | collective-permute-done | bytes 40 | tf_op jit(solution)/shard_map/ppermute | solution.py:28
  33.3 2.0 %collective-permute-start.8 = (bf16[2,128,256]{2,1,0:T(8,128)(2,1)S(1)}, bf16[2,128,256]{2,1,0:T(8,128)(2,1)S(1)}, u32[]{:S(2)}, u32[]{:S(2)}) collective-permute-start(bf16[2,128,256]{2,1,0:T(8,128)(2,1)S(1)} %get-tuple-element.28.refs_0_), channel_id=1, source_target_pairs={{0,4},{4,8},{8,12},{12,16},{16,20},{20,24},{24,28},{28,0},{1,5},{5... | collective-permute-start | bytes 393224 | tf_op jit(solution)/shard_map/ppermute | solution.py:28
  35.3 4.4 %collective-permute-start.11 = (f32[8,128]{1,0:T(8,128)S(1)}, f32[8,128]{1,0:T(8,128)S(1)}, u32[]{:S(2)}, u32[]{:S(2)}) collective-permute-start(f32[8,128]{1,0:T(8,128)S(1)} %get-tuple-element.29), channel_id=1, source_target_pairs={{0,16},{4,20},{8,24},{12,28},{16,0},{20,4},{24,8},{28,12},{1,17},{... | collective-permute-start | bytes 12296 | tf_op jit(solution)/shard_map/ppermute | solution.py:259
  39.7 1.5 %collective-permute-done.8.refs_0_ = bf16[2,128,256]{2,1,0:T(8,128)(2,1)S(1)} collective-permute-done((bf16[2,128,256]{2,1,0:T(8,128)(2,1)S(1)}, bf16[2,128,256]{2,1,0:T(8,128)(2,1)S(1)}, u32[]{:S(2)}, u32[]{:S(2)}) %collective-permute-start.8) | collective-permute-done | bytes 131104 | tf_op jit(solution)/shard_map/ppermute | solution.py:28
  41.4 2.1 %collective-permute-start.15 = (f32[8,128]{1,0:T(8,128)S(1)}, f32[8,128]{1,0:T(8,128)S(1)}, u32[]{:S(2)}, u32[]{:S(2)}) collective-permute-start(f32[8,128]{1,0:T(8,128)S(1)} %add_add_fusion.7), channel_id=1, source_target_pairs={{0,4},{1,5},{2,6},{3,7},{4,0},{5,1},{6,2},{7,3},{8,12},{9,13},{10,... | collective-permute-start | bytes 12296 | tf_op jit(solution)/shard_map/ppermute | solution.py:259
  43.5 1.5 %collective-permute-start.24 = (bf16[5,256,256]{2,1,0:T(8,128)(2,1)S(1)}, bf16[5,256,256]{2,1,0:T(8,128)(2,1)S(1)}, u32[]{:S(2)}, u32[]{:S(2)}) collective-permute-start(bf16[5,256,256]{2,1,0:T(8,128)(2,1)S(1)} %get-tuple-element.35), channel_id=1, source_target_pairs={{0,4},{4,8},{8,12},{12,16},{16,20},{20,24},{24,28},{28,0},{1,5},{5... | collective-permute-start | bytes 1966088 | tf_op jit(solution)/shard_map/ppermute | solution.py:28
  45.2 1.2 collective-permute-done.7.refs_1_
  46.4 2.4 %shard_map.83 = (f32[2,128,256]{2,1,0:T(8,128)S(1)}, bf16[2,128,256]{2,1,0:T(8,128)(2,1)S(1)}, bf16[6,256,256]{2,1,0:T(8,128)(2,1)S(1)}, bf16[5,256,256]{2,1,0:T(8,128)(2,1)S(1)}) custom-call(s32[1]{0:T(128)} %bitcast.core, s32[8,2]{1,0:T(8,128)S(1)} %copy.18.partner, bf16[8,2,256,256]{3,2,1,0:T(8,128)(2,1)S(1)} %copy-done, ...), custom_call_target="tpu_custom_call", output_to_operand_aliasing={{2}: (9, {})} | custom-call | tf_op jit(solution)/shard_map/pallas_call | solution.py:54
  49.1 1.2 collective-permute-done.17
  50.3 1.6 %collective-permute-start.18 = (bf16[2,128,256]{2,1,0:T(8,128)(2,1)S(1)}, bf16[2,128,256]{2,1,0:T(8,128)(2,1)S(1)}, u32[]{:S(2)}, u32[]{:S(2)}) collective-permute-start(bf16[2,128,256]{2,1,0:T(8,128)(2,1)S(1)} %add_convert_fusion.2.refs_0_), channel_id=1, source_target_pairs={{0,2},{1,3},{2,0},{3,1},{4,6},{5,7},{6,4},{7,5},{8,10},{9,11},{10,... | collective-permute-start | bytes 393224 | tf_op jit(solution)/shard_map/ppermute | solution.py:41
  51.9 4.0 %collective-permute-done.18.refs_1_ = bf16[2,128,256]{2,1,0:T(8,128)(2,1)S(1)} collective-permute-done((bf16[2,128,256]{2,1,0:T(8,128)(2,1)S(1)}, bf16[2,128,256]{2,1,0:T(8,128)(2,1)S(1)}, u32[]{:S(2)}, u32[]{:S(2)}) %collective-permute-start.18) | collective-permute-done | bytes 131104 | tf_op jit(solution)/shard_map/ppermute | solution.py:41
  56.6 3.3 %collective-permute-start.21 = (bf16[2,128,256]{2,1,0:T(8,128)(2,1)S(1)}, bf16[2,128,256]{2,1,0:T(8,128)(2,1)S(1)}, u32[]{:S(2)}, u32[]{:S(2)}) collective-permute-start(bf16[2,128,256]{2,1,0:T(8,128)(2,1)S(1)} %get-tuple-element.33.refs_0_), channel_id=1, source_target_pairs={{0,28},{4,0},{8,4},{12,8},{16,12},{20,16},{24,20},{28,24},{1,29},{... | collective-permute-start | bytes 393224 | tf_op jit(solution)/shard_map/ppermute | solution.py:28
  60.6 1.6 %collective-permute-start.23 = (f32[8,128]{1,0:T(8,128)S(1)}, f32[8,128]{1,0:T(8,128)S(1)}, u32[]{:S(2)}, u32[]{:S(2)}) collective-permute-start(f32[8,128]{1,0:T(8,128)S(1)} %get-tuple-element.34), channel_id=1, source_target_pairs={{0,16},{4,20},{8,24},{12,28},{16,0},{20,4},{24,8},{28,12},{1,17},{... | collective-permute-start | bytes 12296 | tf_op jit(solution)/shard_map/ppermute | solution.py:259
  62.1 1.3 %collective-permute-done.24.refs_1_ = bf16[5,256,256]{2,1,0:T(8,128)(2,1)S(1)} collective-permute-done((bf16[5,256,256]{2,1,0:T(8,128)(2,1)S(1)}, bf16[5,256,256]{2,1,0:T(8,128)(2,1)S(1)}, u32[]{:S(2)}, u32[]{:S(2)}) %collective-permute-start.24) | collective-permute-done | bytes 655392 | tf_op jit(solution)/shard_map/ppermute | solution.py:28
  63.5 1.5 %collective-permute-start.25 = (f32[8,128]{1,0:T(8,128)S(1)}, f32[8,128]{1,0:T(8,128)S(1)}, u32[]{:S(2)}, u32[]{:S(2)}) collective-permute-start(f32[8,128]{1,0:T(8,128)S(1)} %shard_map.86), channel_id=1, source_target_pairs={{0,8},{4,12},{8,0},{12,4},{16,24},{20,28},{24,16},{28,20},{1,9},{5... | collective-permute-start | bytes 12296 | tf_op jit(solution)/shard_map/ppermute | solution.py:259
  65.0 4.0 %collective-permute-done.21.refs_1_ = bf16[2,128,256]{2,1,0:T(8,128)(2,1)S(1)} collective-permute-done((bf16[2,128,256]{2,1,0:T(8,128)(2,1)S(1)}, bf16[2,128,256]{2,1,0:T(8,128)(2,1)S(1)}, u32[]{:S(2)}, u32[]{:S(2)}) %collective-permute-start.21) | collective-permute-done | bytes 131104 | tf_op jit(solution)/shard_map/ppermute | solution.py:28
  69.2 2.1 %collective-permute-start.28 = (f32[8,128]{1,0:T(8,128)S(1)}, f32[8,128]{1,0:T(8,128)S(1)}, u32[]{:S(2)}, u32[]{:S(2)}) collective-permute-start(f32[8,128]{1,0:T(8,128)S(1)} %add_add_fusion.5), channel_id=1, source_target_pairs={{0,4},{1,5},{2,6},{3,7},{4,0},{5,1},{6,2},{7,3},{8,12},{9,13},{10,... | collective-permute-start | bytes 12296 | tf_op jit(solution)/shard_map/ppermute | solution.py:259
  73.7 2.4 %shard_map.87 = (f32[2,128,256]{2,1,0:T(8,128)S(1)}, bf16[2,128,256]{2,1,0:T(8,128)(2,1)S(1)}, bf16[6,256,256]{2,1,0:T(8,128)(2,1)S(1)}, bf16[2,256,256]{2,1,0:T(8,128)(2,1)S(1)}) custom-call(s32[1]{0:T(128)} %bitcast.core, s32[8,2]{1,0:T(8,128)S(1)} %copy.18.partner, bf16[8,2,256,256]{3,2,1,0:T(8,128)(2,1)S(1)} %copy-done, ...), custom_call_target="tpu_custom_call", output_to_operand_aliasing={{2}: (9, {})} | custom-call | tf_op jit(solution)/shard_map/pallas_call | solution.py:54
  77.6 1.6 %collective-permute-start.31 = (bf16[2,128,256]{2,1,0:T(8,128)(2,1)S(1)}, bf16[2,128,256]{2,1,0:T(8,128)(2,1)S(1)}, u32[]{:S(2)}, u32[]{:S(2)}) collective-permute-start(bf16[2,128,256]{2,1,0:T(8,128)(2,1)S(1)} %add_convert_fusion.1.refs_0_), channel_id=1, source_target_pairs={{0,2},{1,3},{2,0},{3,1},{4,6},{5,7},{6,4},{7,5},{8,10},{9,11},{10,... | collective-permute-start | bytes 393224 | tf_op jit(solution)/shard_map/ppermute | solution.py:41
  79.2 4.2 %collective-permute-done.31.refs_1_ = bf16[2,128,256]{2,1,0:T(8,128)(2,1)S(1)} collective-permute-done((bf16[2,128,256]{2,1,0:T(8,128)(2,1)S(1)}, bf16[2,128,256]{2,1,0:T(8,128)(2,1)S(1)}, u32[]{:S(2)}, u32[]{:S(2)}) %collective-permute-start.31) | collective-permute-done | bytes 131104 | tf_op jit(solution)/shard_map/ppermute | solution.py:41
  84.1 3.6 %collective-permute-start.34 = (bf16[2,128,256]{2,1,0:T(8,128)(2,1)S(1)}, bf16[2,128,256]{2,1,0:T(8,128)(2,1)S(1)}, u32[]{:S(2)}, u32[]{:S(2)}) collective-permute-start(bf16[2,128,256]{2,1,0:T(8,128)(2,1)S(1)} %get-tuple-element.39.refs_0_), channel_id=1, source_target_pairs={{0,28},{4,0},{8,4},{12,8},{16,12},{20,16},{24,20},{28,24},{1,29},{... | collective-permute-start | bytes 393224 | tf_op jit(solution)/shard_map/ppermute | solution.py:28
  87.7 3.6 %collective-permute-done.37.refs_1_.refs_2_ = bf16[5,256,256]{2,1,0:T(8,128)(2,1)S(1)} collective-permute-done((bf16[5,256,256]{2,1,0:T(8,128)(2,1)S(1)}, bf16[5,256,256]{2,1,0:T(8,128)(2,1)S(1)}, u32[]{:S(2)}, u32[]{:S(2)}) %collective-permute-start.37) | collective-permute-done | bytes 655392 | tf_op jit(solution)/shard_map/ppermute | solution.py:28
  91.3 1.7 %collective-permute-start.39 = (f32[8,128]{1,0:T(8,128)S(1)}, f32[8,128]{1,0:T(8,128)S(1)}, u32[]{:S(2)}, u32[]{:S(2)}) collective-permute-start(f32[8,128]{1,0:T(8,128)S(1)} %get-tuple-element.40), channel_id=1, source_target_pairs={{0,24},{4,28},{8,16},{12,20},{16,8},{20,12},{24,0},{28,4},{1,25},{... | collective-permute-start | bytes 12296 | tf_op jit(solution)/shard_map/ppermute | solution.py:259
  93.0 1.8 %collective-permute-start.36 = (f32[8,128]{1,0:T(8,128)S(1)}, f32[8,128]{1,0:T(8,128)S(1)}, u32[]{:S(2)}, u32[]{:S(2)}) collective-permute-start(f32[8,128]{1,0:T(8,128)S(1)} %get-tuple-element.40), channel_id=1, source_target_pairs={{0,16},{4,20},{8,24},{12,28},{16,0},{20,4},{24,8},{28,12},{1,17},{... | collective-permute-start | bytes 12296 | tf_op jit(solution)/shard_map/ppermute | solution.py:259
  94.8 2.0 %collective-permute-done.34.refs_1_ = bf16[2,128,256]{2,1,0:T(8,128)(2,1)S(1)} collective-permute-done((bf16[2,128,256]{2,1,0:T(8,128)(2,1)S(1)}, bf16[2,128,256]{2,1,0:T(8,128)(2,1)S(1)}, u32[]{:S(2)}, u32[]{:S(2)}) %collective-permute-start.34) | collective-permute-done | bytes 131104 | tf_op jit(solution)/shard_map/ppermute | solution.py:28
  97.5 2.5 %collective-permute-start.41 = (f32[8,128]{1,0:T(8,128)S(1)}, f32[8,128]{1,0:T(8,128)S(1)}, u32[]{:S(2)}, u32[]{:S(2)}) collective-permute-start(f32[8,128]{1,0:T(8,128)S(1)} %add_add_fusion.3), channel_id=1, source_target_pairs={{0,4},{1,5},{2,6},{3,7},{4,0},{5,1},{6,2},{7,3},{8,12},{9,13},{10,... | collective-permute-start | bytes 12296 | tf_op jit(solution)/shard_map/ppermute | solution.py:259
  100.6 1.1 collective-permute-done.41
  101.7 2.4 %shard_map.91 = (f32[2,128,256]{2,1,0:T(8,128)S(1)}, bf16[2,128,256]{2,1,0:T(8,128)(2,1)S(1)}, bf16[6,256,256]{2,1,0:T(8,128)(2,1)S(1)}) custom-call(s32[1]{0:T(128)} %bitcast.core, s32[8,2]{1,0:T(8,128)S(1)} %copy.18.partner, bf16[8,2,256,256]{3,2,1,0:T(8,128)(2,1)S(1)} %copy-done, ...), custom_call_target="tpu_custom_call", output_to_operand_aliasing={{2}: (9, {})} | custom-call | tf_op jit(solution)/shard_map/pallas_call | solution.py:54
  105.1 1.2 collective-permute-start.46
  106.3 1.6 %collective-permute-start.44 = (bf16[2,128,256]{2,1,0:T(8,128)(2,1)S(1)}, bf16[2,128,256]{2,1,0:T(8,128)(2,1)S(1)}, u32[]{:S(2)}, u32[]{:S(2)}) collective-permute-start(bf16[2,128,256]{2,1,0:T(8,128)(2,1)S(1)} %add_convert_fusion.refs_0_), channel_id=1, source_target_pairs={{0,2},{1,3},{2,0},{3,1},{4,6},{5,7},{6,4},{7,5},{8,10},{9,11},{10,... | collective-permute-start | bytes 393224 | tf_op jit(solution)/shard_map/ppermute | solution.py:41
  107.9 4.1 %collective-permute-done.44.refs_1_ = bf16[2,128,256]{2,1,0:T(8,128)(2,1)S(1)} collective-permute-done((bf16[2,128,256]{2,1,0:T(8,128)(2,1)S(1)}, bf16[2,128,256]{2,1,0:T(8,128)(2,1)S(1)}, u32[]{:S(2)}, u32[]{:S(2)}) %collective-permute-start.44) | collective-permute-done | bytes 131104 | tf_op jit(solution)/shard_map/ppermute | solution.py:41
  112.6 1.3 %collective-permute-start.52 = (bf16[2,128,256]{2,1,0:T(8,128)(2,1)S(1)}, bf16[2,128,256]{2,1,0:T(8,128)(2,1)S(1)}, u32[]{:S(2)}, u32[]{:S(2)}) collective-permute-start(bf16[2,128,256]{2,1,0:T(8,128)(2,1)S(1)} %get-tuple-element.47.refs_1_), channel_id=1, source_target_pairs={{0,4},{4,8},{8,12},{12,16},{16,20},{20,24},{24,28},{28,0},{1,5},{5... | collective-permute-start | bytes 393224 | tf_op jit(solution)/shard_map/ppermute | solution.py:28
  113.9 2.5 %collective-permute-start.48 = (f32[8,128]{1,0:T(8,128)S(1)}, f32[8,128]{1,0:T(8,128)S(1)}, u32[]{:S(2)}, u32[]{:S(2)}) collective-permute-start(f32[8,128]{1,0:T(8,128)S(1)} %get-tuple-element.45), channel_id=1, source_target_pairs={{0,24},{4,28},{8,16},{12,20},{16,8},{20,12},{24,0},{28,4},{1,25},{... | collective-permute-start | bytes 12296 | tf_op jit(solution)/shard_map/ppermute | solution.py:259
  116.4 1.9 %collective-permute-start.47 = (f32[8,128]{1,0:T(8,128)S(1)}, f32[8,128]{1,0:T(8,128)S(1)}, u32[]{:S(2)}, u32[]{:S(2)}) collective-permute-start(f32[8,128]{1,0:T(8,128)S(1)} %shard_map.93), channel_id=1, source_target_pairs={{0,8},{4,12},{8,0},{12,4},{16,24},{20,28},{24,16},{28,20},{1,9},{5... | collective-permute-start | bytes 12296 | tf_op jit(solution)/shard_map/ppermute | solution.py:259
  118.3 2.1 %collective-permute-done.52.refs_0_ = bf16[2,128,256]{2,1,0:T(8,128)(2,1)S(1)} collective-permute-done((bf16[2,128,256]{2,1,0:T(8,128)(2,1)S(1)}, bf16[2,128,256]{2,1,0:T(8,128)(2,1)S(1)}, u32[]{:S(2)}, u32[]{:S(2)}) %collective-permute-start.52) | collective-permute-done | bytes 131104 | tf_op jit(solution)/shard_map/ppermute | solution.py:28
  121.0 1.7 %collective-permute-start.50 = (f32[8,128]{1,0:T(8,128)S(1)}, f32[8,128]{1,0:T(8,128)S(1)}, u32[]{:S(2)}, u32[]{:S(2)}) collective-permute-start(f32[8,128]{1,0:T(8,128)S(1)} %add_add_fusion.1), channel_id=1, source_target_pairs={{0,4},{1,5},{2,6},{3,7},{4,0},{5,1},{6,2},{7,3},{8,12},{9,13},{10,... | collective-permute-start | bytes 12296 | tf_op jit(solution)/shard_map/ppermute | solution.py:259
  122.9 1.2 collective-permute-done.51
  124.7 3.8 %shard_map.95 = (bf16[2,256,256]{2,1,0:T(8,128)(2,1)}, bf16[8,2,256,256]{3,2,1,0:T(8,128)(2,1)}) custom-call(s32[1]{0:T(128)} %bitcast.core, s32[2]{0:T(128)S(1)} %collective-permute-done.refs_2_.kept, f32[8,128]{1,0:T(8,128)S(1)} %add_add_fusion.sums, bf16[6,256,256]{2,1,0:T(8,128)(2,1)S(1)} %get-tuple-element.42.state, ...), custom_call_target="tpu_custom_call" | custom-call | flops 1073741824 | bytes 4194304 | tf_op jit(solution)/shard_map/pallas_call | solution.py:346
  (112 shorter events, 13.0 us)
Async XLA Ops:
  1.7 8.8 %collective-permute-start.2 = (bf16[2,128,256]{2,1,0:T(8,128)(2,1)S(1)}, bf16[2,128,256]{2,1,0:T(8,128)(2,1)S(1)}, u32[]{:S(2)}, u32[]{:S(2)}) collective-permute-start(bf16[2,128,256]{2,1,0:T(8,128)(2,1)S(1)} %get-tuple-element.49.refs_0_), channel_id=1, source_target_pairs={{0,28},{4,0},{8,4},{12,8},{16,12},{20,16},{24,20},{28,24},{1,29},{... | collective-permute-start | bytes 393224 | tf_op jit(solution)/shard_map/ppermute | solution.py:28
  7.7 7.7 %collective-permute-start.1 = (bf16[2,128,256]{2,1,0:T(8,128)(2,1)S(1)}, bf16[2,128,256]{2,1,0:T(8,128)(2,1)S(1)}, u32[]{:S(2)}, u32[]{:S(2)}) collective-permute-start(bf16[2,128,256]{2,1,0:T(8,128)(2,1)S(1)} %get-tuple-element.49.refs_0_), channel_id=1, source_target_pairs={{0,4},{4,8},{8,12},{12,16},{16,20},{20,24},{24,28},{28,0},{1,5},{5... | collective-permute-start | bytes 393224 | tf_op jit(solution)/shard_map/ppermute | solution.py:28
  15.4 1.7 %collective-permute-start.3 = (bf16[4,128,256]{2,1,0:T(8,128)(2,1)S(1)}, bf16[4,128,256]{2,1,0:T(8,128)(2,1)}, u32[]{:S(2)}, u32[]{:S(2)}) collective-permute-start(bf16[4,128,256]{2,1,0:T(8,128)(2,1)S(1)} %shard_map.79.refs_2_), channel_id=1, source_target_pairs={{0,1},{1,0},{2,3},{3,2},{4,5},{5,4},{6,7},{7,6},{8,9},{9,8},{10,11... | collective-permute-start | bytes 786440 | tf_op jit(solution)/shard_map/ppermute | solution.py:32
  15.5 17.1 %collective-permute-start.6 = (bf16[4,256,256]{2,1,0:T(8,128)(2,1)S(1)}, bf16[4,256,256]{2,1,0:T(8,128)(2,1)S(1)}, u32[]{:S(2)}, u32[]{:S(2)}) collective-permute-start(bf16[4,256,256]{2,1,0:T(8,128)(2,1)S(1)} %shard_map.77.refs_1_), channel_id=1, source_target_pairs={{0,4},{4,8},{8,12},{12,16},{16,20},{20,24},{24,28},{28,0},{1,5},{5... | collective-permute-start | bytes 1572872 | tf_op jit(solution)/shard_map/ppermute | solution.py:28
  23.6 9.0 %collective-permute-start.5 = (bf16[2,128,256]{2,1,0:T(8,128)(2,1)S(1)}, bf16[2,128,256]{2,1,0:T(8,128)(2,1)S(1)}, u32[]{:S(2)}, u32[]{:S(2)}) collective-permute-start(bf16[2,128,256]{2,1,0:T(8,128)(2,1)S(1)} %add_convert_fusion.3.refs_0_), channel_id=1, source_target_pairs={{0,2},{1,3},{2,0},{3,1},{4,6},{5,7},{6,4},{7,5},{8,10},{9,11},{10,... | collective-permute-start | bytes 393224 | tf_op jit(solution)/shard_map/ppermute | solution.py:41
  25.2 7.4 %collective-permute-start = (s32[2]{0:T(128)S(1)}, s32[2]{0:T(128)S(1)}, u32[]{:S(2)}, u32[]{:S(2)}) collective-permute-start(s32[2]{0:T(128)S(1)} %copy-done.7), channel_id=1, source_target_pairs={{0,4},{4,8},{8,12},{12,16},{16,20},{20,24},{24,28},{28,0},{1,5},{5... | collective-permute-start | bytes 32 | tf_op jit(solution)/shard_map/ppermute | solution.py:28
  33.2 6.5 %collective-permute-start.9 = (bf16[2,128,256]{2,1,0:T(8,128)(2,1)S(1)}, bf16[2,128,256]{2,1,0:T(8,128)(2,1)S(1)}, u32[]{:S(2)}, u32[]{:S(2)}) collective-permute-start(bf16[2,128,256]{2,1,0:T(8,128)(2,1)S(1)} %get-tuple-element.28.refs_0_), channel_id=1, source_target_pairs={{0,28},{4,0},{8,4},{12,8},{16,12},{20,16},{24,20},{28,24},{1,29},{... | collective-permute-start | bytes 393224 | tf_op jit(solution)/shard_map/ppermute | solution.py:28
  33.3 7.9 %collective-permute-start.8 = (bf16[2,128,256]{2,1,0:T(8,128)(2,1)S(1)}, bf16[2,128,256]{2,1,0:T(8,128)(2,1)S(1)}, u32[]{:S(2)}, u32[]{:S(2)}) collective-permute-start(bf16[2,128,256]{2,1,0:T(8,128)(2,1)S(1)} %get-tuple-element.28.refs_0_), channel_id=1, source_target_pairs={{0,4},{4,8},{8,12},{12,16},{16,20},{20,24},{24,28},{28,0},{1,5},{5... | collective-permute-start | bytes 393224 | tf_op jit(solution)/shard_map/ppermute | solution.py:28
  35.3 6.0 %collective-permute-start.13 = (f32[8,128]{1,0:T(8,128)S(1)}, f32[8,128]{1,0:T(8,128)S(1)}, u32[]{:S(2)}, u32[]{:S(2)}) collective-permute-start(f32[8,128]{1,0:T(8,128)S(1)} %get-tuple-element.29), channel_id=1, source_target_pairs={{0,24},{4,28},{8,16},{12,20},{16,8},{20,12},{24,0},{28,4},{1,25},{... | collective-permute-start | bytes 12296 | tf_op jit(solution)/shard_map/ppermute | solution.py:259
  35.3 6.0 %collective-permute-start.12 = (f32[8,128]{1,0:T(8,128)S(1)}, f32[8,128]{1,0:T(8,128)S(1)}, u32[]{:S(2)}, u32[]{:S(2)}) collective-permute-start(f32[8,128]{1,0:T(8,128)S(1)} %get-tuple-element.29), channel_id=1, source_target_pairs={{0,8},{4,12},{8,0},{12,4},{16,24},{20,28},{24,16},{28,20},{1,9},{5... | collective-permute-start | bytes 12296 | tf_op jit(solution)/shard_map/ppermute | solution.py:259
  35.3 6.0 %collective-permute-start.11 = (f32[8,128]{1,0:T(8,128)S(1)}, f32[8,128]{1,0:T(8,128)S(1)}, u32[]{:S(2)}, u32[]{:S(2)}) collective-permute-start(f32[8,128]{1,0:T(8,128)S(1)} %get-tuple-element.29), channel_id=1, source_target_pairs={{0,16},{4,20},{8,24},{12,28},{16,0},{20,4},{24,8},{28,12},{1,17},{... | collective-permute-start | bytes 12296 | tf_op jit(solution)/shard_map/ppermute | solution.py:259
  41.2 5.2 %collective-permute-start.10 = (bf16[4,128,256]{2,1,0:T(8,128)(2,1)S(1)}, bf16[4,128,256]{2,1,0:T(8,128)(2,1)S(1)}, u32[]{:S(2)}, u32[]{:S(2)}) collective-permute-start(bf16[4,128,256]{2,1,0:T(8,128)(2,1)S(1)} %shard_map.82.refs_2_), channel_id=1, source_target_pairs={{0,1},{1,0},{2,3},{3,2},{4,5},{5,4},{6,7},{7,6},{8,9},{9,8},{10,11... | collective-permute-start | bytes 786440 | tf_op jit(solution)/shard_map/ppermute | solution.py:32
  41.3 3.7 %collective-permute-start.16 = (f32[8,128]{1,0:T(8,128)S(1)}, f32[8,128]{1,0:T(8,128)S(1)}, u32[]{:S(2)}, u32[]{:S(2)}) collective-permute-start(f32[8,128]{1,0:T(8,128)S(1)} %add_add_fusion.7), channel_id=1, source_target_pairs={{0,5},{1,4},{2,7},{3,6},{4,1},{5,0},{6,3},{7,2},{8,13},{9,12},{10,... | collective-permute-start | bytes 12296 | tf_op jit(solution)/shard_map/ppermute | solution.py:259
  41.4 3.8 %collective-permute-start.15 = (f32[8,128]{1,0:T(8,128)S(1)}, f32[8,128]{1,0:T(8,128)S(1)}, u32[]{:S(2)}, u32[]{:S(2)}) collective-permute-start(f32[8,128]{1,0:T(8,128)S(1)} %add_add_fusion.7), channel_id=1, source_target_pairs={{0,4},{1,5},{2,6},{3,7},{4,0},{5,1},{6,2},{7,3},{8,12},{9,13},{10,... | collective-permute-start | bytes 12296 | tf_op jit(solution)/shard_map/ppermute | solution.py:259
  43.5 1.6 %collective-permute-start.14 = (f32[8,128]{1,0:T(8,128)S(1)}, f32[8,128]{1,0:T(8,128)S(1)}, u32[]{:S(2)}, u32[]{:S(2)}) collective-permute-start(f32[8,128]{1,0:T(8,128)S(1)} %add_add_fusion.7), channel_id=1, source_target_pairs={{0,1},{1,0},{2,3},{3,2},{4,5},{5,4},{6,7},{7,6},{8,9},{9,8},{10,11... | collective-permute-start | bytes 12296 | tf_op jit(solution)/shard_map/ppermute | solution.py:259
  43.5 19.9 %collective-permute-start.24 = (bf16[5,256,256]{2,1,0:T(8,128)(2,1)S(1)}, bf16[5,256,256]{2,1,0:T(8,128)(2,1)S(1)}, u32[]{:S(2)}, u32[]{:S(2)}) collective-permute-start(bf16[5,256,256]{2,1,0:T(8,128)(2,1)S(1)} %get-tuple-element.35), channel_id=1, source_target_pairs={{0,4},{4,8},{8,12},{12,16},{16,20},{20,24},{24,28},{28,0},{1,5},{5... | collective-permute-start | bytes 1966088 | tf_op jit(solution)/shard_map/ppermute | solution.py:28
  50.3 5.6 %collective-permute-start.18 = (bf16[2,128,256]{2,1,0:T(8,128)(2,1)S(1)}, bf16[2,128,256]{2,1,0:T(8,128)(2,1)S(1)}, u32[]{:S(2)}, u32[]{:S(2)}) collective-permute-start(bf16[2,128,256]{2,1,0:T(8,128)(2,1)S(1)} %add_convert_fusion.2.refs_0_), channel_id=1, source_target_pairs={{0,2},{1,3},{2,0},{3,1},{4,6},{5,7},{6,4},{7,5},{8,10},{9,11},{10,... | collective-permute-start | bytes 393224 | tf_op jit(solution)/shard_map/ppermute | solution.py:41
  56.6 12.4 %collective-permute-start.21 = (bf16[2,128,256]{2,1,0:T(8,128)(2,1)S(1)}, bf16[2,128,256]{2,1,0:T(8,128)(2,1)S(1)}, u32[]{:S(2)}, u32[]{:S(2)}) collective-permute-start(bf16[2,128,256]{2,1,0:T(8,128)(2,1)S(1)} %get-tuple-element.33.refs_0_), channel_id=1, source_target_pairs={{0,28},{4,0},{8,4},{12,8},{16,12},{20,16},{24,20},{28,24},{1,29},{... | collective-permute-start | bytes 393224 | tf_op jit(solution)/shard_map/ppermute | solution.py:28
  59.9 9.1 %collective-permute-start.20 = (bf16[2,128,256]{2,1,0:T(8,128)(2,1)S(1)}, bf16[2,128,256]{2,1,0:T(8,128)(2,1)S(1)}, u32[]{:S(2)}, u32[]{:S(2)}) collective-permute-start(bf16[2,128,256]{2,1,0:T(8,128)(2,1)S(1)} %get-tuple-element.33.refs_0_), channel_id=1, source_target_pairs={{0,4},{4,8},{8,12},{12,16},{16,20},{20,24},{24,28},{28,0},{1,5},{5... | collective-permute-start | bytes 393224 | tf_op jit(solution)/shard_map/ppermute | solution.py:28
  59.9 9.2 %collective-permute-start.26 = (f32[8,128]{1,0:T(8,128)S(1)}, f32[8,128]{1,0:T(8,128)S(1)}, u32[]{:S(2)}, u32[]{:S(2)}) collective-permute-start(f32[8,128]{1,0:T(8,128)S(1)} %get-tuple-element.34), channel_id=1, source_target_pairs={{0,24},{4,28},{8,16},{12,20},{16,8},{20,12},{24,0},{28,4},{1,25},{... | collective-permute-start | bytes 12296 | tf_op jit(solution)/shard_map/ppermute | solution.py:259
  60.6 8.6 %collective-permute-start.23 = (f32[8,128]{1,0:T(8,128)S(1)}, f32[8,128]{1,0:T(8,128)S(1)}, u32[]{:S(2)}, u32[]{:S(2)}) collective-permute-start(f32[8,128]{1,0:T(8,128)S(1)} %get-tuple-element.34), channel_id=1, source_target_pairs={{0,16},{4,20},{8,24},{12,28},{16,0},{20,4},{24,8},{28,12},{1,17},{... | collective-permute-start | bytes 12296 | tf_op jit(solution)/shard_map/ppermute | solution.py:259
  63.5 5.6 %collective-permute-start.25 = (f32[8,128]{1,0:T(8,128)S(1)}, f32[8,128]{1,0:T(8,128)S(1)}, u32[]{:S(2)}, u32[]{:S(2)}) collective-permute-start(f32[8,128]{1,0:T(8,128)S(1)} %shard_map.86), channel_id=1, source_target_pairs={{0,8},{4,12},{8,0},{12,4},{16,24},{20,28},{24,16},{28,20},{1,9},{5... | collective-permute-start | bytes 12296 | tf_op jit(solution)/shard_map/ppermute | solution.py:259
  69.0 4.7 %collective-permute-start.22 = (bf16[4,128,256]{2,1,0:T(8,128)(2,1)S(1)}, bf16[4,128,256]{2,1,0:T(8,128)(2,1)S(1)}, u32[]{:S(2)}, u32[]{:S(2)}) collective-permute-start(bf16[4,128,256]{2,1,0:T(8,128)(2,1)S(1)} %shard_map.85.refs_2_), channel_id=1, source_target_pairs={{0,1},{1,0},{2,3},{3,2},{4,5},{5,4},{6,7},{7,6},{8,9},{9,8},{10,11... | collective-permute-start | bytes 786440 | tf_op jit(solution)/shard_map/ppermute | solution.py:32
  69.1 3.1 %collective-permute-start.29 = (f32[8,128]{1,0:T(8,128)S(1)}, f32[8,128]{1,0:T(8,128)S(1)}, u32[]{:S(2)}, u32[]{:S(2)}) collective-permute-start(f32[8,128]{1,0:T(8,128)S(1)} %add_add_fusion.5), channel_id=1, source_target_pairs={{0,5},{1,4},{2,7},{3,6},{4,1},{5,0},{6,3},{7,2},{8,13},{9,12},{10,... | collective-permute-start | bytes 12296 | tf_op jit(solution)/shard_map/ppermute | solution.py:259
  69.2 3.8 %collective-permute-start.28 = (f32[8,128]{1,0:T(8,128)S(1)}, f32[8,128]{1,0:T(8,128)S(1)}, u32[]{:S(2)}, u32[]{:S(2)}) collective-permute-start(f32[8,128]{1,0:T(8,128)S(1)} %add_add_fusion.5), channel_id=1, source_target_pairs={{0,4},{1,5},{2,6},{3,7},{4,0},{5,1},{6,2},{7,3},{8,12},{9,13},{10,... | collective-permute-start | bytes 12296 | tf_op jit(solution)/shard_map/ppermute | solution.py:259
  71.3 1.6 %collective-permute-start.27 = (f32[8,128]{1,0:T(8,128)S(1)}, f32[8,128]{1,0:T(8,128)S(1)}, u32[]{:S(2)}, u32[]{:S(2)}) collective-permute-start(f32[8,128]{1,0:T(8,128)S(1)} %add_add_fusion.5), channel_id=1, source_target_pairs={{0,1},{1,0},{2,3},{3,2},{4,5},{5,4},{6,7},{7,6},{8,9},{9,8},{10,11... | collective-permute-start | bytes 12296 | tf_op jit(solution)/shard_map/ppermute | solution.py:259
  71.3 19.9 %collective-permute-start.37 = (bf16[5,256,256]{2,1,0:T(8,128)(2,1)S(1)}, bf16[5,256,256]{2,1,0:T(8,128)(2,1)S(1)}, u32[]{:S(2)}, u32[]{:S(2)}) collective-permute-start(bf16[5,256,256]{2,1,0:T(8,128)(2,1)S(1)} %get-tuple-element.41), channel_id=1, source_target_pairs={{0,4},{4,8},{8,12},{12,16},{16,20},{20,24},{24,28},{28,0},{1,5},{5... | collective-permute-start | bytes 1966088 | tf_op jit(solution)/shard_map/ppermute | solution.py:28
  77.6 5.8 %collective-permute-start.31 = (bf16[2,128,256]{2,1,0:T(8,128)(2,1)S(1)}, bf16[2,128,256]{2,1,0:T(8,128)(2,1)S(1)}, u32[]{:S(2)}, u32[]{:S(2)}) collective-permute-start(bf16[2,128,256]{2,1,0:T(8,128)(2,1)S(1)} %add_convert_fusion.1.refs_0_), channel_id=1, source_target_pairs={{0,2},{1,3},{2,0},{3,1},{4,6},{5,7},{6,4},{7,5},{8,10},{9,11},{10,... | collective-permute-start | bytes 393224 | tf_op jit(solution)/shard_map/ppermute | solution.py:41
  84.1 12.7 %collective-permute-start.34 = (bf16[2,128,256]{2,1,0:T(8,128)(2,1)S(1)}, bf16[2,128,256]{2,1,0:T(8,128)(2,1)S(1)}, u32[]{:S(2)}, u32[]{:S(2)}) collective-permute-start(bf16[2,128,256]{2,1,0:T(8,128)(2,1)S(1)} %get-tuple-element.39.refs_0_), channel_id=1, source_target_pairs={{0,28},{4,0},{8,4},{12,8},{16,12},{20,16},{24,20},{28,24},{1,29},{... | collective-permute-start | bytes 393224 | tf_op jit(solution)/shard_map/ppermute | solution.py:28
  87.7 9.1 %collective-permute-start.33 = (bf16[2,128,256]{2,1,0:T(8,128)(2,1)S(1)}, bf16[2,128,256]{2,1,0:T(8,128)(2,1)S(1)}, u32[]{:S(2)}, u32[]{:S(2)}) collective-permute-start(bf16[2,128,256]{2,1,0:T(8,128)(2,1)S(1)} %get-tuple-element.39.refs_0_), channel_id=1, source_target_pairs={{0,4},{4,8},{8,12},{12,16},{16,20},{20,24},{24,28},{28,0},{1,5},{5... | collective-permute-start | bytes 393224 | tf_op jit(solution)/shard_map/ppermute | solution.py:28
  91.3 5.6 %collective-permute-start.38 = (f32[8,128]{1,0:T(8,128)S(1)}, f32[8,128]{1,0:T(8,128)S(1)}, u32[]{:S(2)}, u32[]{:S(2)}) collective-permute-start(f32[8,128]{1,0:T(8,128)S(1)} %shard_map.90), channel_id=1, source_target_pairs={{0,8},{4,12},{8,0},{12,4},{16,24},{20,28},{24,16},{28,20},{1,9},{5... | collective-permute-start | bytes 12296 | tf_op jit(solution)/shard_map/ppermute | solution.py:259
  91.3 5.6 %collective-permute-start.39 = (f32[8,128]{1,0:T(8,128)S(1)}, f32[8,128]{1,0:T(8,128)S(1)}, u32[]{:S(2)}, u32[]{:S(2)}) collective-permute-start(f32[8,128]{1,0:T(8,128)S(1)} %get-tuple-element.40), channel_id=1, source_target_pairs={{0,24},{4,28},{8,16},{12,20},{16,8},{20,12},{24,0},{28,4},{1,25},{... | collective-permute-start | bytes 12296 | tf_op jit(solution)/shard_map/ppermute | solution.py:259
  93.0 4.5 %collective-permute-start.36 = (f32[8,128]{1,0:T(8,128)S(1)}, f32[8,128]{1,0:T(8,128)S(1)}, u32[]{:S(2)}, u32[]{:S(2)}) collective-permute-start(f32[8,128]{1,0:T(8,128)S(1)} %get-tuple-element.40), channel_id=1, source_target_pairs={{0,16},{4,20},{8,24},{12,28},{16,0},{20,4},{24,8},{28,12},{1,17},{... | collective-permute-start | bytes 12296 | tf_op jit(solution)/shard_map/ppermute | solution.py:259
  96.8 4.9 %collective-permute-start.35 = (bf16[4,128,256]{2,1,0:T(8,128)(2,1)S(1)}, bf16[4,128,256]{2,1,0:T(8,128)(2,1)S(1)}, u32[]{:S(2)}, u32[]{:S(2)}) collective-permute-start(bf16[4,128,256]{2,1,0:T(8,128)(2,1)S(1)} %shard_map.89.refs_2_), channel_id=1, source_target_pairs={{0,1},{1,0},{2,3},{3,2},{4,5},{5,4},{6,7},{7,6},{8,9},{9,8},{10,11... | collective-permute-start | bytes 786440 | tf_op jit(solution)/shard_map/ppermute | solution.py:32
  97.5 3.1 %collective-permute-start.42 = (f32[8,128]{1,0:T(8,128)S(1)}, f32[8,128]{1,0:T(8,128)S(1)}, u32[]{:S(2)}, u32[]{:S(2)}) collective-permute-start(f32[8,128]{1,0:T(8,128)S(1)} %add_add_fusion.3), channel_id=1, source_target_pairs={{0,5},{1,4},{2,7},{3,6},{4,1},{5,0},{6,3},{7,2},{8,13},{9,12},{10,... | collective-permute-start | bytes 12296 | tf_op jit(solution)/shard_map/ppermute | solution.py:259
  97.5 4.1 %collective-permute-start.41 = (f32[8,128]{1,0:T(8,128)S(1)}, f32[8,128]{1,0:T(8,128)S(1)}, u32[]{:S(2)}, u32[]{:S(2)}) collective-permute-start(f32[8,128]{1,0:T(8,128)S(1)} %add_add_fusion.3), channel_id=1, source_target_pairs={{0,4},{1,5},{2,6},{3,7},{4,0},{5,1},{6,2},{7,3},{8,12},{9,13},{10,... | collective-permute-start | bytes 12296 | tf_op jit(solution)/shard_map/ppermute | solution.py:259
  100.1 1.6 %collective-permute-start.40 = (f32[8,128]{1,0:T(8,128)S(1)}, f32[8,128]{1,0:T(8,128)S(1)}, u32[]{:S(2)}, u32[]{:S(2)}) collective-permute-start(f32[8,128]{1,0:T(8,128)S(1)} %add_add_fusion.3), channel_id=1, source_target_pairs={{0,1},{1,0},{2,3},{3,2},{4,5},{5,4},{6,7},{7,6},{8,9},{9,8},{10,11... | collective-permute-start | bytes 12296 | tf_op jit(solution)/shard_map/ppermute | solution.py:259
  104.1 2.2 %collective-permute-start.43 = (bf16[2,128,256]{2,1,0:T(8,128)(2,1)S(1)}, bf16[2,128,256]{2,1,0:T(8,128)(2,1)S(1)}, u32[]{:S(2)}, u32[]{:S(2)}) collective-permute-start(bf16[2,128,256]{2,1,0:T(8,128)(2,1)S(1)} %get-tuple-element.44), channel_id=1, source_target_pairs={{0,1},{1,0},{2,3},{3,2},{4,5},{5,4},{6,7},{7,6},{8,9},{9,8},{10,11... | collective-permute-start | bytes 393224 | tf_op jit(solution)/shard_map/ppermute | solution.py:32
  105.1 11.3 %collective-permute-start.46 = (bf16[2,256,256]{2,1,0:T(8,128)(2,1)S(1)}, bf16[2,256,256]{2,1,0:T(8,128)(2,1)S(1)}, u32[]{:S(2)}, u32[]{:S(2)}) collective-permute-start(bf16[2,256,256]{2,1,0:T(8,128)(2,1)S(1)} %get-tuple-element.46), channel_id=1, source_target_pairs={{0,4},{4,8},{8,12},{12,16},{16,20},{20,24},{24,28},{28,0},{1,5},{5... | collective-permute-start | bytes 786440 | tf_op jit(solution)/shard_map/ppermute | solution.py:28
  106.3 5.6 %collective-permute-start.44 = (bf16[2,128,256]{2,1,0:T(8,128)(2,1)S(1)}, bf16[2,128,256]{2,1,0:T(8,128)(2,1)S(1)}, u32[]{:S(2)}, u32[]{:S(2)}) collective-permute-start(bf16[2,128,256]{2,1,0:T(8,128)(2,1)S(1)} %add_convert_fusion.refs_0_), channel_id=1, source_target_pairs={{0,2},{1,3},{2,0},{3,1},{4,6},{5,7},{6,4},{7,5},{8,10},{9,11},{10,... | collective-permute-start | bytes 393224 | tf_op jit(solution)/shard_map/ppermute | solution.py:41
  112.6 7.8 %collective-permute-start.52 = (bf16[2,128,256]{2,1,0:T(8,128)(2,1)S(1)}, bf16[2,128,256]{2,1,0:T(8,128)(2,1)S(1)}, u32[]{:S(2)}, u32[]{:S(2)}) collective-permute-start(bf16[2,128,256]{2,1,0:T(8,128)(2,1)S(1)} %get-tuple-element.47.refs_1_), channel_id=1, source_target_pairs={{0,4},{4,8},{8,12},{12,16},{16,20},{20,24},{24,28},{28,0},{1,5},{5... | collective-permute-start | bytes 393224 | tf_op jit(solution)/shard_map/ppermute | solution.py:28
  113.9 6.6 %collective-permute-start.48 = (f32[8,128]{1,0:T(8,128)S(1)}, f32[8,128]{1,0:T(8,128)S(1)}, u32[]{:S(2)}, u32[]{:S(2)}) collective-permute-start(f32[8,128]{1,0:T(8,128)S(1)} %get-tuple-element.45), channel_id=1, source_target_pairs={{0,24},{4,28},{8,16},{12,20},{16,8},{20,12},{24,0},{28,4},{1,25},{... | collective-permute-start | bytes 12296 | tf_op jit(solution)/shard_map/ppermute | solution.py:259
  116.4 4.5 %collective-permute-start.45 = (f32[8,128]{1,0:T(8,128)S(1)}, f32[8,128]{1,0:T(8,128)S(1)}, u32[]{:S(2)}, u32[]{:S(2)}) collective-permute-start(f32[8,128]{1,0:T(8,128)S(1)} %get-tuple-element.45), channel_id=1, source_target_pairs={{0,16},{4,20},{8,24},{12,28},{16,0},{20,4},{24,8},{28,12},{1,17},{... | collective-permute-start | bytes 12296 | tf_op jit(solution)/shard_map/ppermute | solution.py:259
  116.4 4.5 %collective-permute-start.47 = (f32[8,128]{1,0:T(8,128)S(1)}, f32[8,128]{1,0:T(8,128)S(1)}, u32[]{:S(2)}, u32[]{:S(2)}) collective-permute-start(f32[8,128]{1,0:T(8,128)S(1)} %shard_map.93), channel_id=1, source_target_pairs={{0,8},{4,12},{8,0},{12,4},{16,24},{20,28},{24,16},{28,20},{1,9},{5... | collective-permute-start | bytes 12296 | tf_op jit(solution)/shard_map/ppermute | solution.py:259
  120.4 4.3 %collective-permute-start.53 = (bf16[4,128,256]{2,1,0:T(8,128)(2,1)S(1)}, bf16[4,128,256]{2,1,0:T(8,128)(2,1)S(1)}, u32[]{:S(2)}, u32[]{:S(2)}) collective-permute-start(bf16[4,128,256]{2,1,0:T(8,128)(2,1)S(1)} %shard_map.94.pair), channel_id=1, source_target_pairs={{0,1},{1,0},{2,3},{3,2},{4,5},{5,4},{6,7},{7,6},{8,9},{9,8},{10,11... | collective-permute-start | bytes 786440 | tf_op jit(solution)/shard_map/ppermute | solution.py:32
  120.9 3.1 %collective-permute-start.51 = (f32[8,128]{1,0:T(8,128)S(1)}, f32[8,128]{1,0:T(8,128)S(1)}, u32[]{:S(2)}, u32[]{:S(2)}) collective-permute-start(f32[8,128]{1,0:T(8,128)S(1)} %add_add_fusion.1), channel_id=1, source_target_pairs={{0,5},{1,4},{2,7},{3,6},{4,1},{5,0},{6,3},{7,2},{8,13},{9,12},{10,... | collective-permute-start | bytes 12296 | tf_op jit(solution)/shard_map/ppermute | solution.py:259
  121.0 3.7 %collective-permute-start.50 = (f32[8,128]{1,0:T(8,128)S(1)}, f32[8,128]{1,0:T(8,128)S(1)}, u32[]{:S(2)}, u32[]{:S(2)}) collective-permute-start(f32[8,128]{1,0:T(8,128)S(1)} %add_add_fusion.1), channel_id=1, source_target_pairs={{0,4},{1,5},{2,6},{3,7},{4,0},{5,1},{6,2},{7,3},{8,12},{9,13},{10,... | collective-permute-start | bytes 12296 | tf_op jit(solution)/shard_map/ppermute | solution.py:259
  122.7 2.0 %collective-permute-start.49 = (f32[8,128]{1,0:T(8,128)S(1)}, f32[8,128]{1,0:T(8,128)S(1)}, u32[]{:S(2)}, u32[]{:S(2)}) collective-permute-start(f32[8,128]{1,0:T(8,128)S(1)} %add_add_fusion.1), channel_id=1, source_target_pairs={{0,1},{1,0},{2,3},{3,2},{4,5},{5,4},{6,7},{7,6},{8,9},{9,8},{10,11... | collective-permute-start | bytes 12296 | tf_op jit(solution)/shard_map/ppermute | solution.py:259
  (14 other events, 92.1 us)

commit v4 on v3

--- a/solution.py
+++ b/solution.py
@@ -63,10 +63,11 @@
     )(*ins)
 
 
-def row_halves(core, width):
+def row_halves(width):
     half = width // 2
-    here = pl.ds(pl.multiple_of(core[0] * half, half), half)
-    there = pl.ds(pl.multiple_of((1 - core[0]) * half, half), half)
+    core = lax.rem(lax.axis_index("op"), 2)
+    here = pl.ds(pl.multiple_of(core * half, half), half)
+    there = pl.ds(pl.multiple_of((1 - core) * half, half), half)
     return here, there
 
 
@@ -102,8 +103,9 @@
                 yield group * sectors + b, rows[side], ref[place + b]
 
 
-def products(partner, left, right, window, kept_part, sent_part, halfway, total, rows):
+def products(partner_in, partner, left, right, window, kept_part, sent_part, halfway, total, rows):
     terms, sectors, width, _ = left.shape
+    partner_in.wait()
     for b in range(sectors):
         for t in range(terms):
             product = jnp.dot(left[t, b], window[partner[t, b]], preferred_element_type=F32)
@@ -129,13 +131,16 @@
     return mine, other
 
 
-def first_apply_kernel(emit, core, partner, left, right, *refs):
-    pieces, (kept_part, sent_part, window, *blocks, halfway, total) = refs[:4], refs[4:]
-    rows = row_halves(core, left.shape[-1])
+def first_apply_kernel(emit, partner_any, left, right, *refs):
+    pieces, refs = refs[:4], refs[4:]
+    kept_part, sent_part, window, *blocks, halfway, total, partner, sem = refs
+    partner_in = pltpu.make_async_copy(partner_any, partner, sem)
+    partner_in.start()
+    rows = row_halves(left.shape[-1])
     for place, row, value in fill_window(rows, window_pieces(left.shape[1], *pieces), window):
         window[place, row, :] = value
     emit_blocks(left, emit, blocks)
-    products(partner, left, right, window, kept_part, sent_part, halfway, total, rows)
+    products(partner_in, partner, left, right, window, kept_part, sent_part, halfway, total, rows)
 
 
 def step_factors(count, sums):
@@ -147,19 +152,21 @@
     return factor * a, -step_size * factor
 
 
-def apply_kernel(emit, count, core, partner, left, right, *refs):
+def apply_kernel(emit, count, partner_any, left, right, *refs):
     pieces, refs = refs[:4], refs[4:]
-    sums, state, kept_part, sent_part, window, *blocks, halfway, total = refs
-    rows = row_halves(core, left.shape[-1])
+    sums, state, kept_part, sent_part, window, *blocks, halfway, total, partner, sem = refs
+    partner_in = pltpu.make_async_copy(partner_any, partner, sem)
+    partner_in.start()
+    rows = row_halves(left.shape[-1])
     alpha, beta = step_factors(count, sums[...])
     for place, row, value in fill_window(rows, window_pieces(left.shape[1], *pieces), window):
         new = alpha * state[place, row, :].astype(F32) + beta * value.astype(F32)
         window[place, row, :] = new.astype(BF16)
     emit_blocks(left, emit, blocks)
-    products(partner, left, right, window, kept_part, sent_part, halfway, total, rows)
-
-
-def apply_terms(core, partner, pieces, left, right, count, sums, state, emit, sizes):
+    products(partner_in, partner, left, right, window, kept_part, sent_part, halfway, total, rows)
+
+
+def apply_terms(partner, pieces, left, right, count, sums, state, emit, sizes):
     terms, sectors, width, _ = left.shape
     half = (sectors, width // 2, width)
     outs = [struct(half), struct(half, BF16), struct((3 * sectors, width, width), BF16)]
@@ -167,28 +174,30 @@
     scratch = [
         pltpu.VMEM((sectors, width, terms * width), BF16),
         pltpu.VMEM((sectors, width, width), F32),
+        pltpu.SMEM(partner.shape, partner.dtype),
+        pltpu.SemaphoreType.DMA,
     ]
-    ins = (core, partner, left, right, *pieces)
-    specs = [SMEM, SMEM] + [VMEM] * 6
+    ins = (partner, left, right, *pieces)
+    specs = [ANY] + [VMEM] * 6
     if sums is None:
         kernel = functools.partial(first_apply_kernel, emit)
         return call(kernel, outs, ins, specs, APPLY_LIMIT, scratch)
     kernel = functools.partial(apply_kernel, emit, count)
     specs += [VMEM, VMEM]
-    return call(kernel, outs, ins + (sums, state), specs, APPLY_LIMIT, scratch, {9: 2})
-
-
-def combine_kernel(count, core, shift, state, *refs):
+    return call(kernel, outs, ins + (sums, state), specs, APPLY_LIMIT, scratch, {8: 2})
+
+
+def combine_kernel(count, shift, state, *refs):
     parts, (rounded, sums) = refs[:count], refs[-2:]
     sectors, half, width = rounded.shape
-    here, _ = row_halves(core, width)
+    here, _ = row_halves(width)
     totals = [jnp.zeros((8, width), F32) for _ in range(3)]
     for b in range(sectors):
         total = parts[0][b].astype(F32)
         for part in parts[1:]:
             total = total + part[b].astype(F32)
         s = state[sectors + b, here, :].astype(F32)
-        total = total + shift[b] * s
+        total = total + shift[b : b + 1, 0:1] * s
         rounded[b] = total.astype(BF16)
         for i, product in enumerate((s * total, s * s, total * total)):
             totals[i] = totals[i] + jnp.sum(product.reshape(-1, 8, width), axis=0)
@@ -216,36 +225,48 @@
     return call(hold_kernel, [struct(x.shape, x.dtype)], (x, *after), specs, alias={0: 0})[0]
 
 
-def finish_kernel(count, sizes, core, kept, sums, state, pair, pair_other, *refs):
+def finish_kernel(count, sizes, kept, sums, state, pair, pair_other, *refs):
     pieces, refs = refs[: len(sizes)], refs[len(sizes) :]
-    final, new_ops, window, results, sems = refs
+    final, new_ops, window, projected, results, sems, final_sem = refs
     sectors, width, _ = final.shape
     alpha, beta = step_factors(count, sums[...])
-    rows = row_halves(core, width)
-    parts = [[(ref, 0), (ref, sectors)] for ref in (pair, pair_other)]
-    for place, row, value in fill_window(rows, parts, window):
-        new = alpha * state[place, row, :].astype(F32) + beta * value.astype(F32)
-        window[place, row, :] = new.astype(BF16)
-    final[...] = window[sectors:]
+    rows = row_halves(width)
+    units = [(piece, i) for piece, size in zip(pieces, sizes) for i in range(size)]
     columns = lax.broadcasted_iota(jnp.int32, (width, width), 1)
-    blocks = []
+    scale = 1.0 / float(width) ** 0.5
+    flipped = []
+
+    def fill(group):
+        for ref, row in zip((pair, pair_other), rows):
+            for b in range(sectors):
+                place = group * sectors + b
+                value = beta * ref[place].astype(F32)
+                new = alpha * state[place, row, :].astype(F32) + value
+                window[place, row, :] = new.astype(BF16)
+
+    fill(0)
+    fill(1)
+    final_out = pltpu.make_async_copy(window.at[pl.ds(sectors, sectors)], final, final_sem)
+    final_out.start()
     for b in range(sectors):
-        block = jnp.where(columns < kept[b], window[b].astype(F32), 0.0).astype(BF16)
-        blocks.append((block, block.T))
+        block = jnp.where(columns < kept[b : b + 1, 0:1], window[b].astype(F32), 0.0)
+        flipped.append((block * scale).astype(BF16).T)
+        block = block.astype(BF16)
+        for t, (piece, i) in enumerate(units[b::sectors]):
+            product = jnp.dot(piece[i], block, preferred_element_type=F32)
+            projected[b, :, t * width : (t + 1) * width] = product.astype(BF16)
     copies = []
-    unit = 0
-    for piece, size in zip(pieces, sizes):
-        for i in range(size):
-            t, b = unit // sectors, unit % sectors
-            block, flipped = blocks[b]
-            projected = jnp.dot(piece[i], block, preferred_element_type=F32).astype(BF16)
-            result = jnp.dot(flipped, projected, preferred_element_type=F32)
-            results[t, b] = (result * (1.0 / float(width) ** 0.5)).astype(BF16)
-            if b == sectors - 1:
-                copy = pltpu.make_async_copy(results.at[t], new_ops.at[t], sems.at[t])
-                copy.start()
-                copies.append(copy)
-            unit += 1
+    for b in range(sectors):
+        for t in range(len(units) // sectors):
+            part = projected[b, :, t * width : (t + 1) * width]
+            result = jnp.dot(flipped[b], part, preferred_element_type=F32)
+            results[t, b] = result.astype(BF16)
+            copy = pltpu.make_async_copy(
+                results.at[t, b], new_ops.at[t, b], sems.at[t * sectors + b]
+            )
+            copy.start()
+            copies.append(copy)
+    final_out.wait()
     for copy in copies:
         copy.wait()
 
@@ -286,7 +307,8 @@
     devices = lax.axis_size("sec")
     count = float(sectors * devices * width * width)
     core_index = lax.axis_index("op") % 2
-    core = core_index.reshape(1).astype(jnp.int32)
+    shifts = jnp.broadcast_to(shift[:, None], (sectors, 128))
+    kepts = jnp.broadcast_to(kept[:, None], (sectors, 128))
     half_shape = (sectors, half, width)
     units = terms * sectors
     plan = list(PLAN[:-1]) + [units - sum(PLAN[:-1])]
@@ -306,11 +328,10 @@
     first = first_blocks(left_ops, plan[0])
     pair = pack(before, hold(after, first))
     pieces = [sec_move(first, 1)]
-    moved_kept = sec_move(kept, 1)
+    moved_kept = sec_move(kepts, 1)
     sums = state = None
     for iteration in range(ITERS):
         kept_part, sent_part, state, *blocks = apply_terms(
-            core,
             partner,
             (own, own_other, pair, core_swap(pair)),
             left_ops,
@@ -330,8 +351,8 @@
         own, sums = call(
             functools.partial(combine_kernel, len(parts)),
             [struct(half_shape, BF16), struct((8, 128))],
-            (core, shift, state, *parts, *gates),
-            [SMEM, SMEM] + [VMEM] * (1 + len(parts)) + [ANY] * len(gates),
+            (shifts, state, *parts, *gates),
+            [VMEM] * (2 + len(parts)) + [ANY] * len(gates),
         )
         sums = far_sums(sums, late)
         if iteration < ITERS - 1:
@@ -346,18 +367,20 @@
     final, new_ops = pl.pallas_call(
         functools.partial(finish_kernel, count, tuple(plan)),
         out_shape=(struct(state_start.shape, BF16), struct(left_ops.shape, BF16)),
-        in_specs=[SMEM] * 2 + [VMEM] * (4 + len(pieces)),
-        out_specs=(VMEM, ANY),
+        in_specs=[VMEM] * (5 + len(pieces)),
+        out_specs=(ANY, ANY),
         scratch_shapes=[
             pltpu.VMEM((2 * sectors, width, width), BF16),
+            pltpu.VMEM((sectors, width, terms * width), BF16),
             pltpu.VMEM(left_ops.shape, BF16),
-            pltpu.SemaphoreType.DMA((terms,)),
+            pltpu.SemaphoreType.DMA((units,)),
+            pltpu.SemaphoreType.DMA,
         ],
         compiler_params=pltpu.CompilerParams(vmem_limit_bytes=8 * MIB),
         cost_estimate=pl.CostEstimate(
             flops=4 * terms * sectors * width**3, bytes_accessed=4 * MIB, transcendentals=0
         ),
-    )(core, moved_kept, sums, state, pair, pair_other, *pieces)
+    )(moved_kept, sums, state, pair, pair_other, *pieces)
     return final, new_ops
 
 

time: 129 us -> 126 us (0.977)
  Pallas kernels: 17.4 us -> 13.7 us
    pallas_call x18, Pallas kernels: 13.6 us -> 11 us  [call(): pl.pallas_call(kernel, out_shape=tuple(outs), in_specs=specs, out_specs=t...]
  transfers between devices with their start and end apart: 54 -> 54, of which waited for: 26 -> 25; matrix products, arithmetic and copies ran while one was open for 0% -> 0% of each run, Pallas kernels for 8% -> 7%
where the time goes in v4:
time: 126 us
  starting transfers between devices  53.6 us (43%)
  waiting for transfers between devices  53.4 us (42%)
  Pallas kernels  13.7 us (11%)
  local copies, waits for them, and re-layouts  3.75 us (3%)
    ppermute x14, waiting for transfers between devices, sec_move(): lax.ppermute(x, 'sec', [(i, (i + distance) % count) for i in range(count)])  29.6 us
    ppermute x24, starting transfers between devices, other(): return lax.ppermute(sent, axes, [(i, i ^ mask) for i in range(size)])  24.7 us
    ppermute x14, starting transfers between devices, sec_move(): lax.ppermute(x, 'sec', [(i, (i + distance) % count) for i in range(count)])  19.2 us
    ppermute x4, waiting for transfers between devices, chip_parts(): parts.append(lax.ppermute(x, 'op', route))  12.3 us
    pallas_call x18, Pallas kernels, call(): pl.pallas_call(kernel, out_shape=tuple(outs), in_specs=specs, out_specs=t...  11 us
    ppermute x12, waiting for transfers between devices, core_swap(): lax.ppermute(x, 'op', [(i, i ^ 1) for i in range(lax.axis_size('op'))])  6.96 us
    ppermute x4, starting transfers between devices, chip_parts(): parts.append(lax.ppermute(x, 'op', route))  6.35 us
    ppermute x24, waiting for transfers between devices, other(): return lax.ppermute(sent, axes, [(i, i ^ mask) for i in range(size)])  4.45 us
  transfers between devices with their start and end apart: 54, of which 25 were waited for; matrix products, arithmetic and copies ran while one was open for 0% of the time, Pallas kernels for 7%

profile of v4, /device:TPU:0, one launch (start us, length us, event | category | flops | bytes accessed | tf_op | source)
XLA Modules:
  0.0 125.6 jit_solution(3361993623127571315)
XLA Ops:
  0.6 1.0 constant_dynamic-slice_fusion
  1.7 6.0 %collective-permute-start.2 = (bf16[2,128,256]{2,1,0:T(8,128)(2,1)S(1)}, bf16[2,128,256]{2,1,0:T(8,128)(2,1)S(1)}, u32[]{:S(2)}, u32[]{:S(2)}) collective-permute-start(bf16[2,128,256]{2,1,0:T(8,128)(2,1)S(1)} %get-tuple-element.49.refs_0_), channel_id=1, source_target_pairs={{0,28},{4,0},{8,4},{12,8},{16,12},{20,16},{24,20},{28,24},{1,29},{... | collective-permute-start | bytes 393224 | tf_op jit(solution)/shard_map/ppermute | solution.py:28
  7.7 1.1 shard_map.77.refs_1_
  8.9 1.6 %collective-permute-done.2.refs_0_ = bf16[2,128,256]{2,1,0:T(8,128)(2,1)S(1)} collective-permute-done((bf16[2,128,256]{2,1,0:T(8,128)(2,1)S(1)}, bf16[2,128,256]{2,1,0:T(8,128)(2,1)S(1)}, u32[]{:S(2)}, u32[]{:S(2)}) %collective-permute-start.2) | collective-permute-done | bytes 131104 | tf_op jit(solution)/shard_map/ppermute | solution.py:28
  10.5 4.9 %collective-permute-done.1.refs_0_ = bf16[2,128,256]{2,1,0:T(8,128)(2,1)S(1)} collective-permute-done((bf16[2,128,256]{2,1,0:T(8,128)(2,1)S(1)}, bf16[2,128,256]{2,1,0:T(8,128)(2,1)S(1)}, u32[]{:S(2)}, u32[]{:S(2)}) %collective-permute-start.1) | collective-permute-done | bytes 131104 | tf_op jit(solution)/shard_map/ppermute | solution.py:28
  15.6 1.5 %collective-permute-done.3.refs_3_ = bf16[4,128,256]{2,1,0:T(8,128)(2,1)} collective-permute-done((bf16[4,128,256]{2,1,0:T(8,128)(2,1)S(1)}, bf16[4,128,256]{2,1,0:T(8,128)(2,1)}, u32[]{:S(2)}, u32[]{:S(2)}) %collective-permute-start.3) | collective-permute-done | bytes 262176 | tf_op jit(solution)/shard_map/ppermute | solution.py:32
  17.1 1.6 %copy-done.1 = bf16[8,2,256,256]{3,2,1,0:T(8,128)(2,1)S(1)} copy-done((bf16[8,2,256,256]{3,2,1,0:T(8,128)(2,1)S(1)}, bf16[8,2,256,256]{3,2,1,0:T(8,128)(2,1)}, u32[]{:S(2)}) %copy-start.1) | copy-done | bytes 2097176
  19.6 3.1 %shard_map.80 = (f32[2,128,256]{2,1,0:T(8,128)S(1)}, bf16[2,128,256]{2,1,0:T(8,128)(2,1)S(1)}, bf16[6,256,256]{2,1,0:T(8,128)(2,1)S(1)}, bf16[5,256,256]{2,1,0:T(8,128)(2,1)S(1)}) custom-call(s32[8,2]{1,0:T(8,128)S(1)} %copy.18.partner_any, bf16[8,2,256,256]{3,2,1,0:T(8,128)(2,1)S(1)} %copy-done, bf16[8,2,256,256]{3,2,1,0:T(8,128)(2,1)S(1)} %copy-done.1, ...), custom_call_target="tpu_custom_call" | custom-call | tf_op jit(solution)/shard_map/pallas_call | solution.py:54
  22.9 1.2 collective-permute-done.4
  24.2 1.6 %collective-permute-start.5 = (bf16[2,128,256]{2,1,0:T(8,128)(2,1)S(1)}, bf16[2,128,256]{2,1,0:T(8,128)(2,1)S(1)}, u32[]{:S(2)}, u32[]{:S(2)}) collective-permute-start(bf16[2,128,256]{2,1,0:T(8,128)(2,1)S(1)} %add_convert_fusion.3.refs_0_), channel_id=1, source_target_pairs={{0,2},{1,3},{2,0},{3,1},{4,6},{5,7},{6,4},{7,5},{8,10},{9,11},{10,... | collective-permute-start | bytes 393224 | tf_op jit(solution)/shard_map/ppermute | solution.py:41
  25.8 6.7 %collective-permute-done.refs_2_.kept = s32[2,128]{1,0:T(2,128)S(1)} collective-permute-done((s32[2,128]{1,0:T(2,128)S(1)}, s32[2,128]{1,0:T(2,128)S(1)}, u32[]{:S(2)}, u32[]{:S(2)}) %collective-permute-start) | collective-permute-done | bytes 1056 | tf_op jit(solution)/shard_map/ppermute | solution.py:28
  33.3 1.6 %collective-permute-start.8 = (bf16[2,128,256]{2,1,0:T(8,128)(2,1)S(1)}, bf16[2,128,256]{2,1,0:T(8,128)(2,1)S(1)}, u32[]{:S(2)}, u32[]{:S(2)}) collective-permute-start(bf16[2,128,256]{2,1,0:T(8,128)(2,1)S(1)} %get-tuple-element.28.refs_0_), channel_id=1, source_target_pairs={{0,4},{4,8},{8,12},{12,16},{16,20},{20,24},{24,28},{28,0},{1,5},{5... | collective-permute-start | bytes 393224 | tf_op jit(solution)/shard_map/ppermute | solution.py:28
  34.9 4.4 %collective-permute-start.11 = (f32[8,128]{1,0:T(8,128)S(1)}, f32[8,128]{1,0:T(8,128)S(1)}, u32[]{:S(2)}, u32[]{:S(2)}) collective-permute-start(f32[8,128]{1,0:T(8,128)S(1)} %get-tuple-element.29), channel_id=1, source_target_pairs={{0,16},{4,20},{8,24},{12,28},{16,0},{20,4},{24,8},{28,12},{1,17},{... | collective-permute-start | bytes 12296 | tf_op jit(solution)/shard_map/ppermute | solution.py:280
  39.3 1.7 %collective-permute-done.8.refs_0_ = bf16[2,128,256]{2,1,0:T(8,128)(2,1)S(1)} collective-permute-done((bf16[2,128,256]{2,1,0:T(8,128)(2,1)S(1)}, bf16[2,128,256]{2,1,0:T(8,128)(2,1)S(1)}, u32[]{:S(2)}, u32[]{:S(2)}) %collective-permute-start.8) | collective-permute-done | bytes 131104 | tf_op jit(solution)/shard_map/ppermute | solution.py:28
  41.2 2.1 %collective-permute-start.15 = (f32[8,128]{1,0:T(8,128)S(1)}, f32[8,128]{1,0:T(8,128)S(1)}, u32[]{:S(2)}, u32[]{:S(2)}) collective-permute-start(f32[8,128]{1,0:T(8,128)S(1)} %add_add_fusion.7), channel_id=1, source_target_pairs={{0,4},{1,5},{2,6},{3,7},{4,0},{5,1},{6,2},{7,3},{8,12},{9,13},{10,... | collective-permute-start | bytes 12296 | tf_op jit(solution)/shard_map/ppermute | solution.py:280
  43.3 1.6 %collective-permute-start.24 = (bf16[5,256,256]{2,1,0:T(8,128)(2,1)S(1)}, bf16[5,256,256]{2,1,0:T(8,128)(2,1)S(1)}, u32[]{:S(2)}, u32[]{:S(2)}) collective-permute-start(bf16[5,256,256]{2,1,0:T(8,128)(2,1)S(1)} %get-tuple-element.35), channel_id=1, source_target_pairs={{0,4},{4,8},{8,12},{12,16},{16,20},{20,24},{24,28},{28,0},{1,5},{5... | collective-permute-start | bytes 1966088 | tf_op jit(solution)/shard_map/ppermute | solution.py:28
  45.0 1.3 %collective-permute-done.7.refs_1_ = bf16[2,128,256]{2,1,0:T(8,128)(2,1)S(1)} collective-permute-done((bf16[2,128,256]{2,1,0:T(8,128)(2,1)S(1)}, bf16[2,128,256]{2,1,0:T(8,128)(2,1)S(1)}, u32[]{:S(2)}, u32[]{:S(2)}) %collective-permute-start.7) | collective-permute-done | bytes 131104 | tf_op jit(solution)/shard_map/ppermute | solution.py:32
  46.3 2.1 %shard_map.83 = (f32[2,128,256]{2,1,0:T(8,128)S(1)}, bf16[2,128,256]{2,1,0:T(8,128)(2,1)S(1)}, bf16[6,256,256]{2,1,0:T(8,128)(2,1)S(1)}, bf16[5,256,256]{2,1,0:T(8,128)(2,1)S(1)}) custom-call(s32[8,2]{1,0:T(8,128)S(1)} %copy.18.partner_any, bf16[8,2,256,256]{3,2,1,0:T(8,128)(2,1)S(1)} %copy-done, ...), custom_call_target="tpu_custom_call", output_to_operand_aliasing={{2}: (8, {})} | custom-call | tf_op jit(solution)/shard_map/pallas_call | solution.py:54
  48.6 1.2 collective-permute-done.17
  49.8 1.6 %collective-permute-start.18 = (bf16[2,128,256]{2,1,0:T(8,128)(2,1)S(1)}, bf16[2,128,256]{2,1,0:T(8,128)(2,1)S(1)}, u32[]{:S(2)}, u32[]{:S(2)}) collective-permute-start(bf16[2,128,256]{2,1,0:T(8,128)(2,1)S(1)} %add_convert_fusion.2.refs_0_), channel_id=1, source_target_pairs={{0,2},{1,3},{2,0},{3,1},{4,6},{5,7},{6,4},{7,5},{8,10},{9,11},{10,... | collective-permute-start | bytes 393224 | tf_op jit(solution)/shard_map/ppermute | solution.py:41
  51.4 4.0 %collective-permute-done.18.refs_1_ = bf16[2,128,256]{2,1,0:T(8,128)(2,1)S(1)} collective-permute-done((bf16[2,128,256]{2,1,0:T(8,128)(2,1)S(1)}, bf16[2,128,256]{2,1,0:T(8,128)(2,1)S(1)}, u32[]{:S(2)}, u32[]{:S(2)}) %collective-permute-start.18) | collective-permute-done | bytes 131104 | tf_op jit(solution)/shard_map/ppermute | solution.py:41
  55.6 3.3 %collective-permute-start.21 = (bf16[2,128,256]{2,1,0:T(8,128)(2,1)S(1)}, bf16[2,128,256]{2,1,0:T(8,128)(2,1)S(1)}, u32[]{:S(2)}, u32[]{:S(2)}) collective-permute-start(bf16[2,128,256]{2,1,0:T(8,128)(2,1)S(1)} %get-tuple-element.33.refs_0_), channel_id=1, source_target_pairs={{0,28},{4,0},{8,4},{12,8},{16,12},{20,16},{24,20},{28,24},{1,29},{... | collective-permute-start | bytes 393224 | tf_op jit(solution)/shard_map/ppermute | solution.py:28
  59.5 1.7 %collective-permute-start.23 = (f32[8,128]{1,0:T(8,128)S(1)}, f32[8,128]{1,0:T(8,128)S(1)}, u32[]{:S(2)}, u32[]{:S(2)}) collective-permute-start(f32[8,128]{1,0:T(8,128)S(1)} %get-tuple-element.34), channel_id=1, source_target_pairs={{0,16},{4,20},{8,24},{12,28},{16,0},{20,4},{24,8},{28,12},{1,17},{... | collective-permute-start | bytes 12296 | tf_op jit(solution)/shard_map/ppermute | solution.py:280
  61.2 2.1 %collective-permute-done.24.refs_1_ = bf16[5,256,256]{2,1,0:T(8,128)(2,1)S(1)} collective-permute-done((bf16[5,256,256]{2,1,0:T(8,128)(2,1)S(1)}, bf16[5,256,256]{2,1,0:T(8,128)(2,1)S(1)}, u32[]{:S(2)}, u32[]{:S(2)}) %collective-permute-start.24) | collective-permute-done | bytes 655392 | tf_op jit(solution)/shard_map/ppermute | solution.py:28
  63.3 1.6 %collective-permute-start.25 = (f32[8,128]{1,0:T(8,128)S(1)}, f32[8,128]{1,0:T(8,128)S(1)}, u32[]{:S(2)}, u32[]{:S(2)}) collective-permute-start(f32[8,128]{1,0:T(8,128)S(1)} %shard_map.86), channel_id=1, source_target_pairs={{0,8},{4,12},{8,0},{12,4},{16,24},{20,28},{24,16},{28,20},{1,9},{5... | collective-permute-start | bytes 12296 | tf_op jit(solution)/shard_map/ppermute | solution.py:280
  64.9 3.9 %collective-permute-done.21.refs_1_ = bf16[2,128,256]{2,1,0:T(8,128)(2,1)S(1)} collective-permute-done((bf16[2,128,256]{2,1,0:T(8,128)(2,1)S(1)}, bf16[2,128,256]{2,1,0:T(8,128)(2,1)S(1)}, u32[]{:S(2)}, u32[]{:S(2)}) %collective-permute-start.21) | collective-permute-done | bytes 131104 | tf_op jit(solution)/shard_map/ppermute | solution.py:28
  69.0 2.1 %collective-permute-start.28 = (f32[8,128]{1,0:T(8,128)S(1)}, f32[8,128]{1,0:T(8,128)S(1)}, u32[]{:S(2)}, u32[]{:S(2)}) collective-permute-start(f32[8,128]{1,0:T(8,128)S(1)} %add_add_fusion.5), channel_id=1, source_target_pairs={{0,4},{1,5},{2,6},{3,7},{4,0},{5,1},{6,2},{7,3},{8,12},{9,13},{10,... | collective-permute-start | bytes 12296 | tf_op jit(solution)/shard_map/ppermute | solution.py:280
  73.5 2.1 %shard_map.87 = (f32[2,128,256]{2,1,0:T(8,128)S(1)}, bf16[2,128,256]{2,1,0:T(8,128)(2,1)S(1)}, bf16[6,256,256]{2,1,0:T(8,128)(2,1)S(1)}, bf16[2,256,256]{2,1,0:T(8,128)(2,1)S(1)}) custom-call(s32[8,2]{1,0:T(8,128)S(1)} %copy.18.partner_any, bf16[8,2,256,256]{3,2,1,0:T(8,128)(2,1)S(1)} %copy-done, ...), custom_call_target="tpu_custom_call", output_to_operand_aliasing={{2}: (8, {})} | custom-call | tf_op jit(solution)/shard_map/pallas_call | solution.py:54
  76.1 1.0 collective-permute-done.30
  77.1 1.6 %collective-permute-start.31 = (bf16[2,128,256]{2,1,0:T(8,128)(2,1)S(1)}, bf16[2,128,256]{2,1,0:T(8,128)(2,1)S(1)}, u32[]{:S(2)}, u32[]{:S(2)}) collective-permute-start(bf16[2,128,256]{2,1,0:T(8,128)(2,1)S(1)} %add_convert_fusion.1.refs_0_), channel_id=1, source_target_pairs={{0,2},{1,3},{2,0},{3,1},{4,6},{5,7},{6,4},{7,5},{8,10},{9,11},{10,... | collective-permute-start | bytes 393224 | tf_op jit(solution)/shard_map/ppermute | solution.py:41
  78.7 4.2 %collective-permute-done.31.refs_1_ = bf16[2,128,256]{2,1,0:T(8,128)(2,1)S(1)} collective-permute-done((bf16[2,128,256]{2,1,0:T(8,128)(2,1)S(1)}, bf16[2,128,256]{2,1,0:T(8,128)(2,1)S(1)}, u32[]{:S(2)}, u32[]{:S(2)}) %collective-permute-start.31) | collective-permute-done | bytes 131104 | tf_op jit(solution)/shard_map/ppermute | solution.py:41
  83.1 3.6 %collective-permute-start.34 = (bf16[2,128,256]{2,1,0:T(8,128)(2,1)S(1)}, bf16[2,128,256]{2,1,0:T(8,128)(2,1)S(1)}, u32[]{:S(2)}, u32[]{:S(2)}) collective-permute-start(bf16[2,128,256]{2,1,0:T(8,128)(2,1)S(1)} %get-tuple-element.39.refs_0_), channel_id=1, source_target_pairs={{0,28},{4,0},{8,4},{12,8},{16,12},{20,16},{24,20},{28,24},{1,29},{... | collective-permute-start | bytes 393224 | tf_op jit(solution)/shard_map/ppermute | solution.py:28
  86.7 4.4 %collective-permute-done.37.refs_1_.refs_2_ = bf16[5,256,256]{2,1,0:T(8,128)(2,1)S(1)} collective-permute-done((bf16[5,256,256]{2,1,0:T(8,128)(2,1)S(1)}, bf16[5,256,256]{2,1,0:T(8,128)(2,1)S(1)}, u32[]{:S(2)}, u32[]{:S(2)}) %collective-permute-start.37) | collective-permute-done | bytes 655392 | tf_op jit(solution)/shard_map/ppermute | solution.py:28
  91.9 2.7 %collective-permute-start.36 = (f32[8,128]{1,0:T(8,128)S(1)}, f32[8,128]{1,0:T(8,128)S(1)}, u32[]{:S(2)}, u32[]{:S(2)}) collective-permute-start(f32[8,128]{1,0:T(8,128)S(1)} %get-tuple-element.40), channel_id=1, source_target_pairs={{0,16},{4,20},{8,24},{12,28},{16,0},{20,4},{24,8},{28,12},{1,17},{... | collective-permute-start | bytes 12296 | tf_op jit(solution)/shard_map/ppermute | solution.py:280
  94.6 2.0 %collective-permute-done.34.refs_1_ = bf16[2,128,256]{2,1,0:T(8,128)(2,1)S(1)} collective-permute-done((bf16[2,128,256]{2,1,0:T(8,128)(2,1)S(1)}, bf16[2,128,256]{2,1,0:T(8,128)(2,1)S(1)}, u32[]{:S(2)}, u32[]{:S(2)}) %collective-permute-start.34) | collective-permute-done | bytes 131104 | tf_op jit(solution)/shard_map/ppermute | solution.py:28
  96.8 2.2 %collective-permute-start.41 = (f32[8,128]{1,0:T(8,128)S(1)}, f32[8,128]{1,0:T(8,128)S(1)}, u32[]{:S(2)}, u32[]{:S(2)}) collective-permute-start(f32[8,128]{1,0:T(8,128)S(1)} %add_add_fusion.3), channel_id=1, source_target_pairs={{0,4},{1,5},{2,6},{3,7},{4,0},{5,1},{6,2},{7,3},{8,12},{9,13},{10,... | collective-permute-start | bytes 12296 | tf_op jit(solution)/shard_map/ppermute | solution.py:280
  100.6 2.1 %shard_map.91 = (f32[2,128,256]{2,1,0:T(8,128)S(1)}, bf16[2,128,256]{2,1,0:T(8,128)(2,1)S(1)}, bf16[6,256,256]{2,1,0:T(8,128)(2,1)S(1)}) custom-call(s32[8,2]{1,0:T(8,128)S(1)} %copy.18.partner_any, bf16[8,2,256,256]{3,2,1,0:T(8,128)(2,1)S(1)} %copy-done, bf16[8,2,256,256]{3,2,1,0:T(8,128)(2,1)S(1)} %copy-done.2, ...), custom_call_target="tpu_custom_call", output_to_operand_aliasing={{2}: (8, {})} | custom-call | tf_op jit(solution)/shard_map/pallas_call | solution.py:54
  102.7 1.0 collective-permute-start.43
  103.7 1.2 collective-permute-start.46
  104.9 1.6 %collective-permute-start.44 = (bf16[2,128,256]{2,1,0:T(8,128)(2,1)S(1)}, bf16[2,128,256]{2,1,0:T(8,128)(2,1)S(1)}, u32[]{:S(2)}, u32[]{:S(2)}) collective-permute-start(bf16[2,128,256]{2,1,0:T(8,128)(2,1)S(1)} %add_convert_fusion.refs_0_), channel_id=1, source_target_pairs={{0,2},{1,3},{2,0},{3,1},{4,6},{5,7},{6,4},{7,5},{8,10},{9,11},{10,... | collective-permute-start | bytes 393224 | tf_op jit(solution)/shard_map/ppermute | solution.py:41
  106.5 4.1 %collective-permute-done.44.refs_1_ = bf16[2,128,256]{2,1,0:T(8,128)(2,1)S(1)} collective-permute-done((bf16[2,128,256]{2,1,0:T(8,128)(2,1)S(1)}, bf16[2,128,256]{2,1,0:T(8,128)(2,1)S(1)}, u32[]{:S(2)}, u32[]{:S(2)}) %collective-permute-start.44) | collective-permute-done | bytes 131104 | tf_op jit(solution)/shard_map/ppermute | solution.py:41
  110.7 1.3 %collective-permute-start.52 = (bf16[2,128,256]{2,1,0:T(8,128)(2,1)S(1)}, bf16[2,128,256]{2,1,0:T(8,128)(2,1)S(1)}, u32[]{:S(2)}, u32[]{:S(2)}) collective-permute-start(bf16[2,128,256]{2,1,0:T(8,128)(2,1)S(1)} %get-tuple-element.47.refs_1_), channel_id=1, source_target_pairs={{0,4},{4,8},{8,12},{12,16},{16,20},{20,24},{24,28},{28,0},{1,5},{5... | collective-permute-start | bytes 393224 | tf_op jit(solution)/shard_map/ppermute | solution.py:28
  112.0 2.7 %collective-permute-start.48 = (f32[8,128]{1,0:T(8,128)S(1)}, f32[8,128]{1,0:T(8,128)S(1)}, u32[]{:S(2)}, u32[]{:S(2)}) collective-permute-start(f32[8,128]{1,0:T(8,128)S(1)} %get-tuple-element.45), channel_id=1, source_target_pairs={{0,24},{4,28},{8,16},{12,20},{16,8},{20,12},{24,0},{28,4},{1,25},{... | collective-permute-start | bytes 12296 | tf_op jit(solution)/shard_map/ppermute | solution.py:280
  114.7 1.7 %collective-permute-start.47 = (f32[8,128]{1,0:T(8,128)S(1)}, f32[8,128]{1,0:T(8,128)S(1)}, u32[]{:S(2)}, u32[]{:S(2)}) collective-permute-start(f32[8,128]{1,0:T(8,128)S(1)} %shard_map.93), channel_id=1, source_target_pairs={{0,8},{4,12},{8,0},{12,4},{16,24},{20,28},{24,16},{28,20},{1,9},{5... | collective-permute-start | bytes 12296 | tf_op jit(solution)/shard_map/ppermute | solution.py:280
  116.4 2.1 %collective-permute-done.52.refs_0_ = bf16[2,128,256]{2,1,0:T(8,128)(2,1)S(1)} collective-permute-done((bf16[2,128,256]{2,1,0:T(8,128)(2,1)S(1)}, bf16[2,128,256]{2,1,0:T(8,128)(2,1)S(1)}, u32[]{:S(2)}, u32[]{:S(2)}) %collective-permute-start.52) | collective-permute-done | bytes 131104 | tf_op jit(solution)/shard_map/ppermute | solution.py:28
  119.3 1.6 %collective-permute-start.50 = (f32[8,128]{1,0:T(8,128)S(1)}, f32[8,128]{1,0:T(8,128)S(1)}, u32[]{:S(2)}, u32[]{:S(2)}) collective-permute-start(f32[8,128]{1,0:T(8,128)S(1)} %add_add_fusion.1), channel_id=1, source_target_pairs={{0,4},{1,5},{2,6},{3,7},{4,0},{5,1},{6,2},{7,3},{8,12},{9,13},{10,... | collective-permute-start | bytes 12296 | tf_op jit(solution)/shard_map/ppermute | solution.py:280
  121.1 1.2 collective-permute-done.51
  122.9 2.7 %shard_map.95 = (bf16[2,256,256]{2,1,0:T(8,128)(2,1)}, bf16[8,2,256,256]{3,2,1,0:T(8,128)(2,1)}) custom-call(s32[2,128]{1,0:T(2,128)S(1)} %collective-permute-done.refs_2_.kept, f32[8,128]{1,0:T(8,128)S(1)} %add_add_fusion.sums, bf16[6,256,256]{2,1,0:T(8,128)(2,1)S(1)} %get-tuple-element.42.state, bf16[4,128,256]{2,1,0:T(8,128)(2,1)S(1)} %shard_map.94.pair, ...), custom_call_target="tpu_custom_call" | custom-call | flops 1073741824 | bytes 4194304 | tf_op jit(solution)/shard_map/pallas_call | solution.py:367
  (114 shorter events, 11.1 us)
Async XLA Ops:
  1.7 8.8 %collective-permute-start.2 = (bf16[2,128,256]{2,1,0:T(8,128)(2,1)S(1)}, bf16[2,128,256]{2,1,0:T(8,128)(2,1)S(1)}, u32[]{:S(2)}, u32[]{:S(2)}) collective-permute-start(bf16[2,128,256]{2,1,0:T(8,128)(2,1)S(1)} %get-tuple-element.49.refs_0_), channel_id=1, source_target_pairs={{0,28},{4,0},{8,4},{12,8},{16,12},{20,16},{24,20},{28,24},{1,29},{... | collective-permute-start | bytes 393224 | tf_op jit(solution)/shard_map/ppermute | solution.py:28
  7.7 7.7 %collective-permute-start.1 = (bf16[2,128,256]{2,1,0:T(8,128)(2,1)S(1)}, bf16[2,128,256]{2,1,0:T(8,128)(2,1)S(1)}, u32[]{:S(2)}, u32[]{:S(2)}) collective-permute-start(bf16[2,128,256]{2,1,0:T(8,128)(2,1)S(1)} %get-tuple-element.49.refs_0_), channel_id=1, source_target_pairs={{0,4},{4,8},{8,12},{12,16},{16,20},{20,24},{24,28},{28,0},{1,5},{5... | collective-permute-start | bytes 393224 | tf_op jit(solution)/shard_map/ppermute | solution.py:28
  15.4 1.7 %collective-permute-start.3 = (bf16[4,128,256]{2,1,0:T(8,128)(2,1)S(1)}, bf16[4,128,256]{2,1,0:T(8,128)(2,1)}, u32[]{:S(2)}, u32[]{:S(2)}) collective-permute-start(bf16[4,128,256]{2,1,0:T(8,128)(2,1)S(1)} %shard_map.79.refs_2_), channel_id=1, source_target_pairs={{0,1},{1,0},{2,3},{3,2},{4,5},{5,4},{6,7},{7,6},{8,9},{9,8},{10,11... | collective-permute-start | bytes 786440 | tf_op jit(solution)/shard_map/ppermute | solution.py:32
  15.5 17.1 %collective-permute-start.6 = (bf16[4,256,256]{2,1,0:T(8,128)(2,1)S(1)}, bf16[4,256,256]{2,1,0:T(8,128)(2,1)S(1)}, u32[]{:S(2)}, u32[]{:S(2)}) collective-permute-start(bf16[4,256,256]{2,1,0:T(8,128)(2,1)S(1)} %shard_map.77.refs_1_), channel_id=1, source_target_pairs={{0,4},{4,8},{8,12},{12,16},{16,20},{20,24},{24,28},{28,0},{1,5},{5... | collective-permute-start | bytes 1572872 | tf_op jit(solution)/shard_map/ppermute | solution.py:28
  24.2 8.4 %collective-permute-start.5 = (bf16[2,128,256]{2,1,0:T(8,128)(2,1)S(1)}, bf16[2,128,256]{2,1,0:T(8,128)(2,1)S(1)}, u32[]{:S(2)}, u32[]{:S(2)}) collective-permute-start(bf16[2,128,256]{2,1,0:T(8,128)(2,1)S(1)} %add_convert_fusion.3.refs_0_), channel_id=1, source_target_pairs={{0,2},{1,3},{2,0},{3,1},{4,6},{5,7},{6,4},{7,5},{8,10},{9,11},{10,... | collective-permute-start | bytes 393224 | tf_op jit(solution)/shard_map/ppermute | solution.py:41
  25.8 6.7 %collective-permute-start = (s32[2,128]{1,0:T(2,128)S(1)}, s32[2,128]{1,0:T(2,128)S(1)}, u32[]{:S(2)}, u32[]{:S(2)}) collective-permute-start(s32[2,128]{1,0:T(2,128)S(1)} %broadcast_in_dim.4), channel_id=1, source_target_pairs={{0,4},{4,8},{8,12},{12,16},{16,20},{20,24},{24,28},{28,0},{1,5},{5... | collective-permute-start | bytes 3080 | tf_op jit(solution)/shard_map/ppermute | solution.py:28
  32.8 6.5 %collective-permute-start.9 = (bf16[2,128,256]{2,1,0:T(8,128)(2,1)S(1)}, bf16[2,128,256]{2,1,0:T(8,128)(2,1)S(1)}, u32[]{:S(2)}, u32[]{:S(2)}) collective-permute-start(bf16[2,128,256]{2,1,0:T(8,128)(2,1)S(1)} %get-tuple-element.28.refs_0_), channel_id=1, source_target_pairs={{0,28},{4,0},{8,4},{12,8},{16,12},{20,16},{24,20},{28,24},{1,29},{... | collective-permute-start | bytes 393224 | tf_op jit(solution)/shard_map/ppermute | solution.py:28
  33.3 7.7 %collective-permute-start.8 = (bf16[2,128,256]{2,1,0:T(8,128)(2,1)S(1)}, bf16[2,128,256]{2,1,0:T(8,128)(2,1)S(1)}, u32[]{:S(2)}, u32[]{:S(2)}) collective-permute-start(bf16[2,128,256]{2,1,0:T(8,128)(2,1)S(1)} %get-tuple-element.28.refs_0_), channel_id=1, source_target_pairs={{0,4},{4,8},{8,12},{12,16},{16,20},{20,24},{24,28},{28,0},{1,5},{5... | collective-permute-start | bytes 393224 | tf_op jit(solution)/shard_map/ppermute | solution.py:28
  34.9 6.2 %collective-permute-start.13 = (f32[8,128]{1,0:T(8,128)S(1)}, f32[8,128]{1,0:T(8,128)S(1)}, u32[]{:S(2)}, u32[]{:S(2)}) collective-permute-start(f32[8,128]{1,0:T(8,128)S(1)} %get-tuple-element.29), channel_id=1, source_target_pairs={{0,24},{4,28},{8,16},{12,20},{16,8},{20,12},{24,0},{28,4},{1,25},{... | collective-permute-start | bytes 12296 | tf_op jit(solution)/shard_map/ppermute | solution.py:280
  34.9 6.2 %collective-permute-start.12 = (f32[8,128]{1,0:T(8,128)S(1)}, f32[8,128]{1,0:T(8,128)S(1)}, u32[]{:S(2)}, u32[]{:S(2)}) collective-permute-start(f32[8,128]{1,0:T(8,128)S(1)} %get-tuple-element.29), channel_id=1, source_target_pairs={{0,8},{4,12},{8,0},{12,4},{16,24},{20,28},{24,16},{28,20},{1,9},{5... | collective-permute-start | bytes 12296 | tf_op jit(solution)/shard_map/ppermute | solution.py:280
  34.9 6.2 %collective-permute-start.11 = (f32[8,128]{1,0:T(8,128)S(1)}, f32[8,128]{1,0:T(8,128)S(1)}, u32[]{:S(2)}, u32[]{:S(2)}) collective-permute-start(f32[8,128]{1,0:T(8,128)S(1)} %get-tuple-element.29), channel_id=1, source_target_pairs={{0,16},{4,20},{8,24},{12,28},{16,0},{20,4},{24,8},{28,12},{1,17},{... | collective-permute-start | bytes 12296 | tf_op jit(solution)/shard_map/ppermute | solution.py:280
  41.0 5.3 %collective-permute-start.10 = (bf16[4,128,256]{2,1,0:T(8,128)(2,1)S(1)}, bf16[4,128,256]{2,1,0:T(8,128)(2,1)S(1)}, u32[]{:S(2)}, u32[]{:S(2)}) collective-permute-start(bf16[4,128,256]{2,1,0:T(8,128)(2,1)S(1)} %shard_map.82.refs_2_), channel_id=1, source_target_pairs={{0,1},{1,0},{2,3},{3,2},{4,5},{5,4},{6,7},{7,6},{8,9},{9,8},{10,11... | collective-permute-start | bytes 786440 | tf_op jit(solution)/shard_map/ppermute | solution.py:32
  41.1 3.8 %collective-permute-start.16 = (f32[8,128]{1,0:T(8,128)S(1)}, f32[8,128]{1,0:T(8,128)S(1)}, u32[]{:S(2)}, u32[]{:S(2)}) collective-permute-start(f32[8,128]{1,0:T(8,128)S(1)} %add_add_fusion.7), channel_id=1, source_target_pairs={{0,5},{1,4},{2,7},{3,6},{4,1},{5,0},{6,3},{7,2},{8,13},{9,12},{10,... | collective-permute-start | bytes 12296 | tf_op jit(solution)/shard_map/ppermute | solution.py:280
  41.2 3.8 %collective-permute-start.15 = (f32[8,128]{1,0:T(8,128)S(1)}, f32[8,128]{1,0:T(8,128)S(1)}, u32[]{:S(2)}, u32[]{:S(2)}) collective-permute-start(f32[8,128]{1,0:T(8,128)S(1)} %add_add_fusion.7), channel_id=1, source_target_pairs={{0,4},{1,5},{2,6},{3,7},{4,0},{5,1},{6,2},{7,3},{8,12},{9,13},{10,... | collective-permute-start | bytes 12296 | tf_op jit(solution)/shard_map/ppermute | solution.py:280
  43.3 1.6 %collective-permute-start.14 = (f32[8,128]{1,0:T(8,128)S(1)}, f32[8,128]{1,0:T(8,128)S(1)}, u32[]{:S(2)}, u32[]{:S(2)}) collective-permute-start(f32[8,128]{1,0:T(8,128)S(1)} %add_add_fusion.7), channel_id=1, source_target_pairs={{0,1},{1,0},{2,3},{3,2},{4,5},{5,4},{6,7},{7,6},{8,9},{9,8},{10,11... | collective-permute-start | bytes 12296 | tf_op jit(solution)/shard_map/ppermute | solution.py:280
  43.3 19.9 %collective-permute-start.24 = (bf16[5,256,256]{2,1,0:T(8,128)(2,1)S(1)}, bf16[5,256,256]{2,1,0:T(8,128)(2,1)S(1)}, u32[]{:S(2)}, u32[]{:S(2)}) collective-permute-start(bf16[5,256,256]{2,1,0:T(8,128)(2,1)S(1)} %get-tuple-element.35), channel_id=1, source_target_pairs={{0,4},{4,8},{8,12},{12,16},{16,20},{20,24},{24,28},{28,0},{1,5},{5... | collective-permute-start | bytes 1966088 | tf_op jit(solution)/shard_map/ppermute | solution.py:28
  49.8 5.6 %collective-permute-start.18 = (bf16[2,128,256]{2,1,0:T(8,128)(2,1)S(1)}, bf16[2,128,256]{2,1,0:T(8,128)(2,1)S(1)}, u32[]{:S(2)}, u32[]{:S(2)}) collective-permute-start(bf16[2,128,256]{2,1,0:T(8,128)(2,1)S(1)} %add_convert_fusion.2.refs_0_), channel_id=1, source_target_pairs={{0,2},{1,3},{2,0},{3,1},{4,6},{5,7},{6,4},{7,5},{8,10},{9,11},{10,... | collective-permute-start | bytes 393224 | tf_op jit(solution)/shard_map/ppermute | solution.py:41
  55.6 13.2 %collective-permute-start.21 = (bf16[2,128,256]{2,1,0:T(8,128)(2,1)S(1)}, bf16[2,128,256]{2,1,0:T(8,128)(2,1)S(1)}, u32[]{:S(2)}, u32[]{:S(2)}) collective-permute-start(bf16[2,128,256]{2,1,0:T(8,128)(2,1)S(1)} %get-tuple-element.33.refs_0_), channel_id=1, source_target_pairs={{0,28},{4,0},{8,4},{12,8},{16,12},{20,16},{24,20},{28,24},{1,29},{... | collective-permute-start | bytes 393224 | tf_op jit(solution)/shard_map/ppermute | solution.py:28
  58.9 9.9 %collective-permute-start.20 = (bf16[2,128,256]{2,1,0:T(8,128)(2,1)S(1)}, bf16[2,128,256]{2,1,0:T(8,128)(2,1)S(1)}, u32[]{:S(2)}, u32[]{:S(2)}) collective-permute-start(bf16[2,128,256]{2,1,0:T(8,128)(2,1)S(1)} %get-tuple-element.33.refs_0_), channel_id=1, source_target_pairs={{0,4},{4,8},{8,12},{12,16},{16,20},{20,24},{24,28},{28,0},{1,5},{5... | collective-permute-start | bytes 393224 | tf_op jit(solution)/shard_map/ppermute | solution.py:28
  58.9 10.0 %collective-permute-start.26 = (f32[8,128]{1,0:T(8,128)S(1)}, f32[8,128]{1,0:T(8,128)S(1)}, u32[]{:S(2)}, u32[]{:S(2)}) collective-permute-start(f32[8,128]{1,0:T(8,128)S(1)} %get-tuple-element.34), channel_id=1, source_target_pairs={{0,24},{4,28},{8,16},{12,20},{16,8},{20,12},{24,0},{28,4},{1,25},{... | collective-permute-start | bytes 12296 | tf_op jit(solution)/shard_map/ppermute | solution.py:280
  59.5 9.4 %collective-permute-start.23 = (f32[8,128]{1,0:T(8,128)S(1)}, f32[8,128]{1,0:T(8,128)S(1)}, u32[]{:S(2)}, u32[]{:S(2)}) collective-permute-start(f32[8,128]{1,0:T(8,128)S(1)} %get-tuple-element.34), channel_id=1, source_target_pairs={{0,16},{4,20},{8,24},{12,28},{16,0},{20,4},{24,8},{28,12},{1,17},{... | collective-permute-start | bytes 12296 | tf_op jit(solution)/shard_map/ppermute | solution.py:280
  63.3 5.6 %collective-permute-start.25 = (f32[8,128]{1,0:T(8,128)S(1)}, f32[8,128]{1,0:T(8,128)S(1)}, u32[]{:S(2)}, u32[]{:S(2)}) collective-permute-start(f32[8,128]{1,0:T(8,128)S(1)} %shard_map.86), channel_id=1, source_target_pairs={{0,8},{4,12},{8,0},{12,4},{16,24},{20,28},{24,16},{28,20},{1,9},{5... | collective-permute-start | bytes 12296 | tf_op jit(solution)/shard_map/ppermute | solution.py:280
  68.8 4.7 %collective-permute-start.22 = (bf16[4,128,256]{2,1,0:T(8,128)(2,1)S(1)}, bf16[4,128,256]{2,1,0:T(8,128)(2,1)S(1)}, u32[]{:S(2)}, u32[]{:S(2)}) collective-permute-start(bf16[4,128,256]{2,1,0:T(8,128)(2,1)S(1)} %shard_map.85.refs_2_), channel_id=1, source_target_pairs={{0,1},{1,0},{2,3},{3,2},{4,5},{5,4},{6,7},{7,6},{8,9},{9,8},{10,11... | collective-permute-start | bytes 786440 | tf_op jit(solution)/shard_map/ppermute | solution.py:32
  69.0 3.1 %collective-permute-start.29 = (f32[8,128]{1,0:T(8,128)S(1)}, f32[8,128]{1,0:T(8,128)S(1)}, u32[]{:S(2)}, u32[]{:S(2)}) collective-permute-start(f32[8,128]{1,0:T(8,128)S(1)} %add_add_fusion.5), channel_id=1, source_target_pairs={{0,5},{1,4},{2,7},{3,6},{4,1},{5,0},{6,3},{7,2},{8,13},{9,12},{10,... | collective-permute-start | bytes 12296 | tf_op jit(solution)/shard_map/ppermute | solution.py:280
  69.0 3.8 %collective-permute-start.28 = (f32[8,128]{1,0:T(8,128)S(1)}, f32[8,128]{1,0:T(8,128)S(1)}, u32[]{:S(2)}, u32[]{:S(2)}) collective-permute-start(f32[8,128]{1,0:T(8,128)S(1)} %add_add_fusion.5), channel_id=1, source_target_pairs={{0,4},{1,5},{2,6},{3,7},{4,0},{5,1},{6,2},{7,3},{8,12},{9,13},{10,... | collective-permute-start | bytes 12296 | tf_op jit(solution)/shard_map/ppermute | solution.py:280
  71.2 1.6 %collective-permute-start.27 = (f32[8,128]{1,0:T(8,128)S(1)}, f32[8,128]{1,0:T(8,128)S(1)}, u32[]{:S(2)}, u32[]{:S(2)}) collective-permute-start(f32[8,128]{1,0:T(8,128)S(1)} %add_add_fusion.5), channel_id=1, source_target_pairs={{0,1},{1,0},{2,3},{3,2},{4,5},{5,4},{6,7},{7,6},{8,9},{9,8},{10,11... | collective-permute-start | bytes 12296 | tf_op jit(solution)/shard_map/ppermute | solution.py:280
  71.2 19.9 %collective-permute-start.37 = (bf16[5,256,256]{2,1,0:T(8,128)(2,1)S(1)}, bf16[5,256,256]{2,1,0:T(8,128)(2,1)S(1)}, u32[]{:S(2)}, u32[]{:S(2)}) collective-permute-start(bf16[5,256,256]{2,1,0:T(8,128)(2,1)S(1)} %get-tuple-element.41), channel_id=1, source_target_pairs={{0,4},{4,8},{8,12},{12,16},{16,20},{20,24},{24,28},{28,0},{1,5},{5... | collective-permute-start | bytes 1966088 | tf_op jit(solution)/shard_map/ppermute | solution.py:28
  77.1 5.8 %collective-permute-start.31 = (bf16[2,128,256]{2,1,0:T(8,128)(2,1)S(1)}, bf16[2,128,256]{2,1,0:T(8,128)(2,1)S(1)}, u32[]{:S(2)}, u32[]{:S(2)}) collective-permute-start(bf16[2,128,256]{2,1,0:T(8,128)(2,1)S(1)} %add_convert_fusion.1.refs_0_), channel_id=1, source_target_pairs={{0,2},{1,3},{2,0},{3,1},{4,6},{5,7},{6,4},{7,5},{8,10},{9,11},{10,... | collective-permute-start | bytes 393224 | tf_op jit(solution)/shard_map/ppermute | solution.py:41
  83.1 13.6 %collective-permute-start.34 = (bf16[2,128,256]{2,1,0:T(8,128)(2,1)S(1)}, bf16[2,128,256]{2,1,0:T(8,128)(2,1)S(1)}, u32[]{:S(2)}, u32[]{:S(2)}) collective-permute-start(bf16[2,128,256]{2,1,0:T(8,128)(2,1)S(1)} %get-tuple-element.39.refs_0_), channel_id=1, source_target_pairs={{0,28},{4,0},{8,4},{12,8},{16,12},{20,16},{24,20},{28,24},{1,29},{... | collective-permute-start | bytes 393224 | tf_op jit(solution)/shard_map/ppermute | solution.py:28
  86.7 9.9 %collective-permute-start.33 = (bf16[2,128,256]{2,1,0:T(8,128)(2,1)S(1)}, bf16[2,128,256]{2,1,0:T(8,128)(2,1)S(1)}, u32[]{:S(2)}, u32[]{:S(2)}) collective-permute-start(bf16[2,128,256]{2,1,0:T(8,128)(2,1)S(1)} %get-tuple-element.39.refs_0_), channel_id=1, source_target_pairs={{0,4},{4,8},{8,12},{12,16},{16,20},{20,24},{24,28},{28,0},{1,5},{5... | collective-permute-start | bytes 393224 | tf_op jit(solution)/shard_map/ppermute | solution.py:28
  91.1 5.6 %collective-permute-start.38 = (f32[8,128]{1,0:T(8,128)S(1)}, f32[8,128]{1,0:T(8,128)S(1)}, u32[]{:S(2)}, u32[]{:S(2)}) collective-permute-start(f32[8,128]{1,0:T(8,128)S(1)} %shard_map.90), channel_id=1, source_target_pairs={{0,8},{4,12},{8,0},{12,4},{16,24},{20,28},{24,16},{28,20},{1,9},{5... | collective-permute-start | bytes 12296 | tf_op jit(solution)/shard_map/ppermute | solution.py:280
  91.1 5.6 %collective-permute-start.39 = (f32[8,128]{1,0:T(8,128)S(1)}, f32[8,128]{1,0:T(8,128)S(1)}, u32[]{:S(2)}, u32[]{:S(2)}) collective-permute-start(f32[8,128]{1,0:T(8,128)S(1)} %get-tuple-element.40), channel_id=1, source_target_pairs={{0,24},{4,28},{8,16},{12,20},{16,8},{20,12},{24,0},{28,4},{1,25},{... | collective-permute-start | bytes 12296 | tf_op jit(solution)/shard_map/ppermute | solution.py:280
  91.9 4.8 %collective-permute-start.36 = (f32[8,128]{1,0:T(8,128)S(1)}, f32[8,128]{1,0:T(8,128)S(1)}, u32[]{:S(2)}, u32[]{:S(2)}) collective-permute-start(f32[8,128]{1,0:T(8,128)S(1)} %get-tuple-element.40), channel_id=1, source_target_pairs={{0,16},{4,20},{8,24},{12,28},{16,0},{20,4},{24,8},{28,12},{1,17},{... | collective-permute-start | bytes 12296 | tf_op jit(solution)/shard_map/ppermute | solution.py:280
  96.6 4.0 %collective-permute-start.35 = (bf16[4,128,256]{2,1,0:T(8,128)(2,1)S(1)}, bf16[4,128,256]{2,1,0:T(8,128)(2,1)S(1)}, u32[]{:S(2)}, u32[]{:S(2)}) collective-permute-start(bf16[4,128,256]{2,1,0:T(8,128)(2,1)S(1)} %shard_map.89.refs_2_), channel_id=1, source_target_pairs={{0,1},{1,0},{2,3},{3,2},{4,5},{5,4},{6,7},{7,6},{8,9},{9,8},{10,11... | collective-permute-start | bytes 786440 | tf_op jit(solution)/shard_map/ppermute | solution.py:32
  96.8 3.1 %collective-permute-start.42 = (f32[8,128]{1,0:T(8,128)S(1)}, f32[8,128]{1,0:T(8,128)S(1)}, u32[]{:S(2)}, u32[]{:S(2)}) collective-permute-start(f32[8,128]{1,0:T(8,128)S(1)} %add_add_fusion.3), channel_id=1, source_target_pairs={{0,5},{1,4},{2,7},{3,6},{4,1},{5,0},{6,3},{7,2},{8,13},{9,12},{10,... | collective-permute-start | bytes 12296 | tf_op jit(solution)/shard_map/ppermute | solution.py:280
  96.8 3.8 %collective-permute-start.41 = (f32[8,128]{1,0:T(8,128)S(1)}, f32[8,128]{1,0:T(8,128)S(1)}, u32[]{:S(2)}, u32[]{:S(2)}) collective-permute-start(f32[8,128]{1,0:T(8,128)S(1)} %add_add_fusion.3), channel_id=1, source_target_pairs={{0,4},{1,5},{2,6},{3,7},{4,0},{5,1},{6,2},{7,3},{8,12},{9,13},{10,... | collective-permute-start | bytes 12296 | tf_op jit(solution)/shard_map/ppermute | solution.py:280
  99.0 1.6 %collective-permute-start.40 = (f32[8,128]{1,0:T(8,128)S(1)}, f32[8,128]{1,0:T(8,128)S(1)}, u32[]{:S(2)}, u32[]{:S(2)}) collective-permute-start(f32[8,128]{1,0:T(8,128)S(1)} %add_add_fusion.3), channel_id=1, source_target_pairs={{0,1},{1,0},{2,3},{3,2},{4,5},{5,4},{6,7},{7,6},{8,9},{9,8},{10,11... | collective-permute-start | bytes 12296 | tf_op jit(solution)/shard_map/ppermute | solution.py:280
  102.7 2.2 %collective-permute-start.43 = (bf16[2,128,256]{2,1,0:T(8,128)(2,1)S(1)}, bf16[2,128,256]{2,1,0:T(8,128)(2,1)S(1)}, u32[]{:S(2)}, u32[]{:S(2)}) collective-permute-start(bf16[2,128,256]{2,1,0:T(8,128)(2,1)S(1)} %get-tuple-element.44), channel_id=1, source_target_pairs={{0,1},{1,0},{2,3},{3,2},{4,5},{5,4},{6,7},{7,6},{8,9},{9,8},{10,11... | collective-permute-start | bytes 393224 | tf_op jit(solution)/shard_map/ppermute | solution.py:32
  103.7 11.0 %collective-permute-start.46 = (bf16[2,256,256]{2,1,0:T(8,128)(2,1)S(1)}, bf16[2,256,256]{2,1,0:T(8,128)(2,1)S(1)}, u32[]{:S(2)}, u32[]{:S(2)}) collective-permute-start(bf16[2,256,256]{2,1,0:T(8,128)(2,1)S(1)} %get-tuple-element.46), channel_id=1, source_target_pairs={{0,4},{4,8},{8,12},{12,16},{16,20},{20,24},{24,28},{28,0},{1,5},{5... | collective-permute-start | bytes 786440 | tf_op jit(solution)/shard_map/ppermute | solution.py:28
  104.9 5.7 %collective-permute-start.44 = (bf16[2,128,256]{2,1,0:T(8,128)(2,1)S(1)}, bf16[2,128,256]{2,1,0:T(8,128)(2,1)S(1)}, u32[]{:S(2)}, u32[]{:S(2)}) collective-permute-start(bf16[2,128,256]{2,1,0:T(8,128)(2,1)S(1)} %add_convert_fusion.refs_0_), channel_id=1, source_target_pairs={{0,2},{1,3},{2,0},{3,1},{4,6},{5,7},{6,4},{7,5},{8,10},{9,11},{10,... | collective-permute-start | bytes 393224 | tf_op jit(solution)/shard_map/ppermute | solution.py:41
  110.7 7.8 %collective-permute-start.52 = (bf16[2,128,256]{2,1,0:T(8,128)(2,1)S(1)}, bf16[2,128,256]{2,1,0:T(8,128)(2,1)S(1)}, u32[]{:S(2)}, u32[]{:S(2)}) collective-permute-start(bf16[2,128,256]{2,1,0:T(8,128)(2,1)S(1)} %get-tuple-element.47.refs_1_), channel_id=1, source_target_pairs={{0,4},{4,8},{8,12},{12,16},{16,20},{20,24},{24,28},{28,0},{1,5},{5... | collective-permute-start | bytes 393224 | tf_op jit(solution)/shard_map/ppermute | solution.py:28
  112.0 6.6 %collective-permute-start.48 = (f32[8,128]{1,0:T(8,128)S(1)}, f32[8,128]{1,0:T(8,128)S(1)}, u32[]{:S(2)}, u32[]{:S(2)}) collective-permute-start(f32[8,128]{1,0:T(8,128)S(1)} %get-tuple-element.45), channel_id=1, source_target_pairs={{0,24},{4,28},{8,16},{12,20},{16,8},{20,12},{24,0},{28,4},{1,25},{... | collective-permute-start | bytes 12296 | tf_op jit(solution)/shard_map/ppermute | solution.py:280
  114.7 4.5 %collective-permute-start.45 = (f32[8,128]{1,0:T(8,128)S(1)}, f32[8,128]{1,0:T(8,128)S(1)}, u32[]{:S(2)}, u32[]{:S(2)}) collective-permute-start(f32[8,128]{1,0:T(8,128)S(1)} %get-tuple-element.45), channel_id=1, source_target_pairs={{0,16},{4,20},{8,24},{12,28},{16,0},{20,4},{24,8},{28,12},{1,17},{... | collective-permute-start | bytes 12296 | tf_op jit(solution)/shard_map/ppermute | solution.py:280
  114.7 4.5 %collective-permute-start.47 = (f32[8,128]{1,0:T(8,128)S(1)}, f32[8,128]{1,0:T(8,128)S(1)}, u32[]{:S(2)}, u32[]{:S(2)}) collective-permute-start(f32[8,128]{1,0:T(8,128)S(1)} %shard_map.93), channel_id=1, source_target_pairs={{0,8},{4,12},{8,0},{12,4},{16,24},{20,28},{24,16},{28,20},{1,9},{5... | collective-permute-start | bytes 12296 | tf_op jit(solution)/shard_map/ppermute | solution.py:280
  118.5 4.4 %collective-permute-start.53 = (bf16[4,128,256]{2,1,0:T(8,128)(2,1)S(1)}, bf16[4,128,256]{2,1,0:T(8,128)(2,1)S(1)}, u32[]{:S(2)}, u32[]{:S(2)}) collective-permute-start(bf16[4,128,256]{2,1,0:T(8,128)(2,1)S(1)} %shard_map.94.pair), channel_id=1, source_target_pairs={{0,1},{1,0},{2,3},{3,2},{4,5},{5,4},{6,7},{7,6},{8,9},{9,8},{10,11... | collective-permute-start | bytes 786440 | tf_op jit(solution)/shard_map/ppermute | solution.py:32
  119.2 3.1 %collective-permute-start.51 = (f32[8,128]{1,0:T(8,128)S(1)}, f32[8,128]{1,0:T(8,128)S(1)}, u32[]{:S(2)}, u32[]{:S(2)}) collective-permute-start(f32[8,128]{1,0:T(8,128)S(1)} %add_add_fusion.1), channel_id=1, source_target_pairs={{0,5},{1,4},{2,7},{3,6},{4,1},{5,0},{6,3},{7,2},{8,13},{9,12},{10,... | collective-permute-start | bytes 12296 | tf_op jit(solution)/shard_map/ppermute | solution.py:280
  119.3 3.7 %collective-permute-start.50 = (f32[8,128]{1,0:T(8,128)S(1)}, f32[8,128]{1,0:T(8,128)S(1)}, u32[]{:S(2)}, u32[]{:S(2)}) collective-permute-start(f32[8,128]{1,0:T(8,128)S(1)} %add_add_fusion.1), channel_id=1, source_target_pairs={{0,4},{1,5},{2,6},{3,7},{4,0},{5,1},{6,2},{7,3},{8,12},{9,13},{10,... | collective-permute-start | bytes 12296 | tf_op jit(solution)/shard_map/ppermute | solution.py:280
  120.8 2.1 %collective-permute-start.49 = (f32[8,128]{1,0:T(8,128)S(1)}, f32[8,128]{1,0:T(8,128)S(1)}, u32[]{:S(2)}, u32[]{:S(2)}) collective-permute-start(f32[8,128]{1,0:T(8,128)S(1)} %add_add_fusion.1), channel_id=1, source_target_pairs={{0,1},{1,0},{2,3},{3,2},{4,5},{5,4},{6,7},{7,6},{8,9},{9,8},{10,11... | collective-permute-start | bytes 12296 | tf_op jit(solution)/shard_map/ppermute | solution.py:280
  (14 other events, 92.0 us)

commit v5 on v4

--- a/solution.py
+++ b/solution.py
@@ -234,7 +234,6 @@
     units = [(piece, i) for piece, size in zip(pieces, sizes) for i in range(size)]
     columns = lax.broadcasted_iota(jnp.int32, (width, width), 1)
     scale = 1.0 / float(width) ** 0.5
-    flipped = []
 
     def fill(group):
         for ref, row in zip((pair, pair_other), rows):
@@ -245,27 +244,29 @@
                 window[place, row, :] = new.astype(BF16)
 
     fill(0)
-    fill(1)
-    final_out = pltpu.make_async_copy(window.at[pl.ds(sectors, sectors)], final, final_sem)
-    final_out.start()
+    copies = []
     for b in range(sectors):
         block = jnp.where(columns < kept[b : b + 1, 0:1], window[b].astype(F32), 0.0)
-        flipped.append((block * scale).astype(BF16).T)
+        flipped = (block * scale).astype(BF16).T
         block = block.astype(BF16)
         for t, (piece, i) in enumerate(units[b::sectors]):
             product = jnp.dot(piece[i], block, preferred_element_type=F32)
             projected[b, :, t * width : (t + 1) * width] = product.astype(BF16)
-    copies = []
-    for b in range(sectors):
         for t in range(len(units) // sectors):
             part = projected[b, :, t * width : (t + 1) * width]
-            result = jnp.dot(flipped[b], part, preferred_element_type=F32)
+            result = jnp.dot(flipped, part, preferred_element_type=F32)
             results[t, b] = result.astype(BF16)
             copy = pltpu.make_async_copy(
                 results.at[t, b], new_ops.at[t, b], sems.at[t * sectors + b]
             )
             copy.start()
             copies.append(copy)
+        if b == 0:
+            fill(1)
+            final_out = pltpu.make_async_copy(
+                window.at[pl.ds(sectors, sectors)], final, final_sem
+            )
+            final_out.start()
     final_out.wait()
     for copy in copies:
         copy.wait()

time: 126 us -> 126 us (level)
  no operation moved by 1% of the time
where the time goes in v5:
time: 126 us; the launch traced here: 125 us
  starting transfers between devices  53.6 us (43%)
  waiting for transfers between devices  53.4 us (42%)
  Pallas kernels  13.6 us (11%)
  local copies, waits for them, and re-layouts  3.75 us (3%)
    ppermute x14, waiting for transfers between devices, sec_move(): lax.ppermute(x, 'sec', [(i, (i + distance) % count) for i in range(count)])  29.6 us
    ppermute x24, starting transfers between devices, other(): return lax.ppermute(sent, axes, [(i, i ^ mask) for i in range(size)])  24.7 us
    ppermute x14, starting transfers between devices, sec_move(): lax.ppermute(x, 'sec', [(i, (i + distance) % count) for i in range(count)])  19.2 us
    ppermute x4, waiting for transfers between devices, chip_parts(): parts.append(lax.ppermute(x, 'op', route))  12.3 us
    pallas_call x18, Pallas kernels, call(): pl.pallas_call(kernel, out_shape=tuple(outs), in_specs=specs, out_specs=t...  11 us
    ppermute x12, waiting for transfers between devices, core_swap(): lax.ppermute(x, 'op', [(i, i ^ 1) for i in range(lax.axis_size('op'))])  6.96 us
    ppermute x4, starting transfers between devices, chip_parts(): parts.append(lax.ppermute(x, 'op', route))  6.35 us
    ppermute x24, waiting for transfers between devices, other(): return lax.ppermute(sent, axes, [(i, i ^ mask) for i in range(size)])  4.45 us
  transfers between devices with their start and end apart: 54, of which 25 were waited for; matrix products, arithmetic and copies ran while one was open for 0% of the time, Pallas kernels for 7%

profile of v5, /device:TPU:0, one launch (start us, length us, event | category | flops | bytes accessed | tf_op | source)
XLA Modules:
  0.0 125.5 jit_solution(7552510183095943813)
XLA Ops:
  0.6 1.0 constant_dynamic-slice_fusion
  1.7 6.0 %collective-permute-start.2 = (bf16[2,128,256]{2,1,0:T(8,128)(2,1)S(1)}, bf16[2,128,256]{2,1,0:T(8,128)(2,1)S(1)}, u32[]{:S(2)}, u32[]{:S(2)}) collective-permute-start(bf16[2,128,256]{2,1,0:T(8,128)(2,1)S(1)} %get-tuple-element.49.refs_0_), channel_id=1, source_target_pairs={{0,28},{4,0},{8,4},{12,8},{16,12},{20,16},{24,20},{28,24},{1,29},{... | collective-permute-start | bytes 393224 | tf_op jit(solution)/shard_map/ppermute | solution.py:28
  7.7 1.1 shard_map.77.refs_1_
  8.9 1.6 %collective-permute-done.2.refs_0_ = bf16[2,128,256]{2,1,0:T(8,128)(2,1)S(1)} collective-permute-done((bf16[2,128,256]{2,1,0:T(8,128)(2,1)S(1)}, bf16[2,128,256]{2,1,0:T(8,128)(2,1)S(1)}, u32[]{:S(2)}, u32[]{:S(2)}) %collective-permute-start.2) | collective-permute-done | bytes 131104 | tf_op jit(solution)/shard_map/ppermute | solution.py:28
  10.5 4.9 %collective-permute-done.1.refs_0_ = bf16[2,128,256]{2,1,0:T(8,128)(2,1)S(1)} collective-permute-done((bf16[2,128,256]{2,1,0:T(8,128)(2,1)S(1)}, bf16[2,128,256]{2,1,0:T(8,128)(2,1)S(1)}, u32[]{:S(2)}, u32[]{:S(2)}) %collective-permute-start.1) | collective-permute-done | bytes 131104 | tf_op jit(solution)/shard_map/ppermute | solution.py:28
  15.6 1.5 %collective-permute-done.3.refs_3_ = bf16[4,128,256]{2,1,0:T(8,128)(2,1)} collective-permute-done((bf16[4,128,256]{2,1,0:T(8,128)(2,1)S(1)}, bf16[4,128,256]{2,1,0:T(8,128)(2,1)}, u32[]{:S(2)}, u32[]{:S(2)}) %collective-permute-start.3) | collective-permute-done | bytes 262176 | tf_op jit(solution)/shard_map/ppermute | solution.py:32
  17.1 1.6 %copy-done.1 = bf16[8,2,256,256]{3,2,1,0:T(8,128)(2,1)S(1)} copy-done((bf16[8,2,256,256]{3,2,1,0:T(8,128)(2,1)S(1)}, bf16[8,2,256,256]{3,2,1,0:T(8,128)(2,1)}, u32[]{:S(2)}) %copy-start.1) | copy-done | bytes 2097176
  19.6 3.1 %shard_map.80 = (f32[2,128,256]{2,1,0:T(8,128)S(1)}, bf16[2,128,256]{2,1,0:T(8,128)(2,1)S(1)}, bf16[6,256,256]{2,1,0:T(8,128)(2,1)S(1)}, bf16[5,256,256]{2,1,0:T(8,128)(2,1)S(1)}) custom-call(s32[8,2]{1,0:T(8,128)S(1)} %copy.18.partner_any, bf16[8,2,256,256]{3,2,1,0:T(8,128)(2,1)S(1)} %copy-done, bf16[8,2,256,256]{3,2,1,0:T(8,128)(2,1)S(1)} %copy-done.1, ...), custom_call_target="tpu_custom_call" | custom-call | tf_op jit(solution)/shard_map/pallas_call | solution.py:54
  22.9 1.2 collective-permute-done.4
  24.2 1.6 %collective-permute-start.5 = (bf16[2,128,256]{2,1,0:T(8,128)(2,1)S(1)}, bf16[2,128,256]{2,1,0:T(8,128)(2,1)S(1)}, u32[]{:S(2)}, u32[]{:S(2)}) collective-permute-start(bf16[2,128,256]{2,1,0:T(8,128)(2,1)S(1)} %add_convert_fusion.3.refs_0_), channel_id=1, source_target_pairs={{0,2},{1,3},{2,0},{3,1},{4,6},{5,7},{6,4},{7,5},{8,10},{9,11},{10,... | collective-permute-start | bytes 393224 | tf_op jit(solution)/shard_map/ppermute | solution.py:41
  25.8 6.7 %collective-permute-done.refs_2_.kept = s32[2,128]{1,0:T(2,128)S(1)} collective-permute-done((s32[2,128]{1,0:T(2,128)S(1)}, s32[2,128]{1,0:T(2,128)S(1)}, u32[]{:S(2)}, u32[]{:S(2)}) %collective-permute-start) | collective-permute-done | bytes 1056 | tf_op jit(solution)/shard_map/ppermute | solution.py:28
  33.3 1.6 %collective-permute-start.8 = (bf16[2,128,256]{2,1,0:T(8,128)(2,1)S(1)}, bf16[2,128,256]{2,1,0:T(8,128)(2,1)S(1)}, u32[]{:S(2)}, u32[]{:S(2)}) collective-permute-start(bf16[2,128,256]{2,1,0:T(8,128)(2,1)S(1)} %get-tuple-element.28.refs_0_), channel_id=1, source_target_pairs={{0,4},{4,8},{8,12},{12,16},{16,20},{20,24},{24,28},{28,0},{1,5},{5... | collective-permute-start | bytes 393224 | tf_op jit(solution)/shard_map/ppermute | solution.py:28
  34.9 4.4 %collective-permute-start.11 = (f32[8,128]{1,0:T(8,128)S(1)}, f32[8,128]{1,0:T(8,128)S(1)}, u32[]{:S(2)}, u32[]{:S(2)}) collective-permute-start(f32[8,128]{1,0:T(8,128)S(1)} %get-tuple-element.29), channel_id=1, source_target_pairs={{0,16},{4,20},{8,24},{12,28},{16,0},{20,4},{24,8},{28,12},{1,17},{... | collective-permute-start | bytes 12296 | tf_op jit(solution)/shard_map/ppermute | solution.py:281
  39.3 1.7 %collective-permute-done.8.refs_0_ = bf16[2,128,256]{2,1,0:T(8,128)(2,1)S(1)} collective-permute-done((bf16[2,128,256]{2,1,0:T(8,128)(2,1)S(1)}, bf16[2,128,256]{2,1,0:T(8,128)(2,1)S(1)}, u32[]{:S(2)}, u32[]{:S(2)}) %collective-permute-start.8) | collective-permute-done | bytes 131104 | tf_op jit(solution)/shard_map/ppermute | solution.py:28
  41.2 2.1 %collective-permute-start.15 = (f32[8,128]{1,0:T(8,128)S(1)}, f32[8,128]{1,0:T(8,128)S(1)}, u32[]{:S(2)}, u32[]{:S(2)}) collective-permute-start(f32[8,128]{1,0:T(8,128)S(1)} %add_add_fusion.7), channel_id=1, source_target_pairs={{0,4},{1,5},{2,6},{3,7},{4,0},{5,1},{6,2},{7,3},{8,12},{9,13},{10,... | collective-permute-start | bytes 12296 | tf_op jit(solution)/shard_map/ppermute | solution.py:281
  43.3 1.6 %collective-permute-start.24 = (bf16[5,256,256]{2,1,0:T(8,128)(2,1)S(1)}, bf16[5,256,256]{2,1,0:T(8,128)(2,1)S(1)}, u32[]{:S(2)}, u32[]{:S(2)}) collective-permute-start(bf16[5,256,256]{2,1,0:T(8,128)(2,1)S(1)} %get-tuple-element.35), channel_id=1, source_target_pairs={{0,4},{4,8},{8,12},{12,16},{16,20},{20,24},{24,28},{28,0},{1,5},{5... | collective-permute-start | bytes 1966088 | tf_op jit(solution)/shard_map/ppermute | solution.py:28
  45.0 1.3 %collective-permute-done.7.refs_1_ = bf16[2,128,256]{2,1,0:T(8,128)(2,1)S(1)} collective-permute-done((bf16[2,128,256]{2,1,0:T(8,128)(2,1)S(1)}, bf16[2,128,256]{2,1,0:T(8,128)(2,1)S(1)}, u32[]{:S(2)}, u32[]{:S(2)}) %collective-permute-start.7) | collective-permute-done | bytes 131104 | tf_op jit(solution)/shard_map/ppermute | solution.py:32
  46.3 2.1 %shard_map.83 = (f32[2,128,256]{2,1,0:T(8,128)S(1)}, bf16[2,128,256]{2,1,0:T(8,128)(2,1)S(1)}, bf16[6,256,256]{2,1,0:T(8,128)(2,1)S(1)}, bf16[5,256,256]{2,1,0:T(8,128)(2,1)S(1)}) custom-call(s32[8,2]{1,0:T(8,128)S(1)} %copy.18.partner_any, bf16[8,2,256,256]{3,2,1,0:T(8,128)(2,1)S(1)} %copy-done, ...), custom_call_target="tpu_custom_call", output_to_operand_aliasing={{2}: (8, {})} | custom-call | tf_op jit(solution)/shard_map/pallas_call | solution.py:54
  48.6 1.2 collective-permute-done.17
  49.8 1.6 %collective-permute-start.18 = (bf16[2,128,256]{2,1,0:T(8,128)(2,1)S(1)}, bf16[2,128,256]{2,1,0:T(8,128)(2,1)S(1)}, u32[]{:S(2)}, u32[]{:S(2)}) collective-permute-start(bf16[2,128,256]{2,1,0:T(8,128)(2,1)S(1)} %add_convert_fusion.2.refs_0_), channel_id=1, source_target_pairs={{0,2},{1,3},{2,0},{3,1},{4,6},{5,7},{6,4},{7,5},{8,10},{9,11},{10,... | collective-permute-start | bytes 393224 | tf_op jit(solution)/shard_map/ppermute | solution.py:41
  51.4 4.0 %collective-permute-done.18.refs_1_ = bf16[2,128,256]{2,1,0:T(8,128)(2,1)S(1)} collective-permute-done((bf16[2,128,256]{2,1,0:T(8,128)(2,1)S(1)}, bf16[2,128,256]{2,1,0:T(8,128)(2,1)S(1)}, u32[]{:S(2)}, u32[]{:S(2)}) %collective-permute-start.18) | collective-permute-done | bytes 131104 | tf_op jit(solution)/shard_map/ppermute | solution.py:41
  55.6 3.3 %collective-permute-start.21 = (bf16[2,128,256]{2,1,0:T(8,128)(2,1)S(1)}, bf16[2,128,256]{2,1,0:T(8,128)(2,1)S(1)}, u32[]{:S(2)}, u32[]{:S(2)}) collective-permute-start(bf16[2,128,256]{2,1,0:T(8,128)(2,1)S(1)} %get-tuple-element.33.refs_0_), channel_id=1, source_target_pairs={{0,28},{4,0},{8,4},{12,8},{16,12},{20,16},{24,20},{28,24},{1,29},{... | collective-permute-start | bytes 393224 | tf_op jit(solution)/shard_map/ppermute | solution.py:28
  59.5 1.7 %collective-permute-start.23 = (f32[8,128]{1,0:T(8,128)S(1)}, f32[8,128]{1,0:T(8,128)S(1)}, u32[]{:S(2)}, u32[]{:S(2)}) collective-permute-start(f32[8,128]{1,0:T(8,128)S(1)} %get-tuple-element.34), channel_id=1, source_target_pairs={{0,16},{4,20},{8,24},{12,28},{16,0},{20,4},{24,8},{28,12},{1,17},{... | collective-permute-start | bytes 12296 | tf_op jit(solution)/shard_map/ppermute | solution.py:281
  61.2 2.1 %collective-permute-done.24.refs_1_ = bf16[5,256,256]{2,1,0:T(8,128)(2,1)S(1)} collective-permute-done((bf16[5,256,256]{2,1,0:T(8,128)(2,1)S(1)}, bf16[5,256,256]{2,1,0:T(8,128)(2,1)S(1)}, u32[]{:S(2)}, u32[]{:S(2)}) %collective-permute-start.24) | collective-permute-done | bytes 655392 | tf_op jit(solution)/shard_map/ppermute | solution.py:28
  63.3 1.6 %collective-permute-start.25 = (f32[8,128]{1,0:T(8,128)S(1)}, f32[8,128]{1,0:T(8,128)S(1)}, u32[]{:S(2)}, u32[]{:S(2)}) collective-permute-start(f32[8,128]{1,0:T(8,128)S(1)} %shard_map.86), channel_id=1, source_target_pairs={{0,8},{4,12},{8,0},{12,4},{16,24},{20,28},{24,16},{28,20},{1,9},{5... | collective-permute-start | bytes 12296 | tf_op jit(solution)/shard_map/ppermute | solution.py:281
  64.9 3.9 %collective-permute-done.21.refs_1_ = bf16[2,128,256]{2,1,0:T(8,128)(2,1)S(1)} collective-permute-done((bf16[2,128,256]{2,1,0:T(8,128)(2,1)S(1)}, bf16[2,128,256]{2,1,0:T(8,128)(2,1)S(1)}, u32[]{:S(2)}, u32[]{:S(2)}) %collective-permute-start.21) | collective-permute-done | bytes 131104 | tf_op jit(solution)/shard_map/ppermute | solution.py:28
  69.0 2.1 %collective-permute-start.28 = (f32[8,128]{1,0:T(8,128)S(1)}, f32[8,128]{1,0:T(8,128)S(1)}, u32[]{:S(2)}, u32[]{:S(2)}) collective-permute-start(f32[8,128]{1,0:T(8,128)S(1)} %add_add_fusion.5), channel_id=1, source_target_pairs={{0,4},{1,5},{2,6},{3,7},{4,0},{5,1},{6,2},{7,3},{8,12},{9,13},{10,... | collective-permute-start | bytes 12296 | tf_op jit(solution)/shard_map/ppermute | solution.py:281
  73.5 2.1 %shard_map.87 = (f32[2,128,256]{2,1,0:T(8,128)S(1)}, bf16[2,128,256]{2,1,0:T(8,128)(2,1)S(1)}, bf16[6,256,256]{2,1,0:T(8,128)(2,1)S(1)}, bf16[2,256,256]{2,1,0:T(8,128)(2,1)S(1)}) custom-call(s32[8,2]{1,0:T(8,128)S(1)} %copy.18.partner_any, bf16[8,2,256,256]{3,2,1,0:T(8,128)(2,1)S(1)} %copy-done, ...), custom_call_target="tpu_custom_call", output_to_operand_aliasing={{2}: (8, {})} | custom-call | tf_op jit(solution)/shard_map/pallas_call | solution.py:54
  76.1 1.0 collective-permute-done.30
  77.1 1.6 %collective-permute-start.31 = (bf16[2,128,256]{2,1,0:T(8,128)(2,1)S(1)}, bf16[2,128,256]{2,1,0:T(8,128)(2,1)S(1)}, u32[]{:S(2)}, u32[]{:S(2)}) collective-permute-start(bf16[2,128,256]{2,1,0:T(8,128)(2,1)S(1)} %add_convert_fusion.1.refs_0_), channel_id=1, source_target_pairs={{0,2},{1,3},{2,0},{3,1},{4,6},{5,7},{6,4},{7,5},{8,10},{9,11},{10,... | collective-permute-start | bytes 393224 | tf_op jit(solution)/shard_map/ppermute | solution.py:41
  78.7 4.2 %collective-permute-done.31.refs_1_ = bf16[2,128,256]{2,1,0:T(8,128)(2,1)S(1)} collective-permute-done((bf16[2,128,256]{2,1,0:T(8,128)(2,1)S(1)}, bf16[2,128,256]{2,1,0:T(8,128)(2,1)S(1)}, u32[]{:S(2)}, u32[]{:S(2)}) %collective-permute-start.31) | collective-permute-done | bytes 131104 | tf_op jit(solution)/shard_map/ppermute | solution.py:41
  83.1 3.6 %collective-permute-start.34 = (bf16[2,128,256]{2,1,0:T(8,128)(2,1)S(1)}, bf16[2,128,256]{2,1,0:T(8,128)(2,1)S(1)}, u32[]{:S(2)}, u32[]{:S(2)}) collective-permute-start(bf16[2,128,256]{2,1,0:T(8,128)(2,1)S(1)} %get-tuple-element.39.refs_0_), channel_id=1, source_target_pairs={{0,28},{4,0},{8,4},{12,8},{16,12},{20,16},{24,20},{28,24},{1,29},{... | collective-permute-start | bytes 393224 | tf_op jit(solution)/shard_map/ppermute | solution.py:28
  86.7 4.4 %collective-permute-done.37.refs_1_.refs_2_ = bf16[5,256,256]{2,1,0:T(8,128)(2,1)S(1)} collective-permute-done((bf16[5,256,256]{2,1,0:T(8,128)(2,1)S(1)}, bf16[5,256,256]{2,1,0:T(8,128)(2,1)S(1)}, u32[]{:S(2)}, u32[]{:S(2)}) %collective-permute-start.37) | collective-permute-done | bytes 655392 | tf_op jit(solution)/shard_map/ppermute | solution.py:28
  91.9 2.7 %collective-permute-start.36 = (f32[8,128]{1,0:T(8,128)S(1)}, f32[8,128]{1,0:T(8,128)S(1)}, u32[]{:S(2)}, u32[]{:S(2)}) collective-permute-start(f32[8,128]{1,0:T(8,128)S(1)} %get-tuple-element.40), channel_id=1, source_target_pairs={{0,16},{4,20},{8,24},{12,28},{16,0},{20,4},{24,8},{28,12},{1,17},{... | collective-permute-start | bytes 12296 | tf_op jit(solution)/shard_map/ppermute | solution.py:281
  94.6 2.0 %collective-permute-done.34.refs_1_ = bf16[2,128,256]{2,1,0:T(8,128)(2,1)S(1)} collective-permute-done((bf16[2,128,256]{2,1,0:T(8,128)(2,1)S(1)}, bf16[2,128,256]{2,1,0:T(8,128)(2,1)S(1)}, u32[]{:S(2)}, u32[]{:S(2)}) %collective-permute-start.34) | collective-permute-done | bytes 131104 | tf_op jit(solution)/shard_map/ppermute | solution.py:28
  96.8 2.2 %collective-permute-start.41 = (f32[8,128]{1,0:T(8,128)S(1)}, f32[8,128]{1,0:T(8,128)S(1)}, u32[]{:S(2)}, u32[]{:S(2)}) collective-permute-start(f32[8,128]{1,0:T(8,128)S(1)} %add_add_fusion.3), channel_id=1, source_target_pairs={{0,4},{1,5},{2,6},{3,7},{4,0},{5,1},{6,2},{7,3},{8,12},{9,13},{10,... | collective-permute-start | bytes 12296 | tf_op jit(solution)/shard_map/ppermute | solution.py:281
  100.6 2.1 %shard_map.91 = (f32[2,128,256]{2,1,0:T(8,128)S(1)}, bf16[2,128,256]{2,1,0:T(8,128)(2,1)S(1)}, bf16[6,256,256]{2,1,0:T(8,128)(2,1)S(1)}) custom-call(s32[8,2]{1,0:T(8,128)S(1)} %copy.18.partner_any, bf16[8,2,256,256]{3,2,1,0:T(8,128)(2,1)S(1)} %copy-done, bf16[8,2,256,256]{3,2,1,0:T(8,128)(2,1)S(1)} %copy-done.2, ...), custom_call_target="tpu_custom_call", output_to_operand_aliasing={{2}: (8, {})} | custom-call | tf_op jit(solution)/shard_map/pallas_call | solution.py:54
  102.7 1.0 collective-permute-start.43
  103.7 1.2 collective-permute-start.46
  104.9 1.6 %collective-permute-start.44 = (bf16[2,128,256]{2,1,0:T(8,128)(2,1)S(1)}, bf16[2,128,256]{2,1,0:T(8,128)(2,1)S(1)}, u32[]{:S(2)}, u32[]{:S(2)}) collective-permute-start(bf16[2,128,256]{2,1,0:T(8,128)(2,1)S(1)} %add_convert_fusion.refs_0_), channel_id=1, source_target_pairs={{0,2},{1,3},{2,0},{3,1},{4,6},{5,7},{6,4},{7,5},{8,10},{9,11},{10,... | collective-permute-start | bytes 393224 | tf_op jit(solution)/shard_map/ppermute | solution.py:41
  106.5 4.1 %collective-permute-done.44.refs_1_ = bf16[2,128,256]{2,1,0:T(8,128)(2,1)S(1)} collective-permute-done((bf16[2,128,256]{2,1,0:T(8,128)(2,1)S(1)}, bf16[2,128,256]{2,1,0:T(8,128)(2,1)S(1)}, u32[]{:S(2)}, u32[]{:S(2)}) %collective-permute-start.44) | collective-permute-done | bytes 131104 | tf_op jit(solution)/shard_map/ppermute | solution.py:41
  110.7 1.3 %collective-permute-start.52 = (bf16[2,128,256]{2,1,0:T(8,128)(2,1)S(1)}, bf16[2,128,256]{2,1,0:T(8,128)(2,1)S(1)}, u32[]{:S(2)}, u32[]{:S(2)}) collective-permute-start(bf16[2,128,256]{2,1,0:T(8,128)(2,1)S(1)} %get-tuple-element.47.refs_1_), channel_id=1, source_target_pairs={{0,4},{4,8},{8,12},{12,16},{16,20},{20,24},{24,28},{28,0},{1,5},{5... | collective-permute-start | bytes 393224 | tf_op jit(solution)/shard_map/ppermute | solution.py:28
  112.0 2.7 %collective-permute-start.48 = (f32[8,128]{1,0:T(8,128)S(1)}, f32[8,128]{1,0:T(8,128)S(1)}, u32[]{:S(2)}, u32[]{:S(2)}) collective-permute-start(f32[8,128]{1,0:T(8,128)S(1)} %get-tuple-element.45), channel_id=1, source_target_pairs={{0,24},{4,28},{8,16},{12,20},{16,8},{20,12},{24,0},{28,4},{1,25},{... | collective-permute-start | bytes 12296 | tf_op jit(solution)/shard_map/ppermute | solution.py:281
  114.7 1.7 %collective-permute-start.47 = (f32[8,128]{1,0:T(8,128)S(1)}, f32[8,128]{1,0:T(8,128)S(1)}, u32[]{:S(2)}, u32[]{:S(2)}) collective-permute-start(f32[8,128]{1,0:T(8,128)S(1)} %shard_map.93), channel_id=1, source_target_pairs={{0,8},{4,12},{8,0},{12,4},{16,24},{20,28},{24,16},{28,20},{1,9},{5... | collective-permute-start | bytes 12296 | tf_op jit(solution)/shard_map/ppermute | solution.py:281
  116.4 2.1 %collective-permute-done.52.refs_0_ = bf16[2,128,256]{2,1,0:T(8,128)(2,1)S(1)} collective-permute-done((bf16[2,128,256]{2,1,0:T(8,128)(2,1)S(1)}, bf16[2,128,256]{2,1,0:T(8,128)(2,1)S(1)}, u32[]{:S(2)}, u32[]{:S(2)}) %collective-permute-start.52) | collective-permute-done | bytes 131104 | tf_op jit(solution)/shard_map/ppermute | solution.py:28
  119.3 1.6 %collective-permute-start.50 = (f32[8,128]{1,0:T(8,128)S(1)}, f32[8,128]{1,0:T(8,128)S(1)}, u32[]{:S(2)}, u32[]{:S(2)}) collective-permute-start(f32[8,128]{1,0:T(8,128)S(1)} %add_add_fusion.1), channel_id=1, source_target_pairs={{0,4},{1,5},{2,6},{3,7},{4,0},{5,1},{6,2},{7,3},{8,12},{9,13},{10,... | collective-permute-start | bytes 12296 | tf_op jit(solution)/shard_map/ppermute | solution.py:281
  121.1 1.2 collective-permute-done.51
  122.9 2.5 %shard_map.95 = (bf16[2,256,256]{2,1,0:T(8,128)(2,1)}, bf16[8,2,256,256]{3,2,1,0:T(8,128)(2,1)}) custom-call(s32[2,128]{1,0:T(2,128)S(1)} %collective-permute-done.refs_2_.kept, f32[8,128]{1,0:T(8,128)S(1)} %add_add_fusion.sums, bf16[6,256,256]{2,1,0:T(8,128)(2,1)S(1)} %get-tuple-element.42.state, bf16[4,128,256]{2,1,0:T(8,128)(2,1)S(1)} %shard_map.94.pair, ...), custom_call_target="tpu_custom_call" | custom-call | flops 1073741824 | bytes 4194304 | tf_op jit(solution)/shard_map/pallas_call | solution.py:368
  (114 shorter events, 11.1 us)
Async XLA Ops:
  1.7 8.8 %collective-permute-start.2 = (bf16[2,128,256]{2,1,0:T(8,128)(2,1)S(1)}, bf16[2,128,256]{2,1,0:T(8,128)(2,1)S(1)}, u32[]{:S(2)}, u32[]{:S(2)}) collective-permute-start(bf16[2,128,256]{2,1,0:T(8,128)(2,1)S(1)} %get-tuple-element.49.refs_0_), channel_id=1, source_target_pairs={{0,28},{4,0},{8,4},{12,8},{16,12},{20,16},{24,20},{28,24},{1,29},{... | collective-permute-start | bytes 393224 | tf_op jit(solution)/shard_map/ppermute | solution.py:28
  7.7 7.7 %collective-permute-start.1 = (bf16[2,128,256]{2,1,0:T(8,128)(2,1)S(1)}, bf16[2,128,256]{2,1,0:T(8,128)(2,1)S(1)}, u32[]{:S(2)}, u32[]{:S(2)}) collective-permute-start(bf16[2,128,256]{2,1,0:T(8,128)(2,1)S(1)} %get-tuple-element.49.refs_0_), channel_id=1, source_target_pairs={{0,4},{4,8},{8,12},{12,16},{16,20},{20,24},{24,28},{28,0},{1,5},{5... | collective-permute-start | bytes 393224 | tf_op jit(solution)/shard_map/ppermute | solution.py:28
  15.4 1.7 %collective-permute-start.3 = (bf16[4,128,256]{2,1,0:T(8,128)(2,1)S(1)}, bf16[4,128,256]{2,1,0:T(8,128)(2,1)}, u32[]{:S(2)}, u32[]{:S(2)}) collective-permute-start(bf16[4,128,256]{2,1,0:T(8,128)(2,1)S(1)} %shard_map.79.refs_2_), channel_id=1, source_target_pairs={{0,1},{1,0},{2,3},{3,2},{4,5},{5,4},{6,7},{7,6},{8,9},{9,8},{10,11... | collective-permute-start | bytes 786440 | tf_op jit(solution)/shard_map/ppermute | solution.py:32
  15.5 17.1 %collective-permute-start.6 = (bf16[4,256,256]{2,1,0:T(8,128)(2,1)S(1)}, bf16[4,256,256]{2,1,0:T(8,128)(2,1)S(1)}, u32[]{:S(2)}, u32[]{:S(2)}) collective-permute-start(bf16[4,256,256]{2,1,0:T(8,128)(2,1)S(1)} %shard_map.77.refs_1_), channel_id=1, source_target_pairs={{0,4},{4,8},{8,12},{12,16},{16,20},{20,24},{24,28},{28,0},{1,5},{5... | collective-permute-start | bytes 1572872 | tf_op jit(solution)/shard_map/ppermute | solution.py:28
  24.2 8.4 %collective-permute-start.5 = (bf16[2,128,256]{2,1,0:T(8,128)(2,1)S(1)}, bf16[2,128,256]{2,1,0:T(8,128)(2,1)S(1)}, u32[]{:S(2)}, u32[]{:S(2)}) collective-permute-start(bf16[2,128,256]{2,1,0:T(8,128)(2,1)S(1)} %add_convert_fusion.3.refs_0_), channel_id=1, source_target_pairs={{0,2},{1,3},{2,0},{3,1},{4,6},{5,7},{6,4},{7,5},{8,10},{9,11},{10,... | collective-permute-start | bytes 393224 | tf_op jit(solution)/shard_map/ppermute | solution.py:41
  25.8 6.7 %collective-permute-start = (s32[2,128]{1,0:T(2,128)S(1)}, s32[2,128]{1,0:T(2,128)S(1)}, u32[]{:S(2)}, u32[]{:S(2)}) collective-permute-start(s32[2,128]{1,0:T(2,128)S(1)} %broadcast_in_dim.4), channel_id=1, source_target_pairs={{0,4},{4,8},{8,12},{12,16},{16,20},{20,24},{24,28},{28,0},{1,5},{5... | collective-permute-start | bytes 3080 | tf_op jit(solution)/shard_map/ppermute | solution.py:28
  32.8 6.5 %collective-permute-start.9 = (bf16[2,128,256]{2,1,0:T(8,128)(2,1)S(1)}, bf16[2,128,256]{2,1,0:T(8,128)(2,1)S(1)}, u32[]{:S(2)}, u32[]{:S(2)}) collective-permute-start(bf16[2,128,256]{2,1,0:T(8,128)(2,1)S(1)} %get-tuple-element.28.refs_0_), channel_id=1, source_target_pairs={{0,28},{4,0},{8,4},{12,8},{16,12},{20,16},{24,20},{28,24},{1,29},{... | collective-permute-start | bytes 393224 | tf_op jit(solution)/shard_map/ppermute | solution.py:28
  33.3 7.7 %collective-permute-start.8 = (bf16[2,128,256]{2,1,0:T(8,128)(2,1)S(1)}, bf16[2,128,256]{2,1,0:T(8,128)(2,1)S(1)}, u32[]{:S(2)}, u32[]{:S(2)}) collective-permute-start(bf16[2,128,256]{2,1,0:T(8,128)(2,1)S(1)} %get-tuple-element.28.refs_0_), channel_id=1, source_target_pairs={{0,4},{4,8},{8,12},{12,16},{16,20},{20,24},{24,28},{28,0},{1,5},{5... | collective-permute-start | bytes 393224 | tf_op jit(solution)/shard_map/ppermute | solution.py:28
  34.9 6.2 %collective-permute-start.13 = (f32[8,128]{1,0:T(8,128)S(1)}, f32[8,128]{1,0:T(8,128)S(1)}, u32[]{:S(2)}, u32[]{:S(2)}) collective-permute-start(f32[8,128]{1,0:T(8,128)S(1)} %get-tuple-element.29), channel_id=1, source_target_pairs={{0,24},{4,28},{8,16},{12,20},{16,8},{20,12},{24,0},{28,4},{1,25},{... | collective-permute-start | bytes 12296 | tf_op jit(solution)/shard_map/ppermute | solution.py:281
  34.9 6.2 %collective-permute-start.12 = (f32[8,128]{1,0:T(8,128)S(1)}, f32[8,128]{1,0:T(8,128)S(1)}, u32[]{:S(2)}, u32[]{:S(2)}) collective-permute-start(f32[8,128]{1,0:T(8,128)S(1)} %get-tuple-element.29), channel_id=1, source_target_pairs={{0,8},{4,12},{8,0},{12,4},{16,24},{20,28},{24,16},{28,20},{1,9},{5... | collective-permute-start | bytes 12296 | tf_op jit(solution)/shard_map/ppermute | solution.py:281
  34.9 6.2 %collective-permute-start.11 = (f32[8,128]{1,0:T(8,128)S(1)}, f32[8,128]{1,0:T(8,128)S(1)}, u32[]{:S(2)}, u32[]{:S(2)}) collective-permute-start(f32[8,128]{1,0:T(8,128)S(1)} %get-tuple-element.29), channel_id=1, source_target_pairs={{0,16},{4,20},{8,24},{12,28},{16,0},{20,4},{24,8},{28,12},{1,17},{... | collective-permute-start | bytes 12296 | tf_op jit(solution)/shard_map/ppermute | solution.py:281
  41.0 5.3 %collective-permute-start.10 = (bf16[4,128,256]{2,1,0:T(8,128)(2,1)S(1)}, bf16[4,128,256]{2,1,0:T(8,128)(2,1)S(1)}, u32[]{:S(2)}, u32[]{:S(2)}) collective-permute-start(bf16[4,128,256]{2,1,0:T(8,128)(2,1)S(1)} %shard_map.82.refs_2_), channel_id=1, source_target_pairs={{0,1},{1,0},{2,3},{3,2},{4,5},{5,4},{6,7},{7,6},{8,9},{9,8},{10,11... | collective-permute-start | bytes 786440 | tf_op jit(solution)/shard_map/ppermute | solution.py:32
  41.1 3.8 %collective-permute-start.16 = (f32[8,128]{1,0:T(8,128)S(1)}, f32[8,128]{1,0:T(8,128)S(1)}, u32[]{:S(2)}, u32[]{:S(2)}) collective-permute-start(f32[8,128]{1,0:T(8,128)S(1)} %add_add_fusion.7), channel_id=1, source_target_pairs={{0,5},{1,4},{2,7},{3,6},{4,1},{5,0},{6,3},{7,2},{8,13},{9,12},{10,... | collective-permute-start | bytes 12296 | tf_op jit(solution)/shard_map/ppermute | solution.py:281
  41.2 3.8 %collective-permute-start.15 = (f32[8,128]{1,0:T(8,128)S(1)}, f32[8,128]{1,0:T(8,128)S(1)}, u32[]{:S(2)}, u32[]{:S(2)}) collective-permute-start(f32[8,128]{1,0:T(8,128)S(1)} %add_add_fusion.7), channel_id=1, source_target_pairs={{0,4},{1,5},{2,6},{3,7},{4,0},{5,1},{6,2},{7,3},{8,12},{9,13},{10,... | collective-permute-start | bytes 12296 | tf_op jit(solution)/shard_map/ppermute | solution.py:281
  43.3 1.6 %collective-permute-start.14 = (f32[8,128]{1,0:T(8,128)S(1)}, f32[8,128]{1,0:T(8,128)S(1)}, u32[]{:S(2)}, u32[]{:S(2)}) collective-permute-start(f32[8,128]{1,0:T(8,128)S(1)} %add_add_fusion.7), channel_id=1, source_target_pairs={{0,1},{1,0},{2,3},{3,2},{4,5},{5,4},{6,7},{7,6},{8,9},{9,8},{10,11... | collective-permute-start | bytes 12296 | tf_op jit(solution)/shard_map/ppermute | solution.py:281
  43.3 19.9 %collective-permute-start.24 = (bf16[5,256,256]{2,1,0:T(8,128)(2,1)S(1)}, bf16[5,256,256]{2,1,0:T(8,128)(2,1)S(1)}, u32[]{:S(2)}, u32[]{:S(2)}) collective-permute-start(bf16[5,256,256]{2,1,0:T(8,128)(2,1)S(1)} %get-tuple-element.35), channel_id=1, source_target_pairs={{0,4},{4,8},{8,12},{12,16},{16,20},{20,24},{24,28},{28,0},{1,5},{5... | collective-permute-start | bytes 1966088 | tf_op jit(solution)/shard_map/ppermute | solution.py:28
  49.8 5.6 %collective-permute-start.18 = (bf16[2,128,256]{2,1,0:T(8,128)(2,1)S(1)}, bf16[2,128,256]{2,1,0:T(8,128)(2,1)S(1)}, u32[]{:S(2)}, u32[]{:S(2)}) collective-permute-start(bf16[2,128,256]{2,1,0:T(8,128)(2,1)S(1)} %add_convert_fusion.2.refs_0_), channel_id=1, source_target_pairs={{0,2},{1,3},{2,0},{3,1},{4,6},{5,7},{6,4},{7,5},{8,10},{9,11},{10,... | collective-permute-start | bytes 393224 | tf_op jit(solution)/shard_map/ppermute | solution.py:41
  55.6 13.2 %collective-permute-start.21 = (bf16[2,128,256]{2,1,0:T(8,128)(2,1)S(1)}, bf16[2,128,256]{2,1,0:T(8,128)(2,1)S(1)}, u32[]{:S(2)}, u32[]{:S(2)}) collective-permute-start(bf16[2,128,256]{2,1,0:T(8,128)(2,1)S(1)} %get-tuple-element.33.refs_0_), channel_id=1, source_target_pairs={{0,28},{4,0},{8,4},{12,8},{16,12},{20,16},{24,20},{28,24},{1,29},{... | collective-permute-start | bytes 393224 | tf_op jit(solution)/shard_map/ppermute | solution.py:28
  58.9 9.9 %collective-permute-start.20 = (bf16[2,128,256]{2,1,0:T(8,128)(2,1)S(1)}, bf16[2,128,256]{2,1,0:T(8,128)(2,1)S(1)}, u32[]{:S(2)}, u32[]{:S(2)}) collective-permute-start(bf16[2,128,256]{2,1,0:T(8,128)(2,1)S(1)} %get-tuple-element.33.refs_0_), channel_id=1, source_target_pairs={{0,4},{4,8},{8,12},{12,16},{16,20},{20,24},{24,28},{28,0},{1,5},{5... | collective-permute-start | bytes 393224 | tf_op jit(solution)/shard_map/ppermute | solution.py:28
  58.9 10.0 %collective-permute-start.26 = (f32[8,128]{1,0:T(8,128)S(1)}, f32[8,128]{1,0:T(8,128)S(1)}, u32[]{:S(2)}, u32[]{:S(2)}) collective-permute-start(f32[8,128]{1,0:T(8,128)S(1)} %get-tuple-element.34), channel_id=1, source_target_pairs={{0,24},{4,28},{8,16},{12,20},{16,8},{20,12},{24,0},{28,4},{1,25},{... | collective-permute-start | bytes 12296 | tf_op jit(solution)/shard_map/ppermute | solution.py:281
  59.5 9.4 %collective-permute-start.23 = (f32[8,128]{1,0:T(8,128)S(1)}, f32[8,128]{1,0:T(8,128)S(1)}, u32[]{:S(2)}, u32[]{:S(2)}) collective-permute-start(f32[8,128]{1,0:T(8,128)S(1)} %get-tuple-element.34), channel_id=1, source_target_pairs={{0,16},{4,20},{8,24},{12,28},{16,0},{20,4},{24,8},{28,12},{1,17},{... | collective-permute-start | bytes 12296 | tf_op jit(solution)/shard_map/ppermute | solution.py:281
  63.3 5.6 %collective-permute-start.25 = (f32[8,128]{1,0:T(8,128)S(1)}, f32[8,128]{1,0:T(8,128)S(1)}, u32[]{:S(2)}, u32[]{:S(2)}) collective-permute-start(f32[8,128]{1,0:T(8,128)S(1)} %shard_map.86), channel_id=1, source_target_pairs={{0,8},{4,12},{8,0},{12,4},{16,24},{20,28},{24,16},{28,20},{1,9},{5... | collective-permute-start | bytes 12296 | tf_op jit(solution)/shard_map/ppermute | solution.py:281
  68.8 4.7 %collective-permute-start.22 = (bf16[4,128,256]{2,1,0:T(8,128)(2,1)S(1)}, bf16[4,128,256]{2,1,0:T(8,128)(2,1)S(1)}, u32[]{:S(2)}, u32[]{:S(2)}) collective-permute-start(bf16[4,128,256]{2,1,0:T(8,128)(2,1)S(1)} %shard_map.85.refs_2_), channel_id=1, source_target_pairs={{0,1},{1,0},{2,3},{3,2},{4,5},{5,4},{6,7},{7,6},{8,9},{9,8},{10,11... | collective-permute-start | bytes 786440 | tf_op jit(solution)/shard_map/ppermute | solution.py:32
  69.0 3.1 %collective-permute-start.29 = (f32[8,128]{1,0:T(8,128)S(1)}, f32[8,128]{1,0:T(8,128)S(1)}, u32[]{:S(2)}, u32[]{:S(2)}) collective-permute-start(f32[8,128]{1,0:T(8,128)S(1)} %add_add_fusion.5), channel_id=1, source_target_pairs={{0,5},{1,4},{2,7},{3,6},{4,1},{5,0},{6,3},{7,2},{8,13},{9,12},{10,... | collective-permute-start | bytes 12296 | tf_op jit(solution)/shard_map/ppermute | solution.py:281
  69.0 3.8 %collective-permute-start.28 = (f32[8,128]{1,0:T(8,128)S(1)}, f32[8,128]{1,0:T(8,128)S(1)}, u32[]{:S(2)}, u32[]{:S(2)}) collective-permute-start(f32[8,128]{1,0:T(8,128)S(1)} %add_add_fusion.5), channel_id=1, source_target_pairs={{0,4},{1,5},{2,6},{3,7},{4,0},{5,1},{6,2},{7,3},{8,12},{9,13},{10,... | collective-permute-start | bytes 12296 | tf_op jit(solution)/shard_map/ppermute | solution.py:281
  71.2 1.6 %collective-permute-start.27 = (f32[8,128]{1,0:T(8,128)S(1)}, f32[8,128]{1,0:T(8,128)S(1)}, u32[]{:S(2)}, u32[]{:S(2)}) collective-permute-start(f32[8,128]{1,0:T(8,128)S(1)} %add_add_fusion.5), channel_id=1, source_target_pairs={{0,1},{1,0},{2,3},{3,2},{4,5},{5,4},{6,7},{7,6},{8,9},{9,8},{10,11... | collective-permute-start | bytes 12296 | tf_op jit(solution)/shard_map/ppermute | solution.py:281
  71.2 19.9 %collective-permute-start.37 = (bf16[5,256,256]{2,1,0:T(8,128)(2,1)S(1)}, bf16[5,256,256]{2,1,0:T(8,128)(2,1)S(1)}, u32[]{:S(2)}, u32[]{:S(2)}) collective-permute-start(bf16[5,256,256]{2,1,0:T(8,128)(2,1)S(1)} %get-tuple-element.41), channel_id=1, source_target_pairs={{0,4},{4,8},{8,12},{12,16},{16,20},{20,24},{24,28},{28,0},{1,5},{5... | collective-permute-start | bytes 1966088 | tf_op jit(solution)/shard_map/ppermute | solution.py:28
  77.1 5.8 %collective-permute-start.31 = (bf16[2,128,256]{2,1,0:T(8,128)(2,1)S(1)}, bf16[2,128,256]{2,1,0:T(8,128)(2,1)S(1)}, u32[]{:S(2)}, u32[]{:S(2)}) collective-permute-start(bf16[2,128,256]{2,1,0:T(8,128)(2,1)S(1)} %add_convert_fusion.1.refs_0_), channel_id=1, source_target_pairs={{0,2},{1,3},{2,0},{3,1},{4,6},{5,7},{6,4},{7,5},{8,10},{9,11},{10,... | collective-permute-start | bytes 393224 | tf_op jit(solution)/shard_map/ppermute | solution.py:41
  83.1 13.6 %collective-permute-start.34 = (bf16[2,128,256]{2,1,0:T(8,128)(2,1)S(1)}, bf16[2,128,256]{2,1,0:T(8,128)(2,1)S(1)}, u32[]{:S(2)}, u32[]{:S(2)}) collective-permute-start(bf16[2,128,256]{2,1,0:T(8,128)(2,1)S(1)} %get-tuple-element.39.refs_0_), channel_id=1, source_target_pairs={{0,28},{4,0},{8,4},{12,8},{16,12},{20,16},{24,20},{28,24},{1,29},{... | collective-permute-start | bytes 393224 | tf_op jit(solution)/shard_map/ppermute | solution.py:28
  86.7 9.9 %collective-permute-start.33 = (bf16[2,128,256]{2,1,0:T(8,128)(2,1)S(1)}, bf16[2,128,256]{2,1,0:T(8,128)(2,1)S(1)}, u32[]{:S(2)}, u32[]{:S(2)}) collective-permute-start(bf16[2,128,256]{2,1,0:T(8,128)(2,1)S(1)} %get-tuple-element.39.refs_0_), channel_id=1, source_target_pairs={{0,4},{4,8},{8,12},{12,16},{16,20},{20,24},{24,28},{28,0},{1,5},{5... | collective-permute-start | bytes 393224 | tf_op jit(solution)/shard_map/ppermute | solution.py:28
  91.1 5.6 %collective-permute-start.38 = (f32[8,128]{1,0:T(8,128)S(1)}, f32[8,128]{1,0:T(8,128)S(1)}, u32[]{:S(2)}, u32[]{:S(2)}) collective-permute-start(f32[8,128]{1,0:T(8,128)S(1)} %shard_map.90), channel_id=1, source_target_pairs={{0,8},{4,12},{8,0},{12,4},{16,24},{20,28},{24,16},{28,20},{1,9},{5... | collective-permute-start | bytes 12296 | tf_op jit(solution)/shard_map/ppermute | solution.py:281
  91.1 5.6 %collective-permute-start.39 = (f32[8,128]{1,0:T(8,128)S(1)}, f32[8,128]{1,0:T(8,128)S(1)}, u32[]{:S(2)}, u32[]{:S(2)}) collective-permute-start(f32[8,128]{1,0:T(8,128)S(1)} %get-tuple-element.40), channel_id=1, source_target_pairs={{0,24},{4,28},{8,16},{12,20},{16,8},{20,12},{24,0},{28,4},{1,25},{... | collective-permute-start | bytes 12296 | tf_op jit(solution)/shard_map/ppermute | solution.py:281
  91.9 4.8 %collective-permute-start.36 = (f32[8,128]{1,0:T(8,128)S(1)}, f32[8,128]{1,0:T(8,128)S(1)}, u32[]{:S(2)}, u32[]{:S(2)}) collective-permute-start(f32[8,128]{1,0:T(8,128)S(1)} %get-tuple-element.40), channel_id=1, source_target_pairs={{0,16},{4,20},{8,24},{12,28},{16,0},{20,4},{24,8},{28,12},{1,17},{... | collective-permute-start | bytes 12296 | tf_op jit(solution)/shard_map/ppermute | solution.py:281
  96.6 4.0 %collective-permute-start.35 = (bf16[4,128,256]{2,1,0:T(8,128)(2,1)S(1)}, bf16[4,128,256]{2,1,0:T(8,128)(2,1)S(1)}, u32[]{:S(2)}, u32[]{:S(2)}) collective-permute-start(bf16[4,128,256]{2,1,0:T(8,128)(2,1)S(1)} %shard_map.89.refs_2_), channel_id=1, source_target_pairs={{0,1},{1,0},{2,3},{3,2},{4,5},{5,4},{6,7},{7,6},{8,9},{9,8},{10,11... | collective-permute-start | bytes 786440 | tf_op jit(solution)/shard_map/ppermute | solution.py:32
  96.8 3.1 %collective-permute-start.42 = (f32[8,128]{1,0:T(8,128)S(1)}, f32[8,128]{1,0:T(8,128)S(1)}, u32[]{:S(2)}, u32[]{:S(2)}) collective-permute-start(f32[8,128]{1,0:T(8,128)S(1)} %add_add_fusion.3), channel_id=1, source_target_pairs={{0,5},{1,4},{2,7},{3,6},{4,1},{5,0},{6,3},{7,2},{8,13},{9,12},{10,... | collective-permute-start | bytes 12296 | tf_op jit(solution)/shard_map/ppermute | solution.py:281
  96.8 3.8 %collective-permute-start.41 = (f32[8,128]{1,0:T(8,128)S(1)}, f32[8,128]{1,0:T(8,128)S(1)}, u32[]{:S(2)}, u32[]{:S(2)}) collective-permute-start(f32[8,128]{1,0:T(8,128)S(1)} %add_add_fusion.3), channel_id=1, source_target_pairs={{0,4},{1,5},{2,6},{3,7},{4,0},{5,1},{6,2},{7,3},{8,12},{9,13},{10,... | collective-permute-start | bytes 12296 | tf_op jit(solution)/shard_map/ppermute | solution.py:281
  99.0 1.6 %collective-permute-start.40 = (f32[8,128]{1,0:T(8,128)S(1)}, f32[8,128]{1,0:T(8,128)S(1)}, u32[]{:S(2)}, u32[]{:S(2)}) collective-permute-start(f32[8,128]{1,0:T(8,128)S(1)} %add_add_fusion.3), channel_id=1, source_target_pairs={{0,1},{1,0},{2,3},{3,2},{4,5},{5,4},{6,7},{7,6},{8,9},{9,8},{10,11... | collective-permute-start | bytes 12296 | tf_op jit(solution)/shard_map/ppermute | solution.py:281
  102.7 2.2 %collective-permute-start.43 = (bf16[2,128,256]{2,1,0:T(8,128)(2,1)S(1)}, bf16[2,128,256]{2,1,0:T(8,128)(2,1)S(1)}, u32[]{:S(2)}, u32[]{:S(2)}) collective-permute-start(bf16[2,128,256]{2,1,0:T(8,128)(2,1)S(1)} %get-tuple-element.44), channel_id=1, source_target_pairs={{0,1},{1,0},{2,3},{3,2},{4,5},{5,4},{6,7},{7,6},{8,9},{9,8},{10,11... | collective-permute-start | bytes 393224 | tf_op jit(solution)/shard_map/ppermute | solution.py:32
  103.7 11.0 %collective-permute-start.46 = (bf16[2,256,256]{2,1,0:T(8,128)(2,1)S(1)}, bf16[2,256,256]{2,1,0:T(8,128)(2,1)S(1)}, u32[]{:S(2)}, u32[]{:S(2)}) collective-permute-start(bf16[2,256,256]{2,1,0:T(8,128)(2,1)S(1)} %get-tuple-element.46), channel_id=1, source_target_pairs={{0,4},{4,8},{8,12},{12,16},{16,20},{20,24},{24,28},{28,0},{1,5},{5... | collective-permute-start | bytes 786440 | tf_op jit(solution)/shard_map/ppermute | solution.py:28
  104.9 5.7 %collective-permute-start.44 = (bf16[2,128,256]{2,1,0:T(8,128)(2,1)S(1)}, bf16[2,128,256]{2,1,0:T(8,128)(2,1)S(1)}, u32[]{:S(2)}, u32[]{:S(2)}) collective-permute-start(bf16[2,128,256]{2,1,0:T(8,128)(2,1)S(1)} %add_convert_fusion.refs_0_), channel_id=1, source_target_pairs={{0,2},{1,3},{2,0},{3,1},{4,6},{5,7},{6,4},{7,5},{8,10},{9,11},{10,... | collective-permute-start | bytes 393224 | tf_op jit(solution)/shard_map/ppermute | solution.py:41
  110.7 7.8 %collective-permute-start.52 = (bf16[2,128,256]{2,1,0:T(8,128)(2,1)S(1)}, bf16[2,128,256]{2,1,0:T(8,128)(2,1)S(1)}, u32[]{:S(2)}, u32[]{:S(2)}) collective-permute-start(bf16[2,128,256]{2,1,0:T(8,128)(2,1)S(1)} %get-tuple-element.47.refs_1_), channel_id=1, source_target_pairs={{0,4},{4,8},{8,12},{12,16},{16,20},{20,24},{24,28},{28,0},{1,5},{5... | collective-permute-start | bytes 393224 | tf_op jit(solution)/shard_map/ppermute | solution.py:28
  112.0 6.6 %collective-permute-start.48 = (f32[8,128]{1,0:T(8,128)S(1)}, f32[8,128]{1,0:T(8,128)S(1)}, u32[]{:S(2)}, u32[]{:S(2)}) collective-permute-start(f32[8,128]{1,0:T(8,128)S(1)} %get-tuple-element.45), channel_id=1, source_target_pairs={{0,24},{4,28},{8,16},{12,20},{16,8},{20,12},{24,0},{28,4},{1,25},{... | collective-permute-start | bytes 12296 | tf_op jit(solution)/shard_map/ppermute | solution.py:281
  114.7 4.5 %collective-permute-start.45 = (f32[8,128]{1,0:T(8,128)S(1)}, f32[8,128]{1,0:T(8,128)S(1)}, u32[]{:S(2)}, u32[]{:S(2)}) collective-permute-start(f32[8,128]{1,0:T(8,128)S(1)} %get-tuple-element.45), channel_id=1, source_target_pairs={{0,16},{4,20},{8,24},{12,28},{16,0},{20,4},{24,8},{28,12},{1,17},{... | collective-permute-start | bytes 12296 | tf_op jit(solution)/shard_map/ppermute | solution.py:281
  114.7 4.5 %collective-permute-start.47 = (f32[8,128]{1,0:T(8,128)S(1)}, f32[8,128]{1,0:T(8,128)S(1)}, u32[]{:S(2)}, u32[]{:S(2)}) collective-permute-start(f32[8,128]{1,0:T(8,128)S(1)} %shard_map.93), channel_id=1, source_target_pairs={{0,8},{4,12},{8,0},{12,4},{16,24},{20,28},{24,16},{28,20},{1,9},{5... | collective-permute-start | bytes 12296 | tf_op jit(solution)/shard_map/ppermute | solution.py:281
  118.5 4.4 %collective-permute-start.53 = (bf16[4,128,256]{2,1,0:T(8,128)(2,1)S(1)}, bf16[4,128,256]{2,1,0:T(8,128)(2,1)S(1)}, u32[]{:S(2)}, u32[]{:S(2)}) collective-permute-start(bf16[4,128,256]{2,1,0:T(8,128)(2,1)S(1)} %shard_map.94.pair), channel_id=1, source_target_pairs={{0,1},{1,0},{2,3},{3,2},{4,5},{5,4},{6,7},{7,6},{8,9},{9,8},{10,11... | collective-permute-start | bytes 786440 | tf_op jit(solution)/shard_map/ppermute | solution.py:32
  119.2 3.1 %collective-permute-start.51 = (f32[8,128]{1,0:T(8,128)S(1)}, f32[8,128]{1,0:T(8,128)S(1)}, u32[]{:S(2)}, u32[]{:S(2)}) collective-permute-start(f32[8,128]{1,0:T(8,128)S(1)} %add_add_fusion.1), channel_id=1, source_target_pairs={{0,5},{1,4},{2,7},{3,6},{4,1},{5,0},{6,3},{7,2},{8,13},{9,12},{10,... | collective-permute-start | bytes 12296 | tf_op jit(solution)/shard_map/ppermute | solution.py:281
  119.3 3.7 %collective-permute-start.50 = (f32[8,128]{1,0:T(8,128)S(1)}, f32[8,128]{1,0:T(8,128)S(1)}, u32[]{:S(2)}, u32[]{:S(2)}) collective-permute-start(f32[8,128]{1,0:T(8,128)S(1)} %add_add_fusion.1), channel_id=1, source_target_pairs={{0,4},{1,5},{2,6},{3,7},{4,0},{5,1},{6,2},{7,3},{8,12},{9,13},{10,... | collective-permute-start | bytes 12296 | tf_op jit(solution)/shard_map/ppermute | solution.py:281
  120.8 2.1 %collective-permute-start.49 = (f32[8,128]{1,0:T(8,128)S(1)}, f32[8,128]{1,0:T(8,128)S(1)}, u32[]{:S(2)}, u32[]{:S(2)}) collective-permute-start(f32[8,128]{1,0:T(8,128)S(1)} %add_add_fusion.1), channel_id=1, source_target_pairs={{0,1},{1,0},{2,3},{3,2},{4,5},{5,4},{6,7},{7,6},{8,9},{9,8},{10,11... | collective-permute-start | bytes 12296 | tf_op jit(solution)/shard_map/ppermute | solution.py:281
  (14 other events, 92.0 us)

commit v6 on v5

--- a/solution.py
+++ b/solution.py
@@ -355,9 +355,12 @@
             (shifts, state, *parts, *gates),
             [VMEM] * (2 + len(parts)) + [ANY] * len(gates),
         )
+        if iteration < ITERS - 1:
+            own_other = core_swap(own)
+            if iteration:
+                late = late + [own_other]
         sums = far_sums(sums, late)
         if iteration < ITERS - 1:
-            own_other = core_swap(own)
             pair = pack(sec_move(own, 1), sec_move(own, -1))
             if blocks:
                 pieces.append(sec_move(blocks[0], 1))

time: 126 us -> 125 us (level)
  starting transfers between devices: 53.6 us -> 51.8 us
    ppermute x14, waiting for transfers between devices: 29.6 us -> 31.5 us  [sec_move(): lax.ppermute(x, 'sec', [(i, (i + distance) % count) for i in range(count)])]
    ppermute x12, starting transfers between devices: 3.21 us -> 1.35 us  [core_swap(): lax.ppermute(x, 'op', [(i, i ^ 1) for i in range(lax.axis_size('op'))])]
    ppermute x14, starting transfers between devices: 19.2 us -> 20.6 us  [sec_move(): lax.ppermute(x, 'sec', [(i, (i + distance) % count) for i in range(count)])]
    ppermute x24, starting transfers between devices: 24.7 us -> 23.5 us  [other(): return lax.ppermute(sent, axes, [(i, i ^ mask) for i in range(size)])]
  transfers between devices with their start and end apart: 54 -> 54, of which waited for: 25 -> 23; matrix products, arithmetic and copies ran while one was open for 0% -> 0% of each run, Pallas kernels for 7% -> 7%
where the time goes in v6:
time: 125 us
  waiting for transfers between devices  54.5 us (44%)
  starting transfers between devices  51.8 us (41%)
  Pallas kernels  13.6 us (11%)
  local copies, waits for them, and re-layouts  3.75 us (3%)
    ppermute x14, waiting for transfers between devices, sec_move(): lax.ppermute(x, 'sec', [(i, (i + distance) % count) for i in range(count)])  31.5 us
    ppermute x24, starting transfers between devices, other(): return lax.ppermute(sent, axes, [(i, i ^ mask) for i in range(size)])  23.5 us
    ppermute x14, starting transfers between devices, sec_move(): lax.ppermute(x, 'sec', [(i, (i + distance) % count) for i in range(count)])  20.6 us
    ppermute x4, waiting for transfers between devices, chip_parts(): parts.append(lax.ppermute(x, 'op', route))  12.1 us
    pallas_call x18, Pallas kernels, call(): pl.pallas_call(kernel, out_shape=tuple(outs), in_specs=specs, out_specs=t...  11 us
    ppermute x12, waiting for transfers between devices, core_swap(): lax.ppermute(x, 'op', [(i, i ^ 1) for i in range(lax.axis_size('op'))])  6.55 us
    ppermute x4, starting transfers between devices, chip_parts(): parts.append(lax.ppermute(x, 'op', route))  6.34 us
    ppermute x24, waiting for transfers between devices, other(): return lax.ppermute(sent, axes, [(i, i ^ mask) for i in range(size)])  4.35 us
  transfers between devices with their start and end apart: 54, of which 23 were waited for; matrix products, arithmetic and copies ran while one was open for 0% of the time, Pallas kernels for 7%

profile of v6, /device:TPU:0, one launch (start us, length us, event | category | flops | bytes accessed | tf_op | source)
XLA Modules:
  0.0 124.9 jit_solution(13284113659217980029)
XLA Ops:
  0.6 1.0 constant_dynamic-slice_fusion
  1.7 6.0 %collective-permute-start.2 = (bf16[2,128,256]{2,1,0:T(8,128)(2,1)S(1)}, bf16[2,128,256]{2,1,0:T(8,128)(2,1)S(1)}, u32[]{:S(2)}, u32[]{:S(2)}) collective-permute-start(bf16[2,128,256]{2,1,0:T(8,128)(2,1)S(1)} %get-tuple-element.49.refs_0_), channel_id=1, source_target_pairs={{0,28},{4,0},{8,4},{12,8},{16,12},{20,16},{24,20},{28,24},{1,29},{... | collective-permute-start | bytes 393224 | tf_op jit(solution)/shard_map/ppermute | solution.py:28
  7.7 1.1 shard_map.77.refs_1_
  8.9 1.6 %collective-permute-done.2.refs_0_ = bf16[2,128,256]{2,1,0:T(8,128)(2,1)S(1)} collective-permute-done((bf16[2,128,256]{2,1,0:T(8,128)(2,1)S(1)}, bf16[2,128,256]{2,1,0:T(8,128)(2,1)S(1)}, u32[]{:S(2)}, u32[]{:S(2)}) %collective-permute-start.2) | collective-permute-done | bytes 131104 | tf_op jit(solution)/shard_map/ppermute | solution.py:28
  10.5 4.9 %collective-permute-done.1.refs_0_ = bf16[2,128,256]{2,1,0:T(8,128)(2,1)S(1)} collective-permute-done((bf16[2,128,256]{2,1,0:T(8,128)(2,1)S(1)}, bf16[2,128,256]{2,1,0:T(8,128)(2,1)S(1)}, u32[]{:S(2)}, u32[]{:S(2)}) %collective-permute-start.1) | collective-permute-done | bytes 131104 | tf_op jit(solution)/shard_map/ppermute | solution.py:28
  15.6 1.5 %collective-permute-done.3.refs_3_ = bf16[4,128,256]{2,1,0:T(8,128)(2,1)} collective-permute-done((bf16[4,128,256]{2,1,0:T(8,128)(2,1)S(1)}, bf16[4,128,256]{2,1,0:T(8,128)(2,1)}, u32[]{:S(2)}, u32[]{:S(2)}) %collective-permute-start.3) | collective-permute-done | bytes 262176 | tf_op jit(solution)/shard_map/ppermute | solution.py:32
  17.1 1.6 %copy-done.1 = bf16[8,2,256,256]{3,2,1,0:T(8,128)(2,1)S(1)} copy-done((bf16[8,2,256,256]{3,2,1,0:T(8,128)(2,1)S(1)}, bf16[8,2,256,256]{3,2,1,0:T(8,128)(2,1)}, u32[]{:S(2)}) %copy-start.1) | copy-done | bytes 2097176
  18.7 0.9 copy-done.4
  19.6 3.1 %shard_map.80 = (f32[2,128,256]{2,1,0:T(8,128)S(1)}, bf16[2,128,256]{2,1,0:T(8,128)(2,1)S(1)}, bf16[6,256,256]{2,1,0:T(8,128)(2,1)S(1)}, bf16[5,256,256]{2,1,0:T(8,128)(2,1)S(1)}) custom-call(s32[8,2]{1,0:T(8,128)S(1)} %copy.18.partner_any, bf16[8,2,256,256]{3,2,1,0:T(8,128)(2,1)S(1)} %copy-done, bf16[8,2,256,256]{3,2,1,0:T(8,128)(2,1)S(1)} %copy-done.1, ...), custom_call_target="tpu_custom_call" | custom-call | tf_op jit(solution)/shard_map/pallas_call | solution.py:54
  22.9 1.2 collective-permute-done.4
  24.2 1.6 %collective-permute-start.5 = (bf16[2,128,256]{2,1,0:T(8,128)(2,1)S(1)}, bf16[2,128,256]{2,1,0:T(8,128)(2,1)S(1)}, u32[]{:S(2)}, u32[]{:S(2)}) collective-permute-start(bf16[2,128,256]{2,1,0:T(8,128)(2,1)S(1)} %add_convert_fusion.3.refs_0_), channel_id=1, source_target_pairs={{0,2},{1,3},{2,0},{3,1},{4,6},{5,7},{6,4},{7,5},{8,10},{9,11},{10,... | collective-permute-start | bytes 393224 | tf_op jit(solution)/shard_map/ppermute | solution.py:41
  25.8 6.7 %collective-permute-done.refs_2_.kept = s32[2,128]{1,0:T(2,128)S(1)} collective-permute-done((s32[2,128]{1,0:T(2,128)S(1)}, s32[2,128]{1,0:T(2,128)S(1)}, u32[]{:S(2)}, u32[]{:S(2)}) %collective-permute-start) | collective-permute-done | bytes 1056 | tf_op jit(solution)/shard_map/ppermute | solution.py:28
  33.3 1.6 %collective-permute-start.8 = (bf16[2,128,256]{2,1,0:T(8,128)(2,1)S(1)}, bf16[2,128,256]{2,1,0:T(8,128)(2,1)S(1)}, u32[]{:S(2)}, u32[]{:S(2)}) collective-permute-start(bf16[2,128,256]{2,1,0:T(8,128)(2,1)S(1)} %get-tuple-element.28.refs_0_), channel_id=1, source_target_pairs={{0,4},{4,8},{8,12},{12,16},{16,20},{20,24},{24,28},{28,0},{1,5},{5... | collective-permute-start | bytes 393224 | tf_op jit(solution)/shard_map/ppermute | solution.py:28
  34.9 4.4 %collective-permute-start.11 = (f32[8,128]{1,0:T(8,128)S(1)}, f32[8,128]{1,0:T(8,128)S(1)}, u32[]{:S(2)}, u32[]{:S(2)}) collective-permute-start(f32[8,128]{1,0:T(8,128)S(1)} %get-tuple-element.29), channel_id=1, source_target_pairs={{0,16},{4,20},{8,24},{12,28},{16,0},{20,4},{24,8},{28,12},{1,17},{... | collective-permute-start | bytes 12296 | tf_op jit(solution)/shard_map/ppermute | solution.py:281
  39.3 1.7 %collective-permute-done.8.refs_0_ = bf16[2,128,256]{2,1,0:T(8,128)(2,1)S(1)} collective-permute-done((bf16[2,128,256]{2,1,0:T(8,128)(2,1)S(1)}, bf16[2,128,256]{2,1,0:T(8,128)(2,1)S(1)}, u32[]{:S(2)}, u32[]{:S(2)}) %collective-permute-start.8) | collective-permute-done | bytes 131104 | tf_op jit(solution)/shard_map/ppermute | solution.py:28
  41.2 2.1 %collective-permute-start.15 = (f32[8,128]{1,0:T(8,128)S(1)}, f32[8,128]{1,0:T(8,128)S(1)}, u32[]{:S(2)}, u32[]{:S(2)}) collective-permute-start(f32[8,128]{1,0:T(8,128)S(1)} %add_add_fusion.7), channel_id=1, source_target_pairs={{0,4},{1,5},{2,6},{3,7},{4,0},{5,1},{6,2},{7,3},{8,12},{9,13},{10,... | collective-permute-start | bytes 12296 | tf_op jit(solution)/shard_map/ppermute | solution.py:281
  43.3 1.6 %collective-permute-start.24 = (bf16[5,256,256]{2,1,0:T(8,128)(2,1)S(1)}, bf16[5,256,256]{2,1,0:T(8,128)(2,1)S(1)}, u32[]{:S(2)}, u32[]{:S(2)}) collective-permute-start(bf16[5,256,256]{2,1,0:T(8,128)(2,1)S(1)} %get-tuple-element.35), channel_id=1, source_target_pairs={{0,4},{4,8},{8,12},{12,16},{16,20},{20,24},{24,28},{28,0},{1,5},{5... | collective-permute-start | bytes 1966088 | tf_op jit(solution)/shard_map/ppermute | solution.py:28
  45.0 1.3 %collective-permute-done.7.refs_1_ = bf16[2,128,256]{2,1,0:T(8,128)(2,1)S(1)} collective-permute-done((bf16[2,128,256]{2,1,0:T(8,128)(2,1)S(1)}, bf16[2,128,256]{2,1,0:T(8,128)(2,1)S(1)}, u32[]{:S(2)}, u32[]{:S(2)}) %collective-permute-start.7) | collective-permute-done | bytes 131104 | tf_op jit(solution)/shard_map/ppermute | solution.py:32
  46.3 2.1 %shard_map.83 = (f32[2,128,256]{2,1,0:T(8,128)S(1)}, bf16[2,128,256]{2,1,0:T(8,128)(2,1)S(1)}, bf16[6,256,256]{2,1,0:T(8,128)(2,1)S(1)}, bf16[5,256,256]{2,1,0:T(8,128)(2,1)S(1)}) custom-call(s32[8,2]{1,0:T(8,128)S(1)} %copy.18.partner_any, bf16[8,2,256,256]{3,2,1,0:T(8,128)(2,1)S(1)} %copy-done, ...), custom_call_target="tpu_custom_call", output_to_operand_aliasing={{2}: (8, {})} | custom-call | tf_op jit(solution)/shard_map/pallas_call | solution.py:54
  48.6 1.2 collective-permute-done.17
  49.8 1.6 %collective-permute-start.18 = (bf16[2,128,256]{2,1,0:T(8,128)(2,1)S(1)}, bf16[2,128,256]{2,1,0:T(8,128)(2,1)S(1)}, u32[]{:S(2)}, u32[]{:S(2)}) collective-permute-start(bf16[2,128,256]{2,1,0:T(8,128)(2,1)S(1)} %add_convert_fusion.2.refs_0_), channel_id=1, source_target_pairs={{0,2},{1,3},{2,0},{3,1},{4,6},{5,7},{6,4},{7,5},{8,10},{9,11},{10,... | collective-permute-start | bytes 393224 | tf_op jit(solution)/shard_map/ppermute | solution.py:41
  51.4 4.0 %collective-permute-done.18.refs_1_ = bf16[2,128,256]{2,1,0:T(8,128)(2,1)S(1)} collective-permute-done((bf16[2,128,256]{2,1,0:T(8,128)(2,1)S(1)}, bf16[2,128,256]{2,1,0:T(8,128)(2,1)S(1)}, u32[]{:S(2)}, u32[]{:S(2)}) %collective-permute-start.18) | collective-permute-done | bytes 131104 | tf_op jit(solution)/shard_map/ppermute | solution.py:41
  55.7 3.3 %collective-permute-start.21 = (bf16[2,128,256]{2,1,0:T(8,128)(2,1)S(1)}, bf16[2,128,256]{2,1,0:T(8,128)(2,1)S(1)}, u32[]{:S(2)}, u32[]{:S(2)}) collective-permute-start(bf16[2,128,256]{2,1,0:T(8,128)(2,1)S(1)} %get-tuple-element.33.refs_0_), channel_id=1, source_target_pairs={{0,28},{4,0},{8,4},{12,8},{16,12},{20,16},{24,20},{28,24},{1,29},{... | collective-permute-start | bytes 393224 | tf_op jit(solution)/shard_map/ppermute | solution.py:28
  59.6 3.7 %collective-permute-done.24.refs_1_ = bf16[5,256,256]{2,1,0:T(8,128)(2,1)S(1)} collective-permute-done((bf16[5,256,256]{2,1,0:T(8,128)(2,1)S(1)}, bf16[5,256,256]{2,1,0:T(8,128)(2,1)S(1)}, u32[]{:S(2)}, u32[]{:S(2)}) %collective-permute-start.24) | collective-permute-done | bytes 655392 | tf_op jit(solution)/shard_map/ppermute | solution.py:28
  63.8 1.1 collective-permute-start.25
  64.9 3.9 %collective-permute-done.21.refs_1_ = bf16[2,128,256]{2,1,0:T(8,128)(2,1)S(1)} collective-permute-done((bf16[2,128,256]{2,1,0:T(8,128)(2,1)S(1)}, bf16[2,128,256]{2,1,0:T(8,128)(2,1)S(1)}, u32[]{:S(2)}, u32[]{:S(2)}) %collective-permute-start.21) | collective-permute-done | bytes 131104 | tf_op jit(solution)/shard_map/ppermute | solution.py:28
  69.1 2.1 %collective-permute-start.28 = (f32[8,128]{1,0:T(8,128)S(1)}, f32[8,128]{1,0:T(8,128)S(1)}, u32[]{:S(2)}, u32[]{:S(2)}) collective-permute-start(f32[8,128]{1,0:T(8,128)S(1)} %add_add_fusion.5), channel_id=1, source_target_pairs={{0,4},{1,5},{2,6},{3,7},{4,0},{5,1},{6,2},{7,3},{8,12},{9,13},{10,... | collective-permute-start | bytes 12296 | tf_op jit(solution)/shard_map/ppermute | solution.py:281
  72.8 2.1 %shard_map.87 = (f32[2,128,256]{2,1,0:T(8,128)S(1)}, bf16[2,128,256]{2,1,0:T(8,128)(2,1)S(1)}, bf16[6,256,256]{2,1,0:T(8,128)(2,1)S(1)}, bf16[2,256,256]{2,1,0:T(8,128)(2,1)S(1)}) custom-call(s32[8,2]{1,0:T(8,128)S(1)} %copy.18.partner_any, bf16[8,2,256,256]{3,2,1,0:T(8,128)(2,1)S(1)} %copy-done, ...), custom_call_target="tpu_custom_call", output_to_operand_aliasing={{2}: (8, {})} | custom-call | tf_op jit(solution)/shard_map/pallas_call | solution.py:54
  75.0 1.3 %collective-permute-done.30 = bf16[2,128,256]{2,1,0:T(8,128)(2,1)S(1)} collective-permute-done((bf16[2,128,256]{2,1,0:T(8,128)(2,1)S(1)}, bf16[2,128,256]{2,1,0:T(8,128)(2,1)S(1)}, u32[]{:S(2)}, u32[]{:S(2)}) %collective-permute-start.30) | collective-permute-done | bytes 131104 | tf_op jit(solution)/shard_map/ppermute | solution.py:32
  76.3 1.6 %collective-permute-start.31 = (bf16[2,128,256]{2,1,0:T(8,128)(2,1)S(1)}, bf16[2,128,256]{2,1,0:T(8,128)(2,1)S(1)}, u32[]{:S(2)}, u32[]{:S(2)}) collective-permute-start(bf16[2,128,256]{2,1,0:T(8,128)(2,1)S(1)} %add_convert_fusion.1.refs_0_), channel_id=1, source_target_pairs={{0,2},{1,3},{2,0},{3,1},{4,6},{5,7},{6,4},{7,5},{8,10},{9,11},{10,... | collective-permute-start | bytes 393224 | tf_op jit(solution)/shard_map/ppermute | solution.py:41
  77.9 4.0 %collective-permute-done.31.refs_1_ = bf16[2,128,256]{2,1,0:T(8,128)(2,1)S(1)} collective-permute-done((bf16[2,128,256]{2,1,0:T(8,128)(2,1)S(1)}, bf16[2,128,256]{2,1,0:T(8,128)(2,1)S(1)}, u32[]{:S(2)}, u32[]{:S(2)}) %collective-permute-start.31) | collective-permute-done | bytes 131104 | tf_op jit(solution)/shard_map/ppermute | solution.py:41
  82.1 3.8 %collective-permute-start.34 = (bf16[2,128,256]{2,1,0:T(8,128)(2,1)S(1)}, bf16[2,128,256]{2,1,0:T(8,128)(2,1)S(1)}, u32[]{:S(2)}, u32[]{:S(2)}) collective-permute-start(bf16[2,128,256]{2,1,0:T(8,128)(2,1)S(1)} %get-tuple-element.39.refs_0_), channel_id=1, source_target_pairs={{0,28},{4,0},{8,4},{12,8},{16,12},{20,16},{24,20},{28,24},{1,29},{... | collective-permute-start | bytes 393224 | tf_op jit(solution)/shard_map/ppermute | solution.py:28
  85.9 1.3 %collective-permute-start.39 = (f32[8,128]{1,0:T(8,128)S(1)}, f32[8,128]{1,0:T(8,128)S(1)}, u32[]{:S(2)}, u32[]{:S(2)}) collective-permute-start(f32[8,128]{1,0:T(8,128)S(1)} %get-tuple-element.40), channel_id=1, source_target_pairs={{0,24},{4,28},{8,16},{12,20},{16,8},{20,12},{24,0},{28,4},{1,25},{... | collective-permute-start | bytes 12296 | tf_op jit(solution)/shard_map/ppermute | solution.py:281
  87.3 3.9 %collective-permute-done.37.refs_1_.refs_2_ = bf16[5,256,256]{2,1,0:T(8,128)(2,1)S(1)} collective-permute-done((bf16[5,256,256]{2,1,0:T(8,128)(2,1)S(1)}, bf16[5,256,256]{2,1,0:T(8,128)(2,1)S(1)}, u32[]{:S(2)}, u32[]{:S(2)}) %collective-permute-start.37) | collective-permute-done | bytes 655392 | tf_op jit(solution)/shard_map/ppermute | solution.py:28
  91.7 1.8 %collective-permute-start.38 = (f32[8,128]{1,0:T(8,128)S(1)}, f32[8,128]{1,0:T(8,128)S(1)}, u32[]{:S(2)}, u32[]{:S(2)}) collective-permute-start(f32[8,128]{1,0:T(8,128)S(1)} %shard_map.90), channel_id=1, source_target_pairs={{0,8},{4,12},{8,0},{12,4},{16,24},{20,28},{24,16},{28,20},{1,9},{5... | collective-permute-start | bytes 12296 | tf_op jit(solution)/shard_map/ppermute | solution.py:281
  93.6 3.0 %collective-permute-done.34.refs_1_ = bf16[2,128,256]{2,1,0:T(8,128)(2,1)S(1)} collective-permute-done((bf16[2,128,256]{2,1,0:T(8,128)(2,1)S(1)}, bf16[2,128,256]{2,1,0:T(8,128)(2,1)S(1)}, u32[]{:S(2)}, u32[]{:S(2)}) %collective-permute-start.34) | collective-permute-done | bytes 131104 | tf_op jit(solution)/shard_map/ppermute | solution.py:28
  96.9 2.0 %collective-permute-start.41 = (f32[8,128]{1,0:T(8,128)S(1)}, f32[8,128]{1,0:T(8,128)S(1)}, u32[]{:S(2)}, u32[]{:S(2)}) collective-permute-start(f32[8,128]{1,0:T(8,128)S(1)} %add_add_fusion.3), channel_id=1, source_target_pairs={{0,4},{1,5},{2,6},{3,7},{4,0},{5,1},{6,2},{7,3},{8,12},{9,13},{10,... | collective-permute-start | bytes 12296 | tf_op jit(solution)/shard_map/ppermute | solution.py:281
  98.9 1.0 collective-permute-done.42
  100.6 2.1 %shard_map.91 = (f32[2,128,256]{2,1,0:T(8,128)S(1)}, bf16[2,128,256]{2,1,0:T(8,128)(2,1)S(1)}, bf16[6,256,256]{2,1,0:T(8,128)(2,1)S(1)}) custom-call(s32[8,2]{1,0:T(8,128)S(1)} %copy.18.partner_any, bf16[8,2,256,256]{3,2,1,0:T(8,128)(2,1)S(1)} %copy-done, bf16[8,2,256,256]{3,2,1,0:T(8,128)(2,1)S(1)} %copy-done.2, ...), custom_call_target="tpu_custom_call", output_to_operand_aliasing={{2}: (8, {})} | custom-call | tf_op jit(solution)/shard_map/pallas_call | solution.py:54
  102.9 1.9 %collective-permute-start.46 = (bf16[2,256,256]{2,1,0:T(8,128)(2,1)S(1)}, bf16[2,256,256]{2,1,0:T(8,128)(2,1)S(1)}, u32[]{:S(2)}, u32[]{:S(2)}) collective-permute-start(bf16[2,256,256]{2,1,0:T(8,128)(2,1)S(1)} %get-tuple-element.46), channel_id=1, source_target_pairs={{0,4},{4,8},{8,12},{12,16},{16,20},{20,24},{24,28},{28,0},{1,5},{5... | collective-permute-start | bytes 786440 | tf_op jit(solution)/shard_map/ppermute | solution.py:28
  104.8 1.6 %collective-permute-start.44 = (bf16[2,128,256]{2,1,0:T(8,128)(2,1)S(1)}, bf16[2,128,256]{2,1,0:T(8,128)(2,1)S(1)}, u32[]{:S(2)}, u32[]{:S(2)}) collective-permute-start(bf16[2,128,256]{2,1,0:T(8,128)(2,1)S(1)} %add_convert_fusion.refs_0_), channel_id=1, source_target_pairs={{0,2},{1,3},{2,0},{3,1},{4,6},{5,7},{6,4},{7,5},{8,10},{9,11},{10,... | collective-permute-start | bytes 393224 | tf_op jit(solution)/shard_map/ppermute | solution.py:41
  106.4 4.0 %collective-permute-done.44.refs_1_ = bf16[2,128,256]{2,1,0:T(8,128)(2,1)S(1)} collective-permute-done((bf16[2,128,256]{2,1,0:T(8,128)(2,1)S(1)}, bf16[2,128,256]{2,1,0:T(8,128)(2,1)S(1)}, u32[]{:S(2)}, u32[]{:S(2)}) %collective-permute-start.44) | collective-permute-done | bytes 131104 | tf_op jit(solution)/shard_map/ppermute | solution.py:41
  110.6 1.3 %collective-permute-start.52 = (bf16[2,128,256]{2,1,0:T(8,128)(2,1)S(1)}, bf16[2,128,256]{2,1,0:T(8,128)(2,1)S(1)}, u32[]{:S(2)}, u32[]{:S(2)}) collective-permute-start(bf16[2,128,256]{2,1,0:T(8,128)(2,1)S(1)} %get-tuple-element.47.refs_1_), channel_id=1, source_target_pairs={{0,4},{4,8},{8,12},{12,16},{16,20},{20,24},{24,28},{28,0},{1,5},{5... | collective-permute-start | bytes 393224 | tf_op jit(solution)/shard_map/ppermute | solution.py:28
  111.9 2.1 %collective-permute-start.48 = (f32[8,128]{1,0:T(8,128)S(1)}, f32[8,128]{1,0:T(8,128)S(1)}, u32[]{:S(2)}, u32[]{:S(2)}) collective-permute-start(f32[8,128]{1,0:T(8,128)S(1)} %get-tuple-element.45), channel_id=1, source_target_pairs={{0,24},{4,28},{8,16},{12,20},{16,8},{20,12},{24,0},{28,4},{1,25},{... | collective-permute-start | bytes 12296 | tf_op jit(solution)/shard_map/ppermute | solution.py:281
  114.3 2.0 %collective-permute-start.47 = (f32[8,128]{1,0:T(8,128)S(1)}, f32[8,128]{1,0:T(8,128)S(1)}, u32[]{:S(2)}, u32[]{:S(2)}) collective-permute-start(f32[8,128]{1,0:T(8,128)S(1)} %shard_map.93), channel_id=1, source_target_pairs={{0,8},{4,12},{8,0},{12,4},{16,24},{20,28},{24,16},{28,20},{1,9},{5... | collective-permute-start | bytes 12296 | tf_op jit(solution)/shard_map/ppermute | solution.py:281
  116.3 2.0 %collective-permute-done.52.refs_0_ = bf16[2,128,256]{2,1,0:T(8,128)(2,1)S(1)} collective-permute-done((bf16[2,128,256]{2,1,0:T(8,128)(2,1)S(1)}, bf16[2,128,256]{2,1,0:T(8,128)(2,1)S(1)}, u32[]{:S(2)}, u32[]{:S(2)}) %collective-permute-start.52) | collective-permute-done | bytes 131104 | tf_op jit(solution)/shard_map/ppermute | solution.py:28
  118.6 2.1 %collective-permute-start.50 = (f32[8,128]{1,0:T(8,128)S(1)}, f32[8,128]{1,0:T(8,128)S(1)}, u32[]{:S(2)}, u32[]{:S(2)}) collective-permute-start(f32[8,128]{1,0:T(8,128)S(1)} %add_add_fusion.1), channel_id=1, source_target_pairs={{0,4},{1,5},{2,6},{3,7},{4,0},{5,1},{6,2},{7,3},{8,12},{9,13},{10,... | collective-permute-start | bytes 12296 | tf_op jit(solution)/shard_map/ppermute | solution.py:281
  122.3 2.5 %shard_map.95 = (bf16[2,256,256]{2,1,0:T(8,128)(2,1)}, bf16[8,2,256,256]{3,2,1,0:T(8,128)(2,1)}) custom-call(s32[2,128]{1,0:T(2,128)S(1)} %collective-permute-done.refs_2_.kept, f32[8,128]{1,0:T(8,128)S(1)} %add_add_fusion.sums, bf16[6,256,256]{2,1,0:T(8,128)(2,1)S(1)} %get-tuple-element.42.state, bf16[4,128,256]{2,1,0:T(8,128)(2,1)S(1)} %shard_map.94.pair, ...), custom_call_target="tpu_custom_call" | custom-call | flops 1073741824 | bytes 4194304 | tf_op jit(solution)/shard_map/pallas_call | solution.py:371
  (114 shorter events, 9.4 us)
Async XLA Ops:
  1.7 8.8 %collective-permute-start.2 = (bf16[2,128,256]{2,1,0:T(8,128)(2,1)S(1)}, bf16[2,128,256]{2,1,0:T(8,128)(2,1)S(1)}, u32[]{:S(2)}, u32[]{:S(2)}) collective-permute-start(bf16[2,128,256]{2,1,0:T(8,128)(2,1)S(1)} %get-tuple-element.49.refs_0_), channel_id=1, source_target_pairs={{0,28},{4,0},{8,4},{12,8},{16,12},{20,16},{24,20},{28,24},{1,29},{... | collective-permute-start | bytes 393224 | tf_op jit(solution)/shard_map/ppermute | solution.py:28
  7.7 7.7 %collective-permute-start.1 = (bf16[2,128,256]{2,1,0:T(8,128)(2,1)S(1)}, bf16[2,128,256]{2,1,0:T(8,128)(2,1)S(1)}, u32[]{:S(2)}, u32[]{:S(2)}) collective-permute-start(bf16[2,128,256]{2,1,0:T(8,128)(2,1)S(1)} %get-tuple-element.49.refs_0_), channel_id=1, source_target_pairs={{0,4},{4,8},{8,12},{12,16},{16,20},{20,24},{24,28},{28,0},{1,5},{5... | collective-permute-start | bytes 393224 | tf_op jit(solution)/shard_map/ppermute | solution.py:28
  15.4 1.7 %collective-permute-start.3 = (bf16[4,128,256]{2,1,0:T(8,128)(2,1)S(1)}, bf16[4,128,256]{2,1,0:T(8,128)(2,1)}, u32[]{:S(2)}, u32[]{:S(2)}) collective-permute-start(bf16[4,128,256]{2,1,0:T(8,128)(2,1)S(1)} %shard_map.79.refs_2_), channel_id=1, source_target_pairs={{0,1},{1,0},{2,3},{3,2},{4,5},{5,4},{6,7},{7,6},{8,9},{9,8},{10,11... | collective-permute-start | bytes 786440 | tf_op jit(solution)/shard_map/ppermute | solution.py:32
  15.5 17.1 %collective-permute-start.6 = (bf16[4,256,256]{2,1,0:T(8,128)(2,1)S(1)}, bf16[4,256,256]{2,1,0:T(8,128)(2,1)S(1)}, u32[]{:S(2)}, u32[]{:S(2)}) collective-permute-start(bf16[4,256,256]{2,1,0:T(8,128)(2,1)S(1)} %shard_map.77.refs_1_), channel_id=1, source_target_pairs={{0,4},{4,8},{8,12},{12,16},{16,20},{20,24},{24,28},{28,0},{1,5},{5... | collective-permute-start | bytes 1572872 | tf_op jit(solution)/shard_map/ppermute | solution.py:28
  24.2 8.4 %collective-permute-start.5 = (bf16[2,128,256]{2,1,0:T(8,128)(2,1)S(1)}, bf16[2,128,256]{2,1,0:T(8,128)(2,1)S(1)}, u32[]{:S(2)}, u32[]{:S(2)}) collective-permute-start(bf16[2,128,256]{2,1,0:T(8,128)(2,1)S(1)} %add_convert_fusion.3.refs_0_), channel_id=1, source_target_pairs={{0,2},{1,3},{2,0},{3,1},{4,6},{5,7},{6,4},{7,5},{8,10},{9,11},{10,... | collective-permute-start | bytes 393224 | tf_op jit(solution)/shard_map/ppermute | solution.py:41
  25.8 6.7 %collective-permute-start = (s32[2,128]{1,0:T(2,128)S(1)}, s32[2,128]{1,0:T(2,128)S(1)}, u32[]{:S(2)}, u32[]{:S(2)}) collective-permute-start(s32[2,128]{1,0:T(2,128)S(1)} %broadcast_in_dim.4), channel_id=1, source_target_pairs={{0,4},{4,8},{8,12},{12,16},{16,20},{20,24},{24,28},{28,0},{1,5},{5... | collective-permute-start | bytes 3080 | tf_op jit(solution)/shard_map/ppermute | solution.py:28
  32.8 6.5 %collective-permute-start.9 = (bf16[2,128,256]{2,1,0:T(8,128)(2,1)S(1)}, bf16[2,128,256]{2,1,0:T(8,128)(2,1)S(1)}, u32[]{:S(2)}, u32[]{:S(2)}) collective-permute-start(bf16[2,128,256]{2,1,0:T(8,128)(2,1)S(1)} %get-tuple-element.28.refs_0_), channel_id=1, source_target_pairs={{0,28},{4,0},{8,4},{12,8},{16,12},{20,16},{24,20},{28,24},{1,29},{... | collective-permute-start | bytes 393224 | tf_op jit(solution)/shard_map/ppermute | solution.py:28
  33.3 7.7 %collective-permute-start.8 = (bf16[2,128,256]{2,1,0:T(8,128)(2,1)S(1)}, bf16[2,128,256]{2,1,0:T(8,128)(2,1)S(1)}, u32[]{:S(2)}, u32[]{:S(2)}) collective-permute-start(bf16[2,128,256]{2,1,0:T(8,128)(2,1)S(1)} %get-tuple-element.28.refs_0_), channel_id=1, source_target_pairs={{0,4},{4,8},{8,12},{12,16},{16,20},{20,24},{24,28},{28,0},{1,5},{5... | collective-permute-start | bytes 393224 | tf_op jit(solution)/shard_map/ppermute | solution.py:28
  34.9 6.2 %collective-permute-start.13 = (f32[8,128]{1,0:T(8,128)S(1)}, f32[8,128]{1,0:T(8,128)S(1)}, u32[]{:S(2)}, u32[]{:S(2)}) collective-permute-start(f32[8,128]{1,0:T(8,128)S(1)} %get-tuple-element.29), channel_id=1, source_target_pairs={{0,24},{4,28},{8,16},{12,20},{16,8},{20,12},{24,0},{28,4},{1,25},{... | collective-permute-start | bytes 12296 | tf_op jit(solution)/shard_map/ppermute | solution.py:281
  34.9 6.2 %collective-permute-start.12 = (f32[8,128]{1,0:T(8,128)S(1)}, f32[8,128]{1,0:T(8,128)S(1)}, u32[]{:S(2)}, u32[]{:S(2)}) collective-permute-start(f32[8,128]{1,0:T(8,128)S(1)} %get-tuple-element.29), channel_id=1, source_target_pairs={{0,8},{4,12},{8,0},{12,4},{16,24},{20,28},{24,16},{28,20},{1,9},{5... | collective-permute-start | bytes 12296 | tf_op jit(solution)/shard_map/ppermute | solution.py:281
  34.9 6.2 %collective-permute-start.11 = (f32[8,128]{1,0:T(8,128)S(1)}, f32[8,128]{1,0:T(8,128)S(1)}, u32[]{:S(2)}, u32[]{:S(2)}) collective-permute-start(f32[8,128]{1,0:T(8,128)S(1)} %get-tuple-element.29), channel_id=1, source_target_pairs={{0,16},{4,20},{8,24},{12,28},{16,0},{20,4},{24,8},{28,12},{1,17},{... | collective-permute-start | bytes 12296 | tf_op jit(solution)/shard_map/ppermute | solution.py:281
  41.0 5.3 %collective-permute-start.10 = (bf16[4,128,256]{2,1,0:T(8,128)(2,1)S(1)}, bf16[4,128,256]{2,1,0:T(8,128)(2,1)S(1)}, u32[]{:S(2)}, u32[]{:S(2)}) collective-permute-start(bf16[4,128,256]{2,1,0:T(8,128)(2,1)S(1)} %shard_map.82.refs_2_), channel_id=1, source_target_pairs={{0,1},{1,0},{2,3},{3,2},{4,5},{5,4},{6,7},{7,6},{8,9},{9,8},{10,11... | collective-permute-start | bytes 786440 | tf_op jit(solution)/shard_map/ppermute | solution.py:32
  41.1 3.8 %collective-permute-start.16 = (f32[8,128]{1,0:T(8,128)S(1)}, f32[8,128]{1,0:T(8,128)S(1)}, u32[]{:S(2)}, u32[]{:S(2)}) collective-permute-start(f32[8,128]{1,0:T(8,128)S(1)} %add_add_fusion.7), channel_id=1, source_target_pairs={{0,5},{1,4},{2,7},{3,6},{4,1},{5,0},{6,3},{7,2},{8,13},{9,12},{10,... | collective-permute-start | bytes 12296 | tf_op jit(solution)/shard_map/ppermute | solution.py:281
  41.2 3.8 %collective-permute-start.15 = (f32[8,128]{1,0:T(8,128)S(1)}, f32[8,128]{1,0:T(8,128)S(1)}, u32[]{:S(2)}, u32[]{:S(2)}) collective-permute-start(f32[8,128]{1,0:T(8,128)S(1)} %add_add_fusion.7), channel_id=1, source_target_pairs={{0,4},{1,5},{2,6},{3,7},{4,0},{5,1},{6,2},{7,3},{8,12},{9,13},{10,... | collective-permute-start | bytes 12296 | tf_op jit(solution)/shard_map/ppermute | solution.py:281
  43.3 19.9 %collective-permute-start.24 = (bf16[5,256,256]{2,1,0:T(8,128)(2,1)S(1)}, bf16[5,256,256]{2,1,0:T(8,128)(2,1)S(1)}, u32[]{:S(2)}, u32[]{:S(2)}) collective-permute-start(bf16[5,256,256]{2,1,0:T(8,128)(2,1)S(1)} %get-tuple-element.35), channel_id=1, source_target_pairs={{0,4},{4,8},{8,12},{12,16},{16,20},{20,24},{24,28},{28,0},{1,5},{5... | collective-permute-start | bytes 1966088 | tf_op jit(solution)/shard_map/ppermute | solution.py:28
  49.8 5.6 %collective-permute-start.18 = (bf16[2,128,256]{2,1,0:T(8,128)(2,1)S(1)}, bf16[2,128,256]{2,1,0:T(8,128)(2,1)S(1)}, u32[]{:S(2)}, u32[]{:S(2)}) collective-permute-start(bf16[2,128,256]{2,1,0:T(8,128)(2,1)S(1)} %add_convert_fusion.2.refs_0_), channel_id=1, source_target_pairs={{0,2},{1,3},{2,0},{3,1},{4,6},{5,7},{6,4},{7,5},{8,10},{9,11},{10,... | collective-permute-start | bytes 393224 | tf_op jit(solution)/shard_map/ppermute | solution.py:41
  55.6 8.2 %collective-permute-start.19 = (bf16[2,128,256]{2,1,0:T(8,128)(2,1)S(1)}, bf16[2,128,256]{2,1,0:T(8,128)(2,1)S(1)}, u32[]{:S(2)}, u32[]{:S(2)}) collective-permute-start(bf16[2,128,256]{2,1,0:T(8,128)(2,1)S(1)} %get-tuple-element.33.refs_0_), channel_id=1, source_target_pairs={{0,1},{1,0},{2,3},{3,2},{4,5},{5,4},{6,7},{7,6},{8,9},{9,8},{10,11... | collective-permute-start | bytes 393224 | tf_op jit(solution)/shard_map/ppermute | solution.py:32
  55.7 13.1 %collective-permute-start.21 = (bf16[2,128,256]{2,1,0:T(8,128)(2,1)S(1)}, bf16[2,128,256]{2,1,0:T(8,128)(2,1)S(1)}, u32[]{:S(2)}, u32[]{:S(2)}) collective-permute-start(bf16[2,128,256]{2,1,0:T(8,128)(2,1)S(1)} %get-tuple-element.33.refs_0_), channel_id=1, source_target_pairs={{0,28},{4,0},{8,4},{12,8},{16,12},{20,16},{24,20},{28,24},{1,29},{... | collective-permute-start | bytes 393224 | tf_op jit(solution)/shard_map/ppermute | solution.py:28
  58.9 9.9 %collective-permute-start.20 = (bf16[2,128,256]{2,1,0:T(8,128)(2,1)S(1)}, bf16[2,128,256]{2,1,0:T(8,128)(2,1)S(1)}, u32[]{:S(2)}, u32[]{:S(2)}) collective-permute-start(bf16[2,128,256]{2,1,0:T(8,128)(2,1)S(1)} %get-tuple-element.33.refs_0_), channel_id=1, source_target_pairs={{0,4},{4,8},{8,12},{12,16},{16,20},{20,24},{24,28},{28,0},{1,5},{5... | collective-permute-start | bytes 393224 | tf_op jit(solution)/shard_map/ppermute | solution.py:28
  58.9 10.0 %collective-permute-start.26 = (f32[8,128]{1,0:T(8,128)S(1)}, f32[8,128]{1,0:T(8,128)S(1)}, u32[]{:S(2)}, u32[]{:S(2)}) collective-permute-start(f32[8,128]{1,0:T(8,128)S(1)} %get-tuple-element.34), channel_id=1, source_target_pairs={{0,24},{4,28},{8,16},{12,20},{16,8},{20,12},{24,0},{28,4},{1,25},{... | collective-permute-start | bytes 12296 | tf_op jit(solution)/shard_map/ppermute | solution.py:281
  63.3 5.7 %collective-permute-start.23 = (f32[8,128]{1,0:T(8,128)S(1)}, f32[8,128]{1,0:T(8,128)S(1)}, u32[]{:S(2)}, u32[]{:S(2)}) collective-permute-start(f32[8,128]{1,0:T(8,128)S(1)} %get-tuple-element.34), channel_id=1, source_target_pairs={{0,16},{4,20},{8,24},{12,28},{16,0},{20,4},{24,8},{28,12},{1,17},{... | collective-permute-start | bytes 12296 | tf_op jit(solution)/shard_map/ppermute | solution.py:281
  63.8 5.2 %collective-permute-start.25 = (f32[8,128]{1,0:T(8,128)S(1)}, f32[8,128]{1,0:T(8,128)S(1)}, u32[]{:S(2)}, u32[]{:S(2)}) collective-permute-start(f32[8,128]{1,0:T(8,128)S(1)} %shard_map.86), channel_id=1, source_target_pairs={{0,8},{4,12},{8,0},{12,4},{16,24},{20,28},{24,16},{28,20},{1,9},{5... | collective-permute-start | bytes 12296 | tf_op jit(solution)/shard_map/ppermute | solution.py:281
  68.8 3.9 %collective-permute-start.22 = (bf16[4,128,256]{2,1,0:T(8,128)(2,1)S(1)}, bf16[4,128,256]{2,1,0:T(8,128)(2,1)S(1)}, u32[]{:S(2)}, u32[]{:S(2)}) collective-permute-start(bf16[4,128,256]{2,1,0:T(8,128)(2,1)S(1)} %shard_map.85.refs_2_), channel_id=1, source_target_pairs={{0,1},{1,0},{2,3},{3,2},{4,5},{5,4},{6,7},{7,6},{8,9},{9,8},{10,11... | collective-permute-start | bytes 786440 | tf_op jit(solution)/shard_map/ppermute | solution.py:32
  69.0 3.1 %collective-permute-start.29 = (f32[8,128]{1,0:T(8,128)S(1)}, f32[8,128]{1,0:T(8,128)S(1)}, u32[]{:S(2)}, u32[]{:S(2)}) collective-permute-start(f32[8,128]{1,0:T(8,128)S(1)} %add_add_fusion.5), channel_id=1, source_target_pairs={{0,5},{1,4},{2,7},{3,6},{4,1},{5,0},{6,3},{7,2},{8,13},{9,12},{10,... | collective-permute-start | bytes 12296 | tf_op jit(solution)/shard_map/ppermute | solution.py:281
  69.1 3.7 %collective-permute-start.28 = (f32[8,128]{1,0:T(8,128)S(1)}, f32[8,128]{1,0:T(8,128)S(1)}, u32[]{:S(2)}, u32[]{:S(2)}) collective-permute-start(f32[8,128]{1,0:T(8,128)S(1)} %add_add_fusion.5), channel_id=1, source_target_pairs={{0,4},{1,5},{2,6},{3,7},{4,0},{5,1},{6,2},{7,3},{8,12},{9,13},{10,... | collective-permute-start | bytes 12296 | tf_op jit(solution)/shard_map/ppermute | solution.py:281
  71.1 1.6 %collective-permute-start.27 = (f32[8,128]{1,0:T(8,128)S(1)}, f32[8,128]{1,0:T(8,128)S(1)}, u32[]{:S(2)}, u32[]{:S(2)}) collective-permute-start(f32[8,128]{1,0:T(8,128)S(1)} %add_add_fusion.5), channel_id=1, source_target_pairs={{0,1},{1,0},{2,3},{3,2},{4,5},{5,4},{6,7},{7,6},{8,9},{9,8},{10,11... | collective-permute-start | bytes 12296 | tf_op jit(solution)/shard_map/ppermute | solution.py:281
  71.1 20.0 %collective-permute-start.37 = (bf16[5,256,256]{2,1,0:T(8,128)(2,1)S(1)}, bf16[5,256,256]{2,1,0:T(8,128)(2,1)S(1)}, u32[]{:S(2)}, u32[]{:S(2)}) collective-permute-start(bf16[5,256,256]{2,1,0:T(8,128)(2,1)S(1)} %get-tuple-element.41), channel_id=1, source_target_pairs={{0,4},{4,8},{8,12},{12,16},{16,20},{20,24},{24,28},{28,0},{1,5},{5... | collective-permute-start | bytes 1966088 | tf_op jit(solution)/shard_map/ppermute | solution.py:28
  76.3 5.6 %collective-permute-start.31 = (bf16[2,128,256]{2,1,0:T(8,128)(2,1)S(1)}, bf16[2,128,256]{2,1,0:T(8,128)(2,1)S(1)}, u32[]{:S(2)}, u32[]{:S(2)}) collective-permute-start(bf16[2,128,256]{2,1,0:T(8,128)(2,1)S(1)} %add_convert_fusion.1.refs_0_), channel_id=1, source_target_pairs={{0,2},{1,3},{2,0},{3,1},{4,6},{5,7},{6,4},{7,5},{8,10},{9,11},{10,... | collective-permute-start | bytes 393224 | tf_op jit(solution)/shard_map/ppermute | solution.py:41
  82.1 9.7 %collective-permute-start.32 = (bf16[2,128,256]{2,1,0:T(8,128)(2,1)S(1)}, bf16[2,128,256]{2,1,0:T(8,128)(2,1)S(1)}, u32[]{:S(2)}, u32[]{:S(2)}) collective-permute-start(bf16[2,128,256]{2,1,0:T(8,128)(2,1)S(1)} %get-tuple-element.39.refs_0_), channel_id=1, source_target_pairs={{0,1},{1,0},{2,3},{3,2},{4,5},{5,4},{6,7},{7,6},{8,9},{9,8},{10,11... | collective-permute-start | bytes 393224 | tf_op jit(solution)/shard_map/ppermute | solution.py:32
  82.1 14.4 %collective-permute-start.34 = (bf16[2,128,256]{2,1,0:T(8,128)(2,1)S(1)}, bf16[2,128,256]{2,1,0:T(8,128)(2,1)S(1)}, u32[]{:S(2)}, u32[]{:S(2)}) collective-permute-start(bf16[2,128,256]{2,1,0:T(8,128)(2,1)S(1)} %get-tuple-element.39.refs_0_), channel_id=1, source_target_pairs={{0,28},{4,0},{8,4},{12,8},{16,12},{20,16},{24,20},{28,24},{1,29},{... | collective-permute-start | bytes 393224 | tf_op jit(solution)/shard_map/ppermute | solution.py:28
  85.9 10.7 %collective-permute-start.33 = (bf16[2,128,256]{2,1,0:T(8,128)(2,1)S(1)}, bf16[2,128,256]{2,1,0:T(8,128)(2,1)S(1)}, u32[]{:S(2)}, u32[]{:S(2)}) collective-permute-start(bf16[2,128,256]{2,1,0:T(8,128)(2,1)S(1)} %get-tuple-element.39.refs_0_), channel_id=1, source_target_pairs={{0,4},{4,8},{8,12},{12,16},{16,20},{20,24},{24,28},{28,0},{1,5},{5... | collective-permute-start | bytes 393224 | tf_op jit(solution)/shard_map/ppermute | solution.py:28
  85.9 10.9 %collective-permute-start.39 = (f32[8,128]{1,0:T(8,128)S(1)}, f32[8,128]{1,0:T(8,128)S(1)}, u32[]{:S(2)}, u32[]{:S(2)}) collective-permute-start(f32[8,128]{1,0:T(8,128)S(1)} %get-tuple-element.40), channel_id=1, source_target_pairs={{0,24},{4,28},{8,16},{12,20},{16,8},{20,12},{24,0},{28,4},{1,25},{... | collective-permute-start | bytes 12296 | tf_op jit(solution)/shard_map/ppermute | solution.py:281
  91.1 5.7 %collective-permute-start.36 = (f32[8,128]{1,0:T(8,128)S(1)}, f32[8,128]{1,0:T(8,128)S(1)}, u32[]{:S(2)}, u32[]{:S(2)}) collective-permute-start(f32[8,128]{1,0:T(8,128)S(1)} %get-tuple-element.40), channel_id=1, source_target_pairs={{0,16},{4,20},{8,24},{12,28},{16,0},{20,4},{24,8},{28,12},{1,17},{... | collective-permute-start | bytes 12296 | tf_op jit(solution)/shard_map/ppermute | solution.py:281
  91.7 5.1 %collective-permute-start.38 = (f32[8,128]{1,0:T(8,128)S(1)}, f32[8,128]{1,0:T(8,128)S(1)}, u32[]{:S(2)}, u32[]{:S(2)}) collective-permute-start(f32[8,128]{1,0:T(8,128)S(1)} %shard_map.90), channel_id=1, source_target_pairs={{0,8},{4,12},{8,0},{12,4},{16,24},{20,28},{24,16},{28,20},{1,9},{5... | collective-permute-start | bytes 12296 | tf_op jit(solution)/shard_map/ppermute | solution.py:281
  96.6 4.0 %collective-permute-start.35 = (bf16[4,128,256]{2,1,0:T(8,128)(2,1)S(1)}, bf16[4,128,256]{2,1,0:T(8,128)(2,1)S(1)}, u32[]{:S(2)}, u32[]{:S(2)}) collective-permute-start(bf16[4,128,256]{2,1,0:T(8,128)(2,1)S(1)} %shard_map.89.refs_2_), channel_id=1, source_target_pairs={{0,1},{1,0},{2,3},{3,2},{4,5},{5,4},{6,7},{7,6},{8,9},{9,8},{10,11... | collective-permute-start | bytes 786440 | tf_op jit(solution)/shard_map/ppermute | solution.py:32
  96.8 3.1 %collective-permute-start.42 = (f32[8,128]{1,0:T(8,128)S(1)}, f32[8,128]{1,0:T(8,128)S(1)}, u32[]{:S(2)}, u32[]{:S(2)}) collective-permute-start(f32[8,128]{1,0:T(8,128)S(1)} %add_add_fusion.3), channel_id=1, source_target_pairs={{0,5},{1,4},{2,7},{3,6},{4,1},{5,0},{6,3},{7,2},{8,13},{9,12},{10,... | collective-permute-start | bytes 12296 | tf_op jit(solution)/shard_map/ppermute | solution.py:281
  96.9 3.7 %collective-permute-start.41 = (f32[8,128]{1,0:T(8,128)S(1)}, f32[8,128]{1,0:T(8,128)S(1)}, u32[]{:S(2)}, u32[]{:S(2)}) collective-permute-start(f32[8,128]{1,0:T(8,128)S(1)} %add_add_fusion.3), channel_id=1, source_target_pairs={{0,4},{1,5},{2,6},{3,7},{4,0},{5,1},{6,2},{7,3},{8,12},{9,13},{10,... | collective-permute-start | bytes 12296 | tf_op jit(solution)/shard_map/ppermute | solution.py:281
  98.9 1.6 %collective-permute-start.40 = (f32[8,128]{1,0:T(8,128)S(1)}, f32[8,128]{1,0:T(8,128)S(1)}, u32[]{:S(2)}, u32[]{:S(2)}) collective-permute-start(f32[8,128]{1,0:T(8,128)S(1)} %add_add_fusion.3), channel_id=1, source_target_pairs={{0,1},{1,0},{2,3},{3,2},{4,5},{5,4},{6,7},{7,6},{8,9},{9,8},{10,11... | collective-permute-start | bytes 12296 | tf_op jit(solution)/shard_map/ppermute | solution.py:281
  102.7 2.1 %collective-permute-start.43 = (bf16[2,128,256]{2,1,0:T(8,128)(2,1)S(1)}, bf16[2,128,256]{2,1,0:T(8,128)(2,1)S(1)}, u32[]{:S(2)}, u32[]{:S(2)}) collective-permute-start(bf16[2,128,256]{2,1,0:T(8,128)(2,1)S(1)} %get-tuple-element.44), channel_id=1, source_target_pairs={{0,1},{1,0},{2,3},{3,2},{4,5},{5,4},{6,7},{7,6},{8,9},{9,8},{10,11... | collective-permute-start | bytes 393224 | tf_op jit(solution)/shard_map/ppermute | solution.py:32
  102.9 11.5 %collective-permute-start.46 = (bf16[2,256,256]{2,1,0:T(8,128)(2,1)S(1)}, bf16[2,256,256]{2,1,0:T(8,128)(2,1)S(1)}, u32[]{:S(2)}, u32[]{:S(2)}) collective-permute-start(bf16[2,256,256]{2,1,0:T(8,128)(2,1)S(1)} %get-tuple-element.46), channel_id=1, source_target_pairs={{0,4},{4,8},{8,12},{12,16},{16,20},{20,24},{24,28},{28,0},{1,5},{5... | collective-permute-start | bytes 786440 | tf_op jit(solution)/shard_map/ppermute | solution.py:28
  104.8 5.6 %collective-permute-start.44 = (bf16[2,128,256]{2,1,0:T(8,128)(2,1)S(1)}, bf16[2,128,256]{2,1,0:T(8,128)(2,1)S(1)}, u32[]{:S(2)}, u32[]{:S(2)}) collective-permute-start(bf16[2,128,256]{2,1,0:T(8,128)(2,1)S(1)} %add_convert_fusion.refs_0_), channel_id=1, source_target_pairs={{0,2},{1,3},{2,0},{3,1},{4,6},{5,7},{6,4},{7,5},{8,10},{9,11},{10,... | collective-permute-start | bytes 393224 | tf_op jit(solution)/shard_map/ppermute | solution.py:41
  110.6 7.8 %collective-permute-start.52 = (bf16[2,128,256]{2,1,0:T(8,128)(2,1)S(1)}, bf16[2,128,256]{2,1,0:T(8,128)(2,1)S(1)}, u32[]{:S(2)}, u32[]{:S(2)}) collective-permute-start(bf16[2,128,256]{2,1,0:T(8,128)(2,1)S(1)} %get-tuple-element.47.refs_1_), channel_id=1, source_target_pairs={{0,4},{4,8},{8,12},{12,16},{16,20},{20,24},{24,28},{28,0},{1,5},{5... | collective-permute-start | bytes 393224 | tf_op jit(solution)/shard_map/ppermute | solution.py:28
  111.9 6.5 %collective-permute-start.48 = (f32[8,128]{1,0:T(8,128)S(1)}, f32[8,128]{1,0:T(8,128)S(1)}, u32[]{:S(2)}, u32[]{:S(2)}) collective-permute-start(f32[8,128]{1,0:T(8,128)S(1)} %get-tuple-element.45), channel_id=1, source_target_pairs={{0,24},{4,28},{8,16},{12,20},{16,8},{20,12},{24,0},{28,4},{1,25},{... | collective-permute-start | bytes 12296 | tf_op jit(solution)/shard_map/ppermute | solution.py:281
  114.0 4.5 %collective-permute-start.45 = (f32[8,128]{1,0:T(8,128)S(1)}, f32[8,128]{1,0:T(8,128)S(1)}, u32[]{:S(2)}, u32[]{:S(2)}) collective-permute-start(f32[8,128]{1,0:T(8,128)S(1)} %get-tuple-element.45), channel_id=1, source_target_pairs={{0,16},{4,20},{8,24},{12,28},{16,0},{20,4},{24,8},{28,12},{1,17},{... | collective-permute-start | bytes 12296 | tf_op jit(solution)/shard_map/ppermute | solution.py:281
  114.3 4.1 %collective-permute-start.47 = (f32[8,128]{1,0:T(8,128)S(1)}, f32[8,128]{1,0:T(8,128)S(1)}, u32[]{:S(2)}, u32[]{:S(2)}) collective-permute-start(f32[8,128]{1,0:T(8,128)S(1)} %shard_map.93), channel_id=1, source_target_pairs={{0,8},{4,12},{8,0},{12,4},{16,24},{20,28},{24,16},{28,20},{1,9},{5... | collective-permute-start | bytes 12296 | tf_op jit(solution)/shard_map/ppermute | solution.py:281
  118.4 4.0 %collective-permute-start.53 = (bf16[4,128,256]{2,1,0:T(8,128)(2,1)S(1)}, bf16[4,128,256]{2,1,0:T(8,128)(2,1)S(1)}, u32[]{:S(2)}, u32[]{:S(2)}) collective-permute-start(bf16[4,128,256]{2,1,0:T(8,128)(2,1)S(1)} %shard_map.94.pair), channel_id=1, source_target_pairs={{0,1},{1,0},{2,3},{3,2},{4,5},{5,4},{6,7},{7,6},{8,9},{9,8},{10,11... | collective-permute-start | bytes 786440 | tf_op jit(solution)/shard_map/ppermute | solution.py:32
  118.5 3.1 %collective-permute-start.51 = (f32[8,128]{1,0:T(8,128)S(1)}, f32[8,128]{1,0:T(8,128)S(1)}, u32[]{:S(2)}, u32[]{:S(2)}) collective-permute-start(f32[8,128]{1,0:T(8,128)S(1)} %add_add_fusion.1), channel_id=1, source_target_pairs={{0,5},{1,4},{2,7},{3,6},{4,1},{5,0},{6,3},{7,2},{8,13},{9,12},{10,... | collective-permute-start | bytes 12296 | tf_op jit(solution)/shard_map/ppermute | solution.py:281
  118.6 3.8 %collective-permute-start.50 = (f32[8,128]{1,0:T(8,128)S(1)}, f32[8,128]{1,0:T(8,128)S(1)}, u32[]{:S(2)}, u32[]{:S(2)}) collective-permute-start(f32[8,128]{1,0:T(8,128)S(1)} %add_add_fusion.1), channel_id=1, source_target_pairs={{0,4},{1,5},{2,6},{3,7},{4,0},{5,1},{6,2},{7,3},{8,12},{9,13},{10,... | collective-permute-start | bytes 12296 | tf_op jit(solution)/shard_map/ppermute | solution.py:281
  (14 other events, 92.2 us)
